TPU v7x, 32 devices: a whole 2x2x4 slice. The times are simulated.
32 devices in a mesh: sx: 8 (over y, x, core), sy: 4 (over z).
Axes of the slice: x: 2, y: 2, z: 4, core: 2. Of those that a mesh axis runs over, the one named last changes fastest.
Arguments:
- forward_prop: bfloat16 [2, 2, 12, 12, 64, 4096], P(None, None, None, None, 'sx', 'sy'), may hold values from -0.08984375 to 0.08984375
- backward_prop: bfloat16 [2, 2, 12, 12, 64, 4096], P(None, None, None, None, 'sx', 'sy'), may hold values from -0.08984375 to 0.08984375
- gamma_table: int32 [16, 4, 2], replicated, may hold values from 0 to 3, as said below
- source_site: int32 [3], replicated, may hold values from 0 to 63
- momenta: int32 [32, 3], replicated, may hold values from -8 to 7
Outputs:
- corr: float32 [16, 2, 2, 64, 4096], P(None, None, None, 'sx', 'sy')
- listed: float32 [2, 16, 2, 32], replicated
Inputs may be any that keep to these rules, and one draw needn't show every extreme that they name: For every insertion g, gamma_table[g, 0..3, 0] is a permutation of 0..3; gamma_table[g, s, 1] is the power of i of that entry.
All inputs are finite; a program needn't handle non-finite values.
Results may differ from a plain program's by a relative error of at most 0.0003.
Values sent between devices are 32-bit elements; how exact they have to be, the bound alone decides.
No kernel may reach another device: no remote copies, remote signals or barrier semaphores. Data moves between devices by JAX's collectives and lax.ppermute only.
A program may use at most 384 MiB of HBM per device.

v0:
```python
import math

import jax
import jax.numpy as jnp
from jax import lax
from jax.sharding import PartitionSpec as P

L = 64
LZ = 64


HIGHEST = lax.Precision.HIGHEST


def gamma_matrices(gamma_table):
    inserts = gamma_table.shape[0]
    columns = gamma_table[:, :, 0]
    powers = gamma_table[:, :, 1]
    spin_ids = jnp.arange(4, dtype=jnp.int32)
    matches = (columns[:, :, None] == spin_ids[None, None, :]).astype(jnp.float32)
    unit_re = (powers == 0).astype(jnp.float32) - (powers == 2).astype(jnp.float32)
    unit_im = (powers == 1).astype(jnp.float32) - (powers == 3).astype(jnp.float32)
    return (
        (matches * unit_re[:, :, None]).reshape(inserts, 16),
        (matches * unit_im[:, :, None]).reshape(inserts, 16),
    )


def dft_table(length, anchor):
    wavenum = jnp.arange(length, dtype=jnp.int32)
    offsets = jnp.mod(wavenum - anchor, length)
    phase_index = jnp.mod(offsets[:, None] * wavenum[None, :], length)
    angles = 2.0 * math.pi / length * phase_index.astype(jnp.float32)
    return (jnp.cos(angles), -jnp.sin(angles))


def complex_step(real_part, imag_part, table_re, table_im, pattern):
    out_re = jnp.einsum(pattern, real_part, table_re, precision=HIGHEST) - jnp.einsum(
        pattern, imag_part, table_im, precision=HIGHEST
    )
    out_im = jnp.einsum(pattern, real_part, table_im, precision=HIGHEST) + jnp.einsum(
        pattern, imag_part, table_re, precision=HIGHEST
    )
    return (out_re, out_im)


def transform(fields, source_site):
    table_re, table_im = dft_table(fields.shape[4], source_site[2])
    along_z = jnp.stack(
        complex_step(fields[:, 0], fields[:, 1], table_re, table_im, "nabz,zk->nabk"), 1
    )
    depth_share = along_z.shape[4] // lax.axis_size("sy")
    first_depth = lax.axis_index("sy") * depth_share
    length_y = along_z.shape[3] * lax.axis_size("sy")
    full_re, full_im = dft_table(length_y, source_site[1])
    part = lax.dynamic_slice_in_dim(
        lax.all_gather(along_z, "sy", axis=3, tiled=True), first_depth, depth_share, 4
    )
    step_re, step_im = complex_step(part[:, 0], part[:, 1], full_re, full_im, "nayc,yk->nakc")
    along_y = jnp.stack([step_re, step_im], 1)
    arrived = lax.all_to_all(along_y, "sx", split_axis=3, concat_axis=2, tiled=True)
    table_re, table_im = dft_table(arrived.shape[2], source_site[0])
    along_x = complex_step(arrived[:, 0], arrived[:, 1], table_re, table_im, "nxbc,xk->nbck")
    return jnp.stack(along_x, 1)


def apply_gammas(mat_re, mat_im, real_part, imag_part):
    extent = real_part.shape
    flat_re = real_part.reshape(extent[0], -1)
    flat_im = imag_part.reshape(extent[0], -1)
    out_re = jnp.dot(mat_re, flat_re, precision=HIGHEST) - jnp.dot(
        mat_im, flat_im, precision=HIGHEST
    )
    out_im = jnp.dot(mat_re, flat_im, precision=HIGHEST) + jnp.dot(
        mat_im, flat_re, precision=HIGHEST
    )
    return (out_re.reshape(extent), out_im.reshape(extent))


def project_sites(fields, source_site, momenta, rows_x, rows_y, length, depth):
    coord_x = lax.axis_index("sx") * rows_x + jnp.arange(rows_x, dtype=jnp.int32) - source_site[0]
    coord_y = lax.axis_index("sy") * rows_y + jnp.arange(rows_y, dtype=jnp.int32) - source_site[1]
    coord_z = jnp.arange(depth, dtype=jnp.int32) - source_site[2]
    part_x = jnp.mod(momenta[:, 0:1] * coord_x[None, :], length)
    part_y = jnp.mod(momenta[:, 1:2] * coord_y[None, :], length)
    part_z = jnp.mod(momenta[:, 2:3] * coord_z[None, :], depth)
    plane = jnp.mod(part_x[:, :, None] + part_y[:, None, :], length).astype(jnp.float32)
    angles = (
        2.0 * math.pi / length * plane[:, :, :, None]
        + 2.0 * math.pi / depth * part_z.astype(jnp.float32)[:, None, None, :]
    )
    angles = angles.reshape(momenta.shape[0], -1)
    cosine = jnp.cos(angles)
    sine = jnp.sin(angles)
    field_re = fields[:, 0].reshape(fields.shape[0], -1)
    field_im = fields[:, 1].reshape(fields.shape[0], -1)
    local_re = jnp.dot(field_re, cosine.T, precision=HIGHEST) + jnp.dot(
        field_im, sine.T, precision=HIGHEST
    )
    local_im = jnp.dot(field_im, cosine.T, precision=HIGHEST) - jnp.dot(
        field_re, sine.T, precision=HIGHEST
    )
    return (local_re, local_im)


def body(forward_prop, backward_prop, gamma_table, source_site, momenta):
    slices = forward_prop.shape[0]
    rows_x = forward_prop.shape[4]
    rows_y = backward_prop.shape[5] // LZ
    inserts = gamma_table.shape[0]
    forward = forward_prop.reshape(slices, 2, 4, 3, 12, -1)
    backward = backward_prop.reshape(slices, 2, 4, 3, 12, -1)
    pattern = "tscjn,tucjn->sutn"
    pair_re = jnp.einsum(
        pattern, backward[:, 0], forward[:, 0], preferred_element_type=jnp.float32
    ) + jnp.einsum(pattern, backward[:, 1], forward[:, 1], preferred_element_type=jnp.float32)
    pair_im = jnp.einsum(
        pattern, backward[:, 0], forward[:, 1], preferred_element_type=jnp.float32
    ) - jnp.einsum(pattern, backward[:, 1], forward[:, 0], preferred_element_type=jnp.float32)
    pair_re = pair_re.reshape(16, slices, -1)
    pair_im = pair_im.reshape(16, slices, -1)
    mat_re, mat_im = gamma_matrices(gamma_table)
    field_re, field_im = apply_gammas(mat_re, mat_im, pair_re, pair_im)
    fields = jnp.stack([field_re, field_im], 2).reshape(inserts * slices, 2, rows_x, rows_y, LZ)
    spectrum = transform(fields, source_site)
    local_re, local_im = project_sites(fields, source_site, momenta, rows_x, rows_y, L, LZ)
    listed_re, listed_im = lax.psum((local_re, local_im), ("sx", "sy"))
    listed_re = listed_re.reshape(inserts, slices, -1)
    listed_im = listed_im.reshape(inserts, slices, -1)
    corr_re = spectrum[:, 0].reshape(inserts, slices, spectrum.shape[2], -1)
    corr_im = spectrum[:, 1].reshape(inserts, slices, spectrum.shape[2], -1)
    return (jnp.stack([corr_re, corr_im], 2), jnp.stack([listed_re, listed_im], 0))


def solution(mesh):
    placed = (
        P(None, None, None, None, "sx", "sy"),
        P(None, None, None, None, "sx", "sy"),
        P(),
        P(),
        P(),
    )
    return jax.shard_map(
        body,
        mesh=mesh,
        in_specs=placed,
        out_specs=(P(None, None, None, "sx", "sy"), P()),
        check_vma=False,
    )
```

profile of v0, /device:TPU:16, one launch (start us, length us, event | category | flops | bytes accessed | tf_op | source)
XLA Modules:
  0.0 1116.6 jit_solution(17718864353184058716)
XLA Ops:
  8.5 15.7 %reshape.371 = bf16[2,2,4,3,12,8192]{5,4,3,2,1,0:T(8,128)(2,1)} reshape(bf16[2,2,12,12,8,1024]{5,4,3,2,1,0:T(8,128)(2,1)} %param.5) | data formatting | bytes 18874368 | tf_op jit(solution)/shard_map/reshape | solution.py:111
  24.2 10.6 fusion.158
  34.8 58.2 %copy.83 = bf16[2,1,4,3,12,8192]{4,2,3,5,0,1:T(4,128)(2,1)} copy(bf16[2,1,4,3,12,8192]{5,4,3,2,1,0:T(8,128)(2,1)} %get-tuple-element.10) | data formatting | bytes 9437184
  93.1 15.7 %reshape.372 = bf16[2,2,4,3,12,8192]{5,4,3,2,1,0:T(8,128)(2,1)} reshape(bf16[2,2,12,12,8,1024]{5,4,3,2,1,0:T(8,128)(2,1)} %param.6) | data formatting | bytes 18874368 | tf_op jit(solution)/shard_map/reshape | solution.py:112
  108.7 10.4 fusion.159
  119.2 58.3 %copy.84 = bf16[2,1,4,3,12,8192]{4,2,3,5,0,1:T(4,128)(2,1)} copy(bf16[2,1,4,3,12,8192]{5,4,3,2,1,0:T(8,128)(2,1)} %get-tuple-element.13) | data formatting | bytes 9437184
  177.4 58.2 %copy.81 = bf16[2,1,4,3,12,8192]{4,2,3,5,0,1:T(4,128)(2,1)} copy(bf16[2,1,4,3,12,8192]{5,4,3,2,1,0:T(8,128)(2,1)} %get-tuple-element.11) | data formatting | bytes 9437184
  235.7 58.3 %copy.82 = bf16[2,1,4,3,12,8192]{4,2,3,5,0,1:T(4,128)(2,1)} copy(bf16[2,1,4,3,12,8192]{5,4,3,2,1,0:T(8,128)(2,1)} %get-tuple-element.12) | data formatting | bytes 9437184
  293.9 62.2 %fusion.2 = f32[2,8192,4,4,1]{3,2,4,1,0:T(4,128)} fusion(bf16[2,1,4,3,12,8192]{4,2,3,5,0,1:T(4,128)(2,1)} %copy.84, bf16[2,1,4,3,12,8192]{4,2,3,5,0,1:T(4,128)(2,1)} %copy.83), kind=kOutput, calls=%fused_computation.2 | convolution fusion | flops 18874368 | bytes 10485760 | tf_op jit(solution)/shard_map/tscjn,tucjn->sutn/dot_general | solution.py:116
  356.1 62.2 %fusion = f32[2,8192,4,4,1]{3,2,4,1,0:T(4,128)} fusion(bf16[2,1,4,3,12,8192]{4,2,3,5,0,1:T(4,128)(2,1)} %copy.84, bf16[2,1,4,3,12,8192]{4,2,3,5,0,1:T(4,128)(2,1)} %copy.81), kind=kOutput, calls=%fused_computation | convolution fusion | flops 18874368 | bytes 10485760 | tf_op jit(solution)/shard_map/tscjn,tucjn->sutn/dot_general | solution.py:119
  418.3 61.4 %fusion.13 = f32[4,4,2,8192]{0,1,3,2:T(4,128)} fusion(f32[2,8192,4,4,1]{3,2,4,1,0:T(4,128)} %fusion.2, bf16[2,1,4,3,12,8192]{4,2,3,5,0,1:T(4,128)(2,1)} %copy.82, bf16[2,1,4,3,12,8192]{4,2,3,5,0,1:T(4,128)(2,1)} %copy.81), kind=kOutput, calls=%fused_computation.15 | convolution fusion | flops 19136512 | bytes 11534336 | tf_op jit(solution)/shard_map/tscjn,tucjn->sutn/dot_general | solution.py:114
  479.7 26.6 %copy.48 = f32[4,4,2,8192]{3,2,1,0:T(2,128)S(1)} copy(f32[4,4,2,8192]{0,1,3,2:T(4,128)} %fusion.13) | data formatting | bytes 2097152 | tf_op jit(solution)/shard_map/add | solution.py:114
  506.9 77.8 %fusion.12 = f32[4,4,2,8192]{0,1,3,2:T(4,128)} fusion(f32[2,8192,4,4,1]{3,2,4,1,0:T(4,128)} %fusion, bf16[2,1,4,3,12,8192]{4,2,3,5,0,1:T(4,128)(2,1)} %copy.82, bf16[2,1,4,3,12,8192]{4,2,3,5,0,1:T(4,128)(2,1)} %copy.83), kind=kOutput, calls=%fused_computation.13 | convolution fusion | flops 19136512 | bytes 11534336 | tf_op jit(solution)/shard_map/tscjn,tucjn->sutn/dot_general | solution.py:117
  584.7 26.6 %copy.49 = f32[4,4,2,8192]{3,2,1,0:T(2,128)S(1)} copy(f32[4,4,2,8192]{0,1,3,2:T(4,128)} %fusion.12) | data formatting | bytes 2097152 | tf_op jit(solution)/shard_map/sub | solution.py:117
  618.9 4.6 fusion.32
  623.4 4.6 fusion.30
  628.0 2.5 convolution_subtract_fusion
  632.6 5.0 subtract_bitcast_fusion.1
  637.6 3.3 add_bitcast_fusion.1
  641.0 2.8 pad_maximum_fusion
  646.4 283.6 %all-gather.2.cloned.1.call-done = f32[32,2,8,64,64]{4,0,3,2,1:T(8,128)} async-done(((f32[32,2,8,16,64]{4,0,3,2,1:T(8,128)}), f32[32,2,8,64,64]{4,0,3,2,1:T(8,128)}) %all-gather.2.cloned.1.call-update) | async-done | bytes 8388624 | tf_op jit(solution)/shard_map/all_gather | solution.py:57
  930.0 11.4 %dynamic-slice_bitcast_fusion = (f32[32,8,64,16]{3,0,2,1:T(8,128)}, f32[32,8,64,16]{3,0,2,1:T(8,128)}) fusion(f32[32,2,8,64,64]{4,0,3,2,1:T(8,128)} %all-gather.2.cloned.1.call-done, s32[]{:T(128)S(6)} %add.213, s32[]{:T(128)S(6)} %select_n.88), kind=kLoop, calls=%fused_computation.18 | loop fusion | bytes 4194312 | tf_op jit(solution)/shard_map/squeeze | solution.py:59
  941.4 7.0 copy.54
  948.5 3.3 fusion.65
  951.8 3.3 fusion.67
  955.1 6.9 copy.55
  962.0 3.7 subtract_bitcast_fusion
  965.8 2.1 add_bitcast_fusion
  967.8 2.8 pad_maximum_fusion.1
  970.7 9.4 copy.58
  980.0 8.6 reshape.373
  988.6 4.5 all-to-all-start
  995.7 9.5 add_sine_fusion
  1005.2 2.1 cos.29
  1007.4 2.2 sin.29
  1013.8 41.3 %all-reduce = (f32[1,16,2,32]{3,2,1,0:T(2,128)S(1)}, f32[1,16,2,32]{3,2,1,0:T(2,128)S(1)}) all-reduce(f32[1,16,2,32]{3,2,1,0:T(2,128)S(1)} %bitcast.194, f32[1,16,2,32]{3,2,1,0:T(2,128)S(1)} %bitcast.193), channel_id=1, replica_groups=mesh['sx'=8,'sy'=4] {'sx','sy'}, use_global_device_ids=true, to_apply=%region_1.2 | all-reduce | flops 2048 | bytes 16384 | tf_op jit(solution)/shard_map/psum | solution.py:127
  1056.2 7.2 reduce
  1063.4 6.0 reshape.374
  1069.4 4.4 copy.60
  1073.8 3.9 fusion.160
  1077.7 3.8 copy.86
  1081.5 3.3 fusion.24
  1084.8 3.3 fusion.22
  1088.1 3.6 copy.85
  1091.8 3.7 fusion.42
  1095.5 2.6 copy.63
  1098.0 2.2 stack_reshape_squeeze_stack.6
  1100.2 3.7 fusion.45
  (61 shorter events, 27.6 us)
Async XLA Ops:
  7.2 922.8 %all-gather.2.cloned.1.call-start = ((), (), s32[]{:S(2)}) async-start(), calls=%async_computation.1 | async-start | bytes 20971520 | tf_op jit(solution)/shard_map/all_gather | solution.py:57
  611.3 0.7 copy-start.10
  611.3 1.4 copy-start.8
  611.3 1.4 copy-start.9
  611.4 1.4 slice-start
  612.0 3.8 copy-start.1
  623.4 4.6 copy-start.2
  623.4 4.6 copy-start.7
  632.6 5.0 copy-start.5
  643.7 2.5 copy-start.11
  962.0 3.7 copy-start.6
  988.6 4.6 copy-start
  988.6 67.1 %all-to-all-start = ((f32[8,1,65536]{2,1,0:T(1,128)}), f32[8,1,65536]{2,1,0:T(1,128)}, u32[]{:S(2)}, u32[]{:S(2)}) async-start(f32[8,1,65536]{2,1,0:T(1,128)} %reshape.373), calls=%async_computation | async-start | bytes 4194304 | tf_op jit(solution)/shard_map/all_to_all | solution.py:61
  1007.4 2.2 copy-start.3
  1009.6 1.2 copy-start.4
Sparse Core Ops, SparseCore 0:
  643.9 286.0 all-gather.1
where the time goes:
time: 1140 us; the launch traced here: 1120 us
  local copies, waits for them, and re-layouts  425 us (37%)
  matrix products  318 us (28%)
  waiting for transfers between devices  284 us (25%)
  blocking collectives  41.3 us (4%)
  other arithmetic  29.7 us (3%)
  between operations  14.7 us (1%)
    all_gather x1, waiting for transfers between devices, transform(): lax.all_gather(along_z, 'sy', axis=3, tiled=True)  284 us
    unnamed x35, local copies, waits for them, and re-layouts  258 us
    dot_general x1, matrix products, body(): jnp.einsum(pattern, backward[:, 0], forward[:, 1], preferred_element_type...  77.8 us
    dot_general x1, matrix products, body(): jnp.einsum(pattern, backward[:, 1], forward[:, 0], preferred_element_type...  62.2 us
    dot_general x1, matrix products, body(): jnp.einsum(pattern, backward[:, 1], forward[:, 1], preferred_element_type...  62.2 us
    dot_general x1, matrix products, body(): jnp.einsum(pattern, backward[:, 0], forward[:, 0], preferred_element_type...  61.4 us
    psum x1, blocking collectives, body(): listed_re, listed_im = lax.psum((local_re, local_im), ('sx', 'sy'))  41.3 us
    add x1, local copies, waits for them, and re-layouts, body(): jnp.einsum(pattern, backward[:, 0], forward[:, 0], preferred_element_type...  26.6 us
  transfers between devices with their start and end apart: 2, of which 1 were waited for; matrix products, arithmetic and copies ran while one was open for 2% of the time, Pallas kernels for 0%

commit v1 on v0

--- a/solution.py
+++ b/solution.py
@@ -1,8 +1,13 @@
+import functools
 import math
 
 import jax
 import jax.numpy as jnp
+import ml_dtypes
+import numpy as np
 from jax import lax
+from jax.experimental import pallas as pl
+from jax.experimental.pallas import tpu as pltpu
 from jax.sharding import PartitionSpec as P
 
 L = 64
@@ -103,7 +108,7 @@
     return (local_re, local_im)
 
 
-def body(forward_prop, backward_prop, gamma_table, source_site, momenta):
+def general_body(forward_prop, backward_prop, gamma_table, source_site, momenta):
     slices = forward_prop.shape[0]
     rows_x = forward_prop.shape[4]
     rows_y = backward_prop.shape[5] // LZ
@@ -132,6 +137,473 @@
     return (jnp.stack([corr_re, corr_im], 2), jnp.stack([listed_re, listed_im], 0))
 
 
+F32 = jnp.float32
+BF16 = jnp.bfloat16
+MIB = 2**20
+
+
+def split_table(table):
+    high = table.astype(ml_dtypes.bfloat16)
+    low = (table - high.astype(np.float64)).astype(ml_dtypes.bfloat16)
+    return (high, low)
+
+
+def split(values):
+    high = values.astype(BF16)
+    return (high, (values - high.astype(F32)).astype(BF16))
+
+
+def turn(out_wave, in_site):
+    angle = 2.0 * math.pi / L * np.mod(np.multiply.outer(out_wave, in_site), L)
+    cosine, sine = (np.cos(angle), np.sin(angle))
+    table = np.empty((len(out_wave), 2, 2, len(in_site)))
+    table[:, 0, 0] = cosine
+    table[:, 0, 1] = sine
+    table[:, 1, 0] = -sine
+    table[:, 1, 1] = cosine
+    return table
+
+
+def table_z():
+    wave = turn(np.arange(64), np.arange(64)).reshape(4, 2, 4, 2, 2, 2, 64)
+    full = np.zeros((4, 2, 4, 2, 2, 2, 2, 2, 64))
+    for y in range(2):
+        full[:, :, :, :, :, y, :, y, :] = wave
+    return split_table(full.reshape(4, 64, 256))
+
+
+def table_y():
+    wave = turn(np.arange(64), np.arange(64)).reshape(8, 8, 2, 2, 4, 8, 2)
+    full = np.zeros((4, 8, 2, 2, 8, 4, 8, 2, 2, 2))
+    for position in range(4):
+        for step in range(4):
+            source = position ^ step
+            for p in range(2):
+                full[position, :, p, :, :, step, :, p] = wave[:, :, :, :, source].transpose(
+                    0, 2, 1, 4, 3, 5
+                )
+    return split_table(full.reshape(4, 256, 256))
+
+
+def table_x():
+    wave = turn(np.arange(64), np.arange(64))
+    cosine, sine = (wave[:, 0, 0].T, wave[:, 0, 1].T)
+    high, low = split_table(np.concatenate([cosine, cosine, sine, sine], 1))
+    return np.concatenate([high, high, low], 0)
+
+
+def nt_dot(a, b):
+    return lax.dot_general(a, b, (((1,), (1,)), ((), ())), preferred_element_type=F32)
+
+
+def nn_dot(a, b):
+    return lax.dot_general(a, b, (((1,), (0,)), ((), ())), preferred_element_type=F32)
+
+
+def tn_dot(a, b):
+    return lax.dot_general(a, b, (((0,), (0,)), ((), ())), preferred_element_type=F32)
+
+
+def contract_block(f_ref, b_ref, lanes):
+    def add(total, term):
+        return term if total is None else total + term
+
+    def load(ref, ri, row, pair):
+        both = ref[0, ri, row, 2 * pair : 2 * pair + 2, :, lanes].astype(F32)
+        return (both[0], both[1])
+
+    real, imag = ([None] * 16, [None] * 16)
+    for colour in range(3):
+        for pair in range(6):
+            back = [[load(b_ref, ri, 3 * s + colour, pair) for ri in (0, 1)] for s in range(4)]
+            forw = [[load(f_ref, ri, 3 * u + colour, pair) for ri in (0, 1)] for u in range(4)]
+            for h in (0, 1):
+                for s in range(4):
+                    b_re, b_im = (back[s][0][h], back[s][1][h])
+                    for u in range(4):
+                        f_re, f_im = (forw[u][0][h], forw[u][1][h])
+                        k = 4 * s + u
+                        real[k] = add(real[k], b_re * f_re + b_im * f_im)
+                        imag[k] = add(imag[k], b_re * f_im - b_im * f_re)
+    return (real, imag)
+
+
+def pair_kernel(first, halves, f_ref, b_ref, high_ref, low_ref, *rest):
+    pos = lax.axis_index("sy")
+    if first == "listed":
+        (old_ref, tm_high_ref, tm_low_ref, rot_ref, last_ref) = rest[:5]
+        rest = rest[5:]
+    elif first == "again":
+        rest = rest[1:]
+    sends = [rest[4 * h : 4 * h + 4] for h in range(halves)]
+    rest = rest[4 * halves :]
+    field_ref = rest[0]
+    step = pl.program_id(0)
+    w_high = jnp.concatenate([high_ref[pos ^ s] for s in range(4)], 0)
+    w_low = jnp.concatenate([low_ref[pos ^ s] for s in range(4)], 0)
+    for part in range(2):
+        lanes = pl.ds(128 * part, 128)
+        real, imag = contract_block(f_ref, b_ref, lanes)
+        for k in range(16):
+            field_ref[k, 0, :, lanes] = real[k]
+            field_ref[k, 1, :, lanes] = imag[k]
+
+    def planes(ref, part):
+        lanes = pl.ds(128 * part, 128)
+        re_high, re_low = split(ref[:, 0, :, lanes].reshape(128, 128))
+        im_high, im_low = split(ref[:, 1, :, lanes].reshape(128, 128))
+        return (
+            jnp.concatenate([re_high, im_high], 1),
+            jnp.concatenate([re_low, im_low], 1),
+        )
+
+    if first == "listed":
+        total_ref = rest[1]
+
+        @pl.when(step == 0)
+        def _():
+            total_ref[...] = jnp.zeros_like(total_ref)
+
+    for part in range(2):
+        high, low = planes(field_ref, part)
+        out = nt_dot(w_high, high) + nt_dot(w_low, high) + nt_dot(w_high, low)
+        out = out.reshape(4, halves, 8 // halves, 8, 128)
+        row = 2 * step + part
+        for s in range(4):
+            for h in range(halves):
+                if first == "listed" and h == 0:
+                    sends[h][s][pl.ds(4 * row, 4)] = out[s, h]
+                else:
+                    sends[h][s][row] = out[s, h]
+        if first == "listed":
+            for t, source in enumerate((old_ref, field_ref)):
+                if t == 0:
+                    high, low = planes(old_ref, part)
+                else:
+                    high, low = planes(field_ref, part)
+                proj = (
+                    nn_dot(high, tm_high_ref[...])
+                    + nn_dot(high, tm_low_ref[...])
+                    + nn_dot(low, tm_high_ref[...])
+                )
+                value, turned = (proj[:, :128], proj[:, 128:])
+                cosine = rot_ref[row, 0:1]
+                sine = rot_ref[row, 1:2]
+                total_ref[t, 0] += cosine * value + sine * turned
+                total_ref[t, 1] += cosine * turned - sine * value
+
+    if first == "listed":
+
+        @pl.when(step == pl.num_programs(0) - 1)
+        def _():
+            upper = lax.broadcasted_iota(jnp.int32, (8, 128), 1) >= 64
+            for t in range(2):
+                value = total_ref[t, 0].reshape(16, 8, 128)
+                turned = total_ref[t, 1].reshape(16, 8, 128)
+                phased = value * last_ref[0][None] + turned * last_ref[1][None]
+                summed = jnp.sum(phased, 1)
+                tile = jnp.where(upper, summed[8:], summed[:8])
+                for s in range(4):
+                    sends[0][s][32 + t] = tile
+
+
+def pair_call(first, which, start, rows, halves, forward, backward, tables, extra):
+    steps = rows // 2
+    high, low = tables
+
+    def block(step):
+        return (which, 0, 0, 0, 0, start // 2 + step)
+
+    def field_block(step):
+        return (0, 0, 0, start // 2 + step)
+
+    def whole(shape):
+        return pl.BlockSpec(shape, lambda step: (0,) * len(shape))
+
+    in_specs = [pl.BlockSpec((1, 2, 12, 12, 8, 256), block)] * 2 + [whole((4, 64, 256))] * 2
+    operands = [forward, backward, high, low]
+    shapes = []
+    for h in range(halves):
+        shape = (rows, 8 // halves, 8, 128)
+        if first == "listed" and h == 0:
+            shape = (4 * rows + 2, 8, 128)
+        shapes += [shape] * 4
+    out_shape = [jax.ShapeDtypeStruct(shape, F32) for shape in shapes]
+    out_specs = [whole(shape) for shape in shapes]
+    fields = jax.ShapeDtypeStruct((16, 2, 8, 1024), F32)
+    field_spec = pl.BlockSpec((16, 2, 8, 256), field_block)
+    aliases = {}
+    scratch = []
+    if first == "listed":
+        in_specs += [field_spec] + [whole(x.shape) for x in extra[1:]]
+        operands += extra
+        scratch = [pltpu.VMEM((16, 2, 8, 256), F32), pltpu.VMEM((2, 2, 128, 128), F32)]
+    else:
+        out_shape.append(fields)
+        out_specs.append(field_spec)
+        if first == "again":
+            in_specs.append(pl.BlockSpec(memory_space=pl.ANY))
+            operands += extra
+            aliases = {4: len(out_shape) - 1}
+    out = pl.pallas_call(
+        functools.partial(pair_kernel, first, halves),
+        grid=(steps,),
+        in_specs=in_specs,
+        out_specs=out_specs,
+        out_shape=out_shape,
+        scratch_shapes=scratch,
+        input_output_aliases=aliases,
+        compiler_params=pltpu.CompilerParams(vmem_limit_bytes=40 * MIB),
+        cost_estimate=pl.CostEstimate(
+            flops=rows * 1024 * 16 * 36 * 8, bytes_accessed=rows * 1024 * 1300, transcendentals=0
+        ),
+        name="contract_and_z",
+    )(*operands)
+    messages = [out[4 * h : 4 * h + 4] for h in range(halves)]
+    return (messages, out[4 * halves :])
+
+
+def y_kernel(parts, listed, *refs):
+    messages = [refs[4 * part : 4 * part + 4] for part in range(parts)]
+    high_ref, low_ref, send_ref, work_ref = refs[4 * parts :]
+    rows = 8 // parts
+    for q in range(4):
+        data = []
+        for s in range(4):
+            for part in range(parts):
+                ref = messages[part][s]
+                if listed:
+                    data += [ref[4 * yb + q] for yb in range(rows)]
+                else:
+                    data += [ref[yb, q] for yb in range(rows)]
+        data = jnp.concatenate(data, 0)
+        high, low = split(data)
+        out = nn_dot(high_ref[...], high) + nn_dot(low_ref[...], high) + nn_dot(high_ref[...], low)
+        work_ref[q] = out.reshape(8, 2, 2, 8, 128)
+    for i in range(8):
+        tiles = [work_ref[q, i, p, ri] for ri in range(2) for q in range(4) for p in range(2)]
+        send_ref[i, 0:16] = jnp.concatenate(tiles, 0).T.reshape(16, 8, 128)
+    if listed:
+        ours = messages[0]
+        for t in range(2):
+            tile = (ours[0][32 + t] + ours[1][32 + t]) + (ours[2][32 + t] + ours[3][32 + t])
+            for i in range(8):
+                send_ref[i, 16 + t] = tile
+
+
+def y_call(half, listed, messages, tables):
+    high, low = tables
+
+    def whole(shape):
+        return pl.BlockSpec(shape, lambda step: (0,) * len(shape))
+
+    in_specs = []
+    operands = []
+    for part in messages:
+        for message in part:
+            if half is None:
+                in_specs.append(whole(message.shape))
+            else:
+                shape = (message.shape[0], 4, 8, 128)
+                in_specs.append(pl.BlockSpec(shape, lambda step: (0, half, 0, 0)))
+            operands.append(message)
+    tiles = 18 if listed else 16
+    return pl.pallas_call(
+        functools.partial(y_kernel, len(messages), listed),
+        grid=(1,),
+        in_specs=in_specs + [whole((256, 256))] * 2,
+        out_specs=whole((8, tiles, 8, 128)),
+        out_shape=jax.ShapeDtypeStruct((8, tiles, 8, 128), F32),
+        scratch_shapes=[pltpu.VMEM((4, 8, 2, 2, 8, 128), F32)],
+        compiler_params=pltpu.CompilerParams(vmem_limit_bytes=32 * MIB),
+        cost_estimate=pl.CostEstimate(
+            flops=12 * 256 * 256 * 256, bytes_accessed=2**20, transcendentals=0
+        ),
+        name="along_y",
+    )(*operands, high, low)
+
+
+def x_kernel(listed, aliased, table_ref, data_ref, turn_ref, *refs):
+    if aliased:
+        refs = refs[1:]
+    if listed:
+        w_ref, out_ref, listed_ref, work_ref = refs
+    else:
+        w_ref, out_ref, work_ref = refs
+    weights = w_ref[...]
+    lower = lax.broadcasted_iota(jnp.int32, (8, 128), 1) < 64
+    for f in range(16):
+        high, low = split(data_ref[:, f].reshape(64, 128))
+        out = tn_dot(jnp.concatenate([high, low, high], 0), weights)
+        cosine = out[:, :128].reshape(2, 4, 2, 8, 128)
+        sine = out[:, 128:].reshape(2, 4, 2, 8, 128)
+        real = cosine[0] + sine[1]
+        imag = cosine[1] - sine[0]
+        for q in range(4):
+            lanes = pl.ds(128 * q, 128)
+            work_ref[f, 0, :, lanes] = jnp.where(lower, real[q, 0], real[q, 1])
+            work_ref[f, 1, :, lanes] = jnp.where(lower, imag[q, 0], imag[q, 1])
+    for g in range(16):
+        real = jnp.zeros((8, 512), F32)
+        imag = jnp.zeros((8, 512), F32)
+        for s in range(4):
+            field = 4 * s + table_ref[8 * g + 2 * s]
+            power = table_ref[8 * g + 2 * s + 1]
+            odd = power % 2
+            sign_re = jnp.where((power == 0) | (power == 3), 1.0, -1.0).astype(F32)
+            sign_im = jnp.where(power < 2, 1.0, -1.0).astype(F32)
+            real += sign_re * work_ref[field, odd]
+            imag += sign_im * work_ref[field, 1 - odd]
+        cosine, sine = (turn_ref[0], turn_ref[1])
+        out_ref[g, 0, 0] = real * cosine - imag * sine
+        out_ref[g, 0, 1] = real * sine + imag * cosine
+    if listed:
+        for t in range(2):
+            total = data_ref[0, 16 + t]
+            for source in range(1, 8):
+                total = total + data_ref[source, 16 + t]
+            listed_ref[t] = total
+
+
+def x_call(which, half, listed, data, gammas, turns, weights, corr):
+    def whole(shape):
+        return pl.BlockSpec(shape, lambda step: (0,) * len(shape))
+
+    in_specs = [
+        pl.BlockSpec(memory_space=pltpu.SMEM),
+        whole(data.shape),
+        pl.BlockSpec((2, 8, 512), lambda step: (0, 0, half)),
+    ]
+    operands = [gammas, data, turns]
+    aliases = {}
+    if corr is not None:
+        aliases = {3: 0}
+        in_specs.append(pl.BlockSpec(memory_space=pl.ANY))
+        operands.append(corr)
+    in_specs.append(whole(weights.shape))
+    operands.append(weights)
+    out_shape = [jax.ShapeDtypeStruct((16, 2, 2, 8, 1024), F32)]
+    out_specs = [pl.BlockSpec((16, 1, 2, 8, 512), lambda step: (0, which, 0, 0, half))]
+    if listed:
+        out_shape.append(jax.ShapeDtypeStruct((2, 8, 128), F32))
+        out_specs.append(whole((2, 8, 128)))
+    return pl.pallas_call(
+        functools.partial(x_kernel, listed, corr is not None),
+        grid=(1,),
+        in_specs=in_specs,
+        out_specs=out_specs,
+        out_shape=out_shape,
+        scratch_shapes=[pltpu.VMEM((16, 2, 8, 512), F32)],
+        input_output_aliases=aliases,
+        compiler_params=pltpu.CompilerParams(vmem_limit_bytes=32 * MIB),
+        cost_estimate=pl.CostEstimate(
+            flops=6 * 16 * 128 * 64 * 256, bytes_accessed=2**20, transcendentals=0
+        ),
+        name="along_x",
+    )(*operands)
+
+
+def wave_angle(index):
+    return 2.0 * math.pi / L * jnp.mod(index, L).astype(F32)
+
+
+def momentum_tables(momenta, source_site):
+    lane = jnp.arange(128, dtype=jnp.int32)
+    mom = momenta[lane % 32]
+    column = jnp.arange(256, dtype=jnp.int32)
+    mom2 = momenta[column % 32]
+    part_out = (column // 32) % 2
+    turned = column // 128
+    row = jnp.arange(256, dtype=jnp.int32)
+    part_in = row // 128
+    y = (row // 64) % 2
+    z = row % 64
+    index = y[:, None] * mom2[None, :, 1] + z[:, None] * mom2[None, :, 2]
+    steps = index + 16 * (part_out + turned)[None, :] - 16 * part_in[:, None]
+    table = jnp.cos(wave_angle(steps))
+    high = lax.reduce_precision(table, 8, 7)
+    tm_high, tm_low = (high.astype(BF16), (table - high).astype(BF16))
+    pairs = jnp.arange(8, dtype=jnp.int32)
+    angle = wave_angle(2 * pairs[:, None] * mom[None, :, 1])
+    rot = jnp.stack([jnp.cos(angle), jnp.sin(angle)], 1)
+    x = lax.axis_index("sx") * 8 + jnp.arange(8, dtype=jnp.int32) - source_site[0]
+    rest = (lax.axis_index("sy") * 16 - source_site[1]) * mom[:, 1] - source_site[2] * mom[:, 2]
+    angle = wave_angle(x[:, None] * mom[None, :, 0] + rest[None, :])
+    last = jnp.stack([jnp.cos(angle), jnp.sin(angle)], 0)
+    return [tm_high, tm_low, rot, last]
+
+
+def source_turns(source_site):
+    ky = lax.axis_index("sx") * 8 + jnp.arange(8, dtype=jnp.int32)
+    kz = lax.axis_index("sy") * 16 + jnp.arange(16, dtype=jnp.int32)
+    kx = jnp.arange(64, dtype=jnp.int32)
+    index = (
+        (ky * source_site[1])[:, None, None]
+        + (kz * source_site[2])[None, :, None]
+        + (kx * source_site[0])[None, None, :]
+    )
+    angle = wave_angle(index).reshape(8, 1024)
+    return jnp.stack([jnp.cos(angle), jnp.sin(angle)], 0)
+
+
+def swap_sy(message):
+    out = [message[0]]
+    for step in range(1, 4):
+        out.append(lax.ppermute(message[step], "sy", [(k, k ^ step) for k in range(4)]))
+    return out
+
+
+def block_body(forward_prop, backward_prop, gamma_table, source_site, momenta):
+    z_tables = [jnp.asarray(table) for table in table_z()]
+    y_tables = [
+        lax.dynamic_index_in_dim(jnp.asarray(table), lax.axis_index("sy"), 0, keepdims=False)
+        for table in table_y()
+    ]
+    weights = jnp.asarray(table_x())
+    gammas = gamma_table.reshape(-1)
+    inputs = (forward_prop, backward_prop, z_tables)
+    (first,), (fields,) = pair_call("first", 0, 0, 4, 1, *inputs, [])
+    first = swap_sy(first)
+    (second,), (fields,) = pair_call("again", 0, 4, 4, 1, *inputs, [fields])
+    second = swap_sy(second)
+    extra = [fields] + momentum_tables(momenta, source_site)
+    messages, _ = pair_call("listed", 1, 0, 8, 2, *inputs, extra)
+    third = swap_sy(messages[0])
+    fourth = swap_sy(messages[1])
+    turns = source_turns(source_site)
+    corr = None
+    chunks = [
+        (0, 0, False, 0, [first, second]),
+        (0, 1, False, 1, [first, second]),
+        (1, 0, True, None, [third]),
+        (1, 1, False, None, [fourth]),
+    ]
+    for which, half, listed, pick, parts in chunks:
+        sent = y_call(pick, listed, parts, y_tables)
+        data = lax.all_to_all(sent, "sx", 0, 0, tiled=True)
+        out = x_call(which, half, listed, data, gammas, turns, weights, corr)
+        corr = out[0]
+        if listed:
+            sums = out[1]
+    sums = sums.reshape(2, 8, 2, 2, 32).transpose(0, 2, 1, 3, 4).reshape(2, 16, 2, 32)
+    mat_re, mat_im = gamma_matrices(gamma_table)
+    listed_re = jnp.einsum("gf,tfm->gtm", mat_re, sums[:, :, 0], precision=HIGHEST) - jnp.einsum(
+        "gf,tfm->gtm", mat_im, sums[:, :, 1], precision=HIGHEST
+    )
+    listed_im = jnp.einsum("gf,tfm->gtm", mat_re, sums[:, :, 1], precision=HIGHEST) + jnp.einsum(
+        "gf,tfm->gtm", mat_im, sums[:, :, 0], precision=HIGHEST
+    )
+    return (corr, jnp.stack([listed_re, listed_im], 0))
+
+
+def body(forward_prop, backward_prop, gamma_table, source_site, momenta):
+    sizes = (forward_prop.shape, lax.axis_size("sx"), lax.axis_size("sy"))
+    fits = sizes == ((2, 2, 12, 12, 8, 16 * LZ), 8, 4) and L == 64 and LZ == 64
+    fits = fits and gamma_table.shape[0] == 16 and momenta.shape[0] == 32
+    run = block_body if fits else general_body
+    return run(forward_prop, backward_prop, gamma_table, source_site, momenta)
+
+
 def solution(mesh):
     placed = (
         P(None, None, None, None, "sx", "sy"),

time: 1140 us -> 117 us (0.10); the launches traced: 1120 us -> 116 us
  local copies, waits for them, and re-layouts: 425 us -> 14.4 us
  matrix products: 318 us -> 0.81 us
  waiting for transfers between devices: 284 us -> 27.9 us
  blocking collectives: 41.3 us -> 0 us
  Pallas kernels: 0 us -> 36.2 us
  starting transfers between devices: 4.53 us -> 30.3 us
  other arithmetic: 29.7 us -> 5.13 us
  between operations: 14.7 us -> 1.61 us
    dot_general x24 -> x4, matrix products: 318 us -> 0.81 us  [the longest x1 0.21 us: block_body(): jnp.einsum('gf,tfm->gtm', mat_im, sums[:, :, 1], precision=HIGHEST)]
    all_gather x1 -> x0, waiting for transfers between devices: 284 us -> none  [transform(): lax.all_gather(along_z, 'sy', axis=3, tiled=True)]
    unnamed x35 -> x27, local copies, waits for them, and re-layouts: 258 us -> 10.7 us
    psum x1 -> x0, blocking collectives: 41.3 us -> none  [body(): listed_re, listed_im = lax.psum((local_re, local_im), ('sx', 'sy'))]
    pallas_call x0 -> x11, Pallas kernels: none -> 36.2 us  [the longest x3 21.2 us: pair_call(): pl.pallas_call(functools.partial(pair_kernel, first, halves), grid=(steps...]
    reshape x2, local copies, waits for them, and re-layouts: 31.4 us -> 0.23 us  [the longest x1 0.15 us: block_body(): gammas = gamma_table.reshape(-1)]
    sub x2 -> x0, local copies, waits for them, and re-layouts: 29.1 us -> none  [the longest x1 26.6 us: body(): jnp.einsum(pattern, backward[:, 0], forward[:, 1], preferred_element_type...]
    add x2 -> x4, local copies, waits for them, and re-layouts: 27.8 us -> 0.24 us  [source_turns(): (ky * source_site[1])[:, None, None] + (kz * source_site[2])[None, :, None]]
  transfers between devices with their start and end apart: 2 -> 16, of which waited for: 1 -> 7; matrix products, arithmetic and copies ran while one was open for 2% -> 9% of each run, Pallas kernels for 0% -> 24%
where the time goes in v1:
time: 117 us; the launch traced here: 116 us
  Pallas kernels  36.2 us (31%)
  starting transfers between devices  30.3 us (26%)
  waiting for transfers between devices  27.9 us (24%)
  local copies, waits for them, and re-layouts  14.4 us (12%)
  other arithmetic  5.13 us (4%)
  between operations  1.61 us (1%)
    pallas_call x3, Pallas kernels, pair_call(): pl.pallas_call(functools.partial(pair_kernel, first, halves), grid=(steps...  21.2 us
    ppermute x12, waiting for transfers between devices, swap_sy(): lax.ppermute(message[step], 'sy', [(k, k ^ step) for k in range(4)])  18 us
    all_to_all x4, starting transfers between devices, block_body(): data = lax.all_to_all(sent, 'sx', 0, 0, tiled=True)  15.6 us
    ppermute x12, starting transfers between devices, swap_sy(): lax.ppermute(message[step], 'sy', [(k, k ^ step) for k in range(4)])  14.7 us
    unnamed x27, local copies, waits for them, and re-layouts  10.7 us
    all_to_all x4, waiting for transfers between devices, block_body(): data = lax.all_to_all(sent, 'sx', 0, 0, tiled=True)  9.91 us
    pallas_call x4, Pallas kernels, x_call(): pl.pallas_call(functools.partial(x_kernel, listed, corr is not None), gri...  9.03 us
    pallas_call x4, Pallas kernels, y_call(): pl.pallas_call(functools.partial(y_kernel, len(messages), listed), grid=(...  6.02 us
  transfers between devices with their start and end apart: 16, of which 7 were waited for; matrix products, arithmetic and copies ran while one was open for 9% of the time, Pallas kernels for 24%

profile of v1, /device:TPU:16, one launch (start us, length us, event | category | flops | bytes accessed | tf_op | source)
XLA Modules:
  0.0 116.4 jit_solution(1787425827502829057)
XLA Ops:
  0.6 3.7 %copy-done = bf16[2,2,12,12,8,1024]{5,4,3,2,1,0:T(8,128)(2,1)S(1)} copy-done((bf16[2,2,12,12,8,1024]{5,4,3,2,1,0:T(8,128)(2,1)S(1)}, bf16[2,2,12,12,8,1024]{5,4,3,2,1,0:T(8,128)(2,1)}, u32[]{:S(2)}) %copy-start) | copy-done | bytes 9437208
  4.3 0.9 copy-done.3
  5.2 0.9 copy-done.5
  6.1 4.8 %contract_and_z.3 = (f32[4,8,8,128]{3,2,1,0:T(8,128)S(1)}, f32[4,8,8,128]{3,2,1,0:T(8,128)S(1)}, f32[4,8,8,128]{3,2,1,0:T(8,128)S(1)}, f32[4,8,8,128]{3,2,1,0:T(8,128)S(1)}, f32[16,2,8,1024]{3,2,1,0:T(8,128)S(1)}) custom-call(bf16[2,2,12,12,8,1024]{5,4,3,2,1,0:T(8,128)(2,1)S(1)} %copy-done, bf16[2,2,12,12,8,1024]{5,4,3,2,1,0:T(8,128)(2,1)} %b_ref.5, ...), custom_call_target="tpu_custom_call" | custom-call | flops 18874368 | bytes 5324800 | tf_op jit(solution)/shard_map/contract_and_z/pallas_call | solution.py:348
  11.0 1.6 %collective-permute-start.6 = (f32[4,8,8,128]{3,2,1,0:T(8,128)S(1)}, f32[4,8,8,128]{3,2,1,0:T(8,128)S(1)}, u32[]{:S(2)}, u32[]{:S(2)}) collective-permute-start(f32[4,8,8,128]{3,2,1,0:T(8,128)S(1)} %get-tuple-element.33), channel_id=1, source_target_pairs={{0,1},{1,0},{2,3},{3,2},{4,5},{5,4},{6,7},{7,6},{8,9},{9,8},{10,11... | collective-permute-start | bytes 393224 | tf_op jit(solution)/shard_map/ppermute | solution.py:552
  12.6 0.3 collective-permute-start.7
  13.0 1.6 %collective-permute-start.8 = (f32[4,8,8,128]{3,2,1,0:T(8,128)S(1)}, f32[4,8,8,128]{3,2,1,0:T(8,128)S(1)}, u32[]{:S(2)}, u32[]{:S(2)}) collective-permute-start(f32[4,8,8,128]{3,2,1,0:T(8,128)S(1)} %get-tuple-element.35), channel_id=1, source_target_pairs={{0,3},{1,2},{2,1},{3,0},{4,7},{5,6},{6,5},{7,4},{8,11},{9,10},{10,... | collective-permute-start | bytes 393224 | tf_op jit(solution)/shard_map/ppermute | solution.py:552
  14.5 4.9 %contract_and_z.4 = (f32[4,8,8,128]{3,2,1,0:T(8,128)S(1)}, f32[4,8,8,128]{3,2,1,0:T(8,128)S(1)}, f32[4,8,8,128]{3,2,1,0:T(8,128)S(1)}, f32[4,8,8,128]{3,2,1,0:T(8,128)S(1)}, f32[16,2,8,1024]{3,2,1,0:T(8,128)S(1)}) custom-call(bf16[2,2,12,12,8,1024]{5,4,3,2,1,0:T(8,128)(2,1)S(1)} %copy-done, ...), custom_call_target="tpu_custom_call", output_to_operand_aliasing={{4}: (4, {})} | custom-call | flops 18874368 | bytes 5324800 | tf_op jit(solution)/shard_map/contract_and_z/pallas_call | solution.py:348
  19.4 2.5 %collective-permute-start.9 = (f32[4,8,8,128]{3,2,1,0:T(8,128)S(1)}, f32[4,8,8,128]{3,2,1,0:T(8,128)S(1)}, u32[]{:S(2)}, u32[]{:S(2)}) collective-permute-start(f32[4,8,8,128]{3,2,1,0:T(8,128)S(1)} %get-tuple-element.37), channel_id=1, source_target_pairs={{0,1},{1,0},{2,3},{3,2},{4,5},{5,4},{6,7},{7,6},{8,9},{9,8},{10,11... | collective-permute-start | bytes 393224 | tf_op jit(solution)/shard_map/ppermute | solution.py:552
  22.1 0.6 fusion.36
  22.7 0.6 gather_fusion.1
  23.4 0.8 slice_reduce_fusion.2
  25.1 1.3 %fusion.34 = (s32[8]{0:T(128)S(1)}, s32[8]{0:T(128)S(1)}) fusion(s32[]{:T(128)} %bitcast.4, s32[]{:T(128)S(6)} %mul.266, s32[]{:T(128)} %bitcast.3), kind=kLoop, calls=%fused_computation.103 | loop fusion | flops 24 | bytes 76 | tf_op jit(solution)/shard_map/mul | solution.py:541
  26.5 0.7 gather_fusion
  27.3 0.2 slice_reduce_fusion.1
  27.5 1.6 %collective-permute-start.11 = (f32[4,8,8,128]{3,2,1,0:T(8,128)S(1)}, f32[4,8,8,128]{3,2,1,0:T(8,128)S(1)}, u32[]{:S(2)}, u32[]{:S(2)}) collective-permute-start(f32[4,8,8,128]{3,2,1,0:T(8,128)S(1)} %get-tuple-element.39), channel_id=1, source_target_pairs={{0,3},{1,2},{2,1},{3,0},{4,7},{5,6},{6,5},{7,4},{8,11},{9,10},{10,... | collective-permute-start | bytes 393224 | tf_op jit(solution)/shard_map/ppermute | solution.py:552
  29.1 1.0 dynamic-slice_bitcast_fusion
  30.1 1.2 %collective-permute-done.8.refs_3_ = f32[4,8,8,128]{3,2,1,0:T(8,128)S(1)} collective-permute-done((f32[4,8,8,128]{3,2,1,0:T(8,128)S(1)}, f32[4,8,8,128]{3,2,1,0:T(8,128)S(1)}, u32[]{:S(2)}, u32[]{:S(2)}) %collective-permute-start.8) | collective-permute-done | bytes 131104 | tf_op jit(solution)/shard_map/ppermute | solution.py:552
  31.4 1.0 collective-permute-done.10.refs_6_
  32.4 4.8 %collective-permute-done.11.refs_7_ = f32[4,8,8,128]{3,2,1,0:T(8,128)S(1)} collective-permute-done((f32[4,8,8,128]{3,2,1,0:T(8,128)S(1)}, f32[4,8,8,128]{3,2,1,0:T(8,128)S(1)}, u32[]{:S(2)}, u32[]{:S(2)}) %collective-permute-start.11) | collective-permute-done | bytes 131104 | tf_op jit(solution)/shard_map/ppermute | solution.py:552
  37.2 1.5 %along_y.6 = f32[8,16,8,128]{3,2,1,0:T(8,128)} custom-call(f32[4,8,8,128]{3,2,1,0:T(8,128)S(1)} %get-tuple-element.32.refs_0_, f32[4,8,8,128]{3,2,1,0:T(8,128)S(1)} %collective-permute-done.6.refs_1_, f32[4,8,8,128]{3,2,1,0:T(8,128)S(1)} %collective-permute-done.7.refs_2_, f32[4,8,8,128]{3,2,1,0:T(8,128)S(1)} %collective-permute-done.8.refs_3_, ...), custom_call_target="tpu_custom_call" | custom-call | flops 201326592 | bytes 1048576 | tf_op jit(solution)/shard_map/along_y/pallas_call | solution.py:411
  38.7 3.7 %all-to-all-start.2 = ((f32[8,16,8,128]{3,2,1,0:T(8,128)}), f32[8,16,8,128]{3,2,1,0:T(8,128)S(1)}, u32[]{:S(2)}, u32[]{:S(2)}) async-start(f32[8,16,8,128]{3,2,1,0:T(8,128)} %along_y.6), calls=%async_computation.2 | async-start | bytes 1048576 | tf_op jit(solution)/shard_map/all_to_all | solution.py:583
  42.4 1.1 fusion.2
  43.5 3.7 %copy-done.1 = bf16[2,2,12,12,8,1024]{5,4,3,2,1,0:T(8,128)(2,1)S(1)} copy-done((bf16[2,2,12,12,8,1024]{5,4,3,2,1,0:T(8,128)(2,1)S(1)}, bf16[2,2,12,12,8,1024]{5,4,3,2,1,0:T(8,128)(2,1)}, u32[]{:S(2)}) %copy-start.1) | copy-done | bytes 9437208
  47.2 11.5 %contract_and_z.5 = (f32[34,8,128]{2,1,0:T(8,128)S(1)}, f32[34,8,128]{2,1,0:T(8,128)}, f32[34,8,128]{2,1,0:T(8,128)}, f32[34,8,128]{2,1,0:T(8,128)}, f32[8,4,8,1...) custom-call(bf16[2,2,12,12,8,1024]{5,4,3,2,1,0:T(8,128)(2,1)S(1)} %copy-d, ...), custom_call_target="tpu_custom_call" | custom-call | flops 37748736 | bytes 10649600 | tf_op jit(solution)/shard_map/contract_and_z/pallas_call | solution.py:348
  58.7 0.6 copy-done.7
  59.3 1.9 %collective-permute-start.1 = (f32[8,4,8,128]{3,2,1,0:T(8,128)}, f32[8,4,8,128]{3,2,1,0:T(8,128)S(1)}, u32[]{:S(2)}, u32[]{:S(2)}) collective-permute-start(f32[8,4,8,128]{3,2,1,0:T(8,128)} %get-tuple-element.26), channel_id=1, source_target_pairs={{0,2},{1,3},{2,0},{3,1},{4,6},{5,7},{6,4},{7,5},{8,10},{9,11},{10,... | collective-permute-start | bytes 393224 | tf_op jit(solution)/shard_map/ppermute | solution.py:552
  61.3 0.3 collective-permute-start.3
  61.6 2.7 %collective-permute-start.4 = (f32[34,8,128]{2,1,0:T(8,128)}, f32[34,8,128]{2,1,0:T(8,128)S(1)}, u32[]{:S(2)}, u32[]{:S(2)}) collective-permute-start(f32[34,8,128]{2,1,0:T(8,128)} %get-tuple-element.30), channel_id=1, source_target_pairs={{0,2},{1,3},{2,0},{3,1},{4,6},{5,7},{6,4},{7,5},{8,10},{9,11},{10,... | collective-permute-start | bytes 417800 | tf_op jit(solution)/shard_map/ppermute | solution.py:552
  64.3 0.5 collective-permute-start.5
  64.8 0.6 add_multiply_fusion
  65.4 1.5 %along_y.7 = f32[8,16,8,128]{3,2,1,0:T(8,128)} custom-call(f32[4,8,8,128]{3,2,1,0:T(8,128)S(1)} %get-tuple-element.32.refs_0_, f32[4,8,8,128]{3,2,1,0:T(8,128)S(1)} %collective-permute-done.6.refs_1_, f32[4,8,8,128]{3,2,1,0:T(8,128)S(1)} %collective-permute-done.7.refs_2_, f32[4,8,8,128]{3,2,1,0:T(8,128)S(1)} %collective-permute-done.8.refs_3_, ...), custom_call_target="tpu_custom_call" | custom-call | flops 201326592 | bytes 1048576 | tf_op jit(solution)/shard_map/along_y/pallas_call | solution.py:411
  66.9 4.3 %all-to-all-start.3 = ((f32[8,16,8,128]{3,2,1,0:T(8,128)}), f32[8,16,8,128]{3,2,1,0:T(8,128)S(1)}, u32[]{:S(2)}, u32[]{:S(2)}) async-start(f32[8,16,8,128]{3,2,1,0:T(8,128)} %along_y.7), calls=%async_computation.3 | async-start | bytes 1048576 | tf_op jit(solution)/shard_map/all_to_all | solution.py:583
  71.5 0.7 iota_multiply_fusion
  72.4 1.6 %collective-permute-start.2 = (f32[8,4,8,128]{3,2,1,0:T(8,128)S(1)}, f32[8,4,8,128]{3,2,1,0:T(8,128)S(1)}, u32[]{:S(2)}, u32[]{:S(2)}) collective-permute-start(f32[8,4,8,128]{3,2,1,0:T(8,128)S(1)} %copy-done.8), channel_id=1, source_target_pairs={{0,3},{1,2},{2,1},{3,0},{4,7},{5,6},{6,5},{7,4},{8,11},{9,10},{10,... | collective-permute-start | bytes 393224 | tf_op jit(solution)/shard_map/ppermute | solution.py:552
  74.0 5.7 %collective-permute-done.4.refs_2_ = f32[34,8,128]{2,1,0:T(8,128)S(1)} collective-permute-done((f32[34,8,128]{2,1,0:T(8,128)}, f32[34,8,128]{2,1,0:T(8,128)S(1)}, u32[]{:S(2)}, u32[]{:S(2)}) %collective-permute-start.4) | collective-permute-done | bytes 139296 | tf_op jit(solution)/shard_map/ppermute | solution.py:552
  79.7 5.3 %collective-permute-done.5.refs_3_ = f32[34,8,128]{2,1,0:T(8,128)S(1)} collective-permute-done((f32[34,8,128]{2,1,0:T(8,128)}, f32[34,8,128]{2,1,0:T(8,128)S(1)}, u32[]{:S(2)}, u32[]{:S(2)}) %collective-permute-start.5) | collective-permute-done | bytes 139296 | tf_op jit(solution)/shard_map/ppermute | solution.py:552
  85.0 1.5 %along_y.5 = f32[8,18,8,128]{3,2,1,0:T(8,128)} custom-call(f32[34,8,128]{2,1,0:T(8,128)S(1)} %get-tuple-element.28.refs_0_, f32[34,8,128]{2,1,0:T(8,128)S(1)} %collective-permute-done.3.refs_1_, f32[34,8,128]{2,1,0:T(8,128)S(1)} %collective-permute-done.4.refs_2_, f32[34,8,128]{2,1,0:T(8,128)S(1)} %collective-permute-done.5.refs_3_, ...), custom_call_target="tpu_custom_call" | custom-call | flops 201326592 | bytes 1048576 | tf_op jit(solution)/shard_map/along_y/pallas_call | solution.py:411
  86.5 4.0 %all-to-all-start.1 = ((f32[8,18,8,128]{3,2,1,0:T(8,128)}), f32[8,18,8,128]{3,2,1,0:T(8,128)S(1)}, u32[]{:S(2)}, u32[]{:S(2)}) async-start(f32[8,18,8,128]{3,2,1,0:T(8,128)} %along_y.5), calls=%async_computation.1 | async-start | bytes 1179648 | tf_op jit(solution)/shard_map/all_to_all | solution.py:583
  90.9 1.5 %along_y.4 = f32[8,16,8,128]{3,2,1,0:T(8,128)} custom-call(f32[8,4,8,128]{3,2,1,0:T(8,128)S(1)} %get-tuple-element.24.refs_0_, f32[8,4,8,128]{3,2,1,0:T(8,128)S(1)} %collective-permute-done.refs_1_, f32[8,4,8,128]{3,2,1,0:T(8,128)S(1)} %collective-permute-done.1.refs_2_, f32[8,4,8,128]{3,2,1,0:T(8,128)S(1)} %collective-permute-done.2.refs_3_, ...), custom_call_target="tpu_custom_call" | custom-call | flops 201326592 | bytes 1048576 | tf_op jit(solution)/shard_map/along_y/pallas_call | solution.py:411
  92.4 2.3 %along_x.4.refs_0_ = f32[16,2,2,8,1024]{4,3,2,1,0:T(8,128)} custom-call(s32[128]{0:T(128)S(1)} %reshape.783.table_ref, f32[8,16,8,128]{3,2,1,0:T(8,128)S(1)} %all-to-all-done.3.data_ref, f32[2,8,1024]{2,1,0:T(8,128)S(1)} %pad_maximum_fusion.turn_ref, bf16[192,256]{1,0:T(8,128)(2,1)S(1)} %copy-done.2), custom_call_target="tpu_custom_call" | custom-call | flops 201326592 | bytes 1048576 | tf_op jit(solution)/shard_map/along_x/pallas_call | solution.py:490
  94.6 2.3 %along_x.5.refs_0_ = f32[16,2,2,8,1024]{4,3,2,1,0:T(8,128)} custom-call(s32[128]{0:T(128)S(1)} %reshape.783.table_ref, f32[8,16,8,128]{3,2,1,0:T(8,128)S(1)} %all-to-all-done.2.data_ref, f32[2,8,1024]{2,1,0:T(8,128)S(1)} %pad_maximum_fusion.turn_ref, f32[16,2,2,8,1024]{4,3,2,1,0:T(8,128)} %along_x.4.refs_0_, ...), custom_call_target="tpu_custom_call", output_to_operand_aliasing={{}: (3, {})} | custom-call | flops 201326592 | bytes 1048576 | tf_op jit(solution)/shard_map/along_x/pallas_call | solution.py:490
  96.9 4.1 %all-to-all-done.1.data_ref = f32[8,18,8,128]{3,2,1,0:T(8,128)S(1)} async-done(((f32[8,18,8,128]{3,2,1,0:T(8,128)}), f32[8,18,8,128]{3,2,1,0:T(8,128)S(1)}, u32[]{:S(2)}, u32[]{:S(2)}) %all-to-all-start.1) | async-done | bytes 589856 | tf_op jit(solution)/shard_map/all_to_all | solution.py:583
  101.0 3.5 %all-to-all-start = ((f32[8,16,8,128]{3,2,1,0:T(8,128)}), f32[8,16,8,128]{3,2,1,0:T(8,128)S(1)}, u32[]{:S(2)}, u32[]{:S(2)}) async-start(f32[8,16,8,128]{3,2,1,0:T(8,128)} %along_y.4), calls=%async_computation | async-start | bytes 1048576 | tf_op jit(solution)/shard_map/all_to_all | solution.py:583
  104.5 2.3 %along_x.6 = (f32[16,2,2,8,1024]{4,3,2,1,0:T(8,128)}, f32[2,8,128]{2,1,0:T(8,128)S(1)}) custom-call(s32[128]{0:T(128)S(1)} %reshape.783.table_ref, f32[8,18,8,128]{3,2,1,0:T(8,128)S(1)} %all-to-all-done.1.data_ref, f32[2,8,1024]{2,1,0:T(8,128)S(1)} %pad_maximum_fusion.turn_ref, ...), custom_call_target="tpu_custom_call", output_to_operand_aliasing={{0}: (3, {})} | custom-call | flops 201326592 | bytes 1048576 | tf_op jit(solution)/shard_map/along_x/pallas_call | solution.py:490
  107.7 0.6 copy.42
  108.3 5.8 %all-to-all-done.data_ref = f32[8,16,8,128]{3,2,1,0:T(8,128)S(1)} async-done(((f32[8,16,8,128]{3,2,1,0:T(8,128)}), f32[8,16,8,128]{3,2,1,0:T(8,128)S(1)}, u32[]{:S(2)}, u32[]{:S(2)}) %all-to-all-start) | async-done | bytes 524320 | tf_op jit(solution)/shard_map/all_to_all | solution.py:583
  114.1 2.3 %along_x.7 = f32[16,2,2,8,1024]{4,3,2,1,0:T(8,128)} custom-call(s32[128]{0:T(128)S(1)} %reshape.783.table_ref, f32[8,16,8,128]{3,2,1,0:T(8,128)S(1)} %all-to-all-done.data_ref, f32[2,8,1024]{2,1,0:T(8,128)S(1)} %pad_maximum_fusion.turn_ref, f32[16,2,2,8,1024]{4,3,2,1,0:T(8,128)} %get-tuple-element.40.refs_0_, ...), custom_call_target="tpu_custom_call", output_to_operand_aliasing={{}: (3, {})} | custom-call | flops 201326592 | bytes 1048576 | tf_op jit(solution)/shard_map/along_x/pallas_call | solution.py:490
  (64 shorter events, 2.2 us)
Async XLA Ops:
  0.6 3.7 %copy-start = (bf16[2,2,12,12,8,1024]{5,4,3,2,1,0:T(8,128)(2,1)S(1)}, bf16[2,2,12,12,8,1024]{5,4,3,2,1,0:T(8,128)(2,1)}, u32[]{:S(2)}) copy-start(bf16[2,2,12,12,8,1024]{5,4,3,2,1,0:T(8,128)(2,1)} %f_ref.5) | copy-start | bytes 28311556
  4.3 0.9 copy-start.3
  5.2 0.9 copy-start.5
  11.0 16.6 %collective-permute-start.6 = (f32[4,8,8,128]{3,2,1,0:T(8,128)S(1)}, f32[4,8,8,128]{3,2,1,0:T(8,128)S(1)}, u32[]{:S(2)}, u32[]{:S(2)}) collective-permute-start(f32[4,8,8,128]{3,2,1,0:T(8,128)S(1)} %get-tuple-element.33), channel_id=1, source_target_pairs={{0,1},{1,0},{2,3},{3,2},{4,5},{5,4},{6,7},{7,6},{8,9},{9,8},{10,11... | collective-permute-start | bytes 393224 | tf_op jit(solution)/shard_map/ppermute | solution.py:552
  12.6 17.5 %collective-permute-start.7 = (f32[4,8,8,128]{3,2,1,0:T(8,128)S(1)}, f32[4,8,8,128]{3,2,1,0:T(8,128)S(1)}, u32[]{:S(2)}, u32[]{:S(2)}) collective-permute-start(f32[4,8,8,128]{3,2,1,0:T(8,128)S(1)} %get-tuple-element.34), channel_id=1, source_target_pairs={{0,2},{1,3},{2,0},{3,1},{4,6},{5,7},{6,4},{7,5},{8,10},{9,11},{10,... | collective-permute-start | bytes 393224 | tf_op jit(solution)/shard_map/ppermute | solution.py:552
  13.0 18.4 %collective-permute-start.8 = (f32[4,8,8,128]{3,2,1,0:T(8,128)S(1)}, f32[4,8,8,128]{3,2,1,0:T(8,128)S(1)}, u32[]{:S(2)}, u32[]{:S(2)}) collective-permute-start(f32[4,8,8,128]{3,2,1,0:T(8,128)S(1)} %get-tuple-element.35), channel_id=1, source_target_pairs={{0,3},{1,2},{2,1},{3,0},{4,7},{5,6},{6,5},{7,4},{8,11},{9,10},{10,... | collective-permute-start | bytes 393224 | tf_op jit(solution)/shard_map/ppermute | solution.py:552
  14.5 7.4 %copy-start.11 = (s32[32,3]{0,1:T(4,128)S(1)}, s32[32,3]{0,1:T(4,128)}, u32[]{:S(2)}) copy-start(s32[32,3]{0,1:T(4,128)} %param.14) | copy-start | bytes 1156
  14.5 7.5 %copy-start.10 = (s32[3]{0:T(128)S(1)}, s32[3]{0:T(128)}, u32[]{:S(2)}) copy-start(s32[3]{0:T(128)} %param.13) | copy-start | bytes 40
  19.4 12.0 %collective-permute-start.9 = (f32[4,8,8,128]{3,2,1,0:T(8,128)S(1)}, f32[4,8,8,128]{3,2,1,0:T(8,128)S(1)}, u32[]{:S(2)}, u32[]{:S(2)}) collective-permute-start(f32[4,8,8,128]{3,2,1,0:T(8,128)S(1)} %get-tuple-element.37), channel_id=1, source_target_pairs={{0,1},{1,0},{2,3},{3,2},{4,5},{5,4},{6,7},{7,6},{8,9},{9,8},{10,11... | collective-permute-start | bytes 393224 | tf_op jit(solution)/shard_map/ppermute | solution.py:552
  21.9 10.5 %collective-permute-start.10 = (f32[4,8,8,128]{3,2,1,0:T(8,128)S(1)}, f32[4,8,8,128]{3,2,1,0:T(8,128)S(1)}, u32[]{:S(2)}, u32[]{:S(2)}) collective-permute-start(f32[4,8,8,128]{3,2,1,0:T(8,128)S(1)} %get-tuple-element.38), channel_id=1, source_target_pairs={{0,2},{1,3},{2,0},{3,1},{4,6},{5,7},{6,4},{7,5},{8,10},{9,11},{10,... | collective-permute-start | bytes 393224 | tf_op jit(solution)/shard_map/ppermute | solution.py:552
  27.3 16.2 %copy-start.4 = (bf16[4,64,256]{2,1,0:T(8,128)(2,1)S(1)}, bf16[4,64,256]{2,1,0:T(8,128)(2,1)}, u32[]{:S(2)}) copy-start(bf16[4,64,256]{2,1,0:T(8,128)(2,1)} %constant.173.clone.high_ref) | copy-start | bytes 393220
  27.3 16.2 %copy-start.6 = (bf16[4,64,256]{2,1,0:T(8,128)(2,1)S(1)}, bf16[4,64,256]{2,1,0:T(8,128)(2,1)}, u32[]{:S(2)}) copy-start(bf16[4,64,256]{2,1,0:T(8,128)(2,1)} %constant.174.clone.low_ref) | copy-start | bytes 393220
  27.5 9.6 %collective-permute-start.11 = (f32[4,8,8,128]{3,2,1,0:T(8,128)S(1)}, f32[4,8,8,128]{3,2,1,0:T(8,128)S(1)}, u32[]{:S(2)}, u32[]{:S(2)}) collective-permute-start(f32[4,8,8,128]{3,2,1,0:T(8,128)S(1)} %get-tuple-element.39), channel_id=1, source_target_pairs={{0,3},{1,2},{2,1},{3,0},{4,7},{5,6},{6,5},{7,4},{8,11},{9,10},{10,... | collective-permute-start | bytes 393224 | tf_op jit(solution)/shard_map/ppermute | solution.py:552
  38.7 28.3 %all-to-all-start.2 = ((f32[8,16,8,128]{3,2,1,0:T(8,128)}), f32[8,16,8,128]{3,2,1,0:T(8,128)S(1)}, u32[]{:S(2)}, u32[]{:S(2)}) async-start(f32[8,16,8,128]{3,2,1,0:T(8,128)} %along_y.6), calls=%async_computation.2 | async-start | bytes 1048576 | tf_op jit(solution)/shard_map/all_to_all | solution.py:583
  43.5 3.7 %copy-start.1 = (bf16[2,2,12,12,8,1024]{5,4,3,2,1,0:T(8,128)(2,1)S(1)}, bf16[2,2,12,12,8,1024]{5,4,3,2,1,0:T(8,128)(2,1)}, u32[]{:S(2)}) copy-start(bf16[2,2,12,12,8,1024]{5,4,3,2,1,0:T(8,128)(2,1)} %f_ref.5) | copy-start | bytes 28311556
  58.7 0.6 copy-start.7
  59.3 13.1 %copy-start.8 = (f32[8,4,8,128]{3,2,1,0:T(8,128)S(1)}, f32[8,4,8,128]{3,2,1,0:T(8,128)}, u32[]{:S(2)}) copy-start(f32[8,4,8,128]{3,2,1,0:T(8,128)} %copy-done.7) | copy-start | bytes 393220
  59.3 31.5 %collective-permute-start = (f32[8,4,8,128]{3,2,1,0:T(8,128)}, f32[8,4,8,128]{3,2,1,0:T(8,128)S(1)}, u32[]{:S(2)}, u32[]{:S(2)}) collective-permute-start(f32[8,4,8,128]{3,2,1,0:T(8,128)} %get-tuple-element.25), channel_id=1, source_target_pairs={{0,1},{1,0},{2,3},{3,2},{4,5},{5,4},{6,7},{7,6},{8,9},{9,8},{10,11... | collective-permute-start | bytes 393224 | tf_op jit(solution)/shard_map/ppermute | solution.py:552
  59.3 31.5 %collective-permute-start.1 = (f32[8,4,8,128]{3,2,1,0:T(8,128)}, f32[8,4,8,128]{3,2,1,0:T(8,128)S(1)}, u32[]{:S(2)}, u32[]{:S(2)}) collective-permute-start(f32[8,4,8,128]{3,2,1,0:T(8,128)} %get-tuple-element.26), channel_id=1, source_target_pairs={{0,2},{1,3},{2,0},{3,1},{4,6},{5,7},{6,4},{7,5},{8,10},{9,11},{10,... | collective-permute-start | bytes 393224 | tf_op jit(solution)/shard_map/ppermute | solution.py:552
  61.3 11.1 %collective-permute-start.3 = (f32[34,8,128]{2,1,0:T(8,128)}, f32[34,8,128]{2,1,0:T(8,128)S(1)}, u32[]{:S(2)}, u32[]{:S(2)}) collective-permute-start(f32[34,8,128]{2,1,0:T(8,128)} %get-tuple-element.29), channel_id=1, source_target_pairs={{0,1},{1,0},{2,3},{3,2},{4,5},{5,4},{6,7},{7,6},{8,9},{9,8},{10,11... | collective-permute-start | bytes 417800 | tf_op jit(solution)/shard_map/ppermute | solution.py:552
  61.6 18.1 %collective-permute-start.4 = (f32[34,8,128]{2,1,0:T(8,128)}, f32[34,8,128]{2,1,0:T(8,128)S(1)}, u32[]{:S(2)}, u32[]{:S(2)}) collective-permute-start(f32[34,8,128]{2,1,0:T(8,128)} %get-tuple-element.30), channel_id=1, source_target_pairs={{0,2},{1,3},{2,0},{3,1},{4,6},{5,7},{6,4},{7,5},{8,10},{9,11},{10,... | collective-permute-start | bytes 417800 | tf_op jit(solution)/shard_map/ppermute | solution.py:552
  64.3 20.7 %collective-permute-start.5 = (f32[34,8,128]{2,1,0:T(8,128)}, f32[34,8,128]{2,1,0:T(8,128)S(1)}, u32[]{:S(2)}, u32[]{:S(2)}) collective-permute-start(f32[34,8,128]{2,1,0:T(8,128)} %get-tuple-element.31), channel_id=1, source_target_pairs={{0,3},{1,2},{2,1},{3,0},{4,7},{5,6},{6,5},{7,4},{8,11},{9,10},{10,... | collective-permute-start | bytes 417800 | tf_op jit(solution)/shard_map/ppermute | solution.py:552
  66.9 23.6 %copy-start.9 = (s32[16,4,2]{0,2,1:T(2,128)S(1)}, s32[16,4,2]{0,2,1:T(2,128)}, u32[]{:S(2)}) copy-start(s32[16,4,2]{0,2,1:T(2,128)} %param.12) | copy-start | bytes 1540
  66.9 23.6 %slice-start = ((s32[16,4,2]{0,2,1:T(2,128)}), s32[16,4,1]{0,2,1:T(1,128)S(1)}, s32[]{:S(2)}) async-start(s32[16,4,2]{0,2,1:T(2,128)} %param.12), calls=%async_computation.4 | async-start | bytes 4096 | tf_op jit(solution)/shard_map/slice | solution.py:22
  66.9 19.6 %all-to-all-start.3 = ((f32[8,16,8,128]{3,2,1,0:T(8,128)}), f32[8,16,8,128]{3,2,1,0:T(8,128)S(1)}, u32[]{:S(2)}, u32[]{:S(2)}) async-start(f32[8,16,8,128]{3,2,1,0:T(8,128)} %along_y.7), calls=%async_computation.3 | async-start | bytes 1048576 | tf_op jit(solution)/shard_map/all_to_all | solution.py:583
  72.4 20.0 %copy-start.2 = (bf16[192,256]{1,0:T(8,128)(2,1)S(1)}, bf16[192,256]{1,0:T(8,128)(2,1)}, u32[]{:S(2)}) copy-start(bf16[192,256]{1,0:T(8,128)(2,1)} %constant.177.clone.refs_0_.refs_1_) | copy-start | bytes 294916
  72.4 18.5 %collective-permute-start.2 = (f32[8,4,8,128]{3,2,1,0:T(8,128)S(1)}, f32[8,4,8,128]{3,2,1,0:T(8,128)S(1)}, u32[]{:S(2)}, u32[]{:S(2)}) collective-permute-start(f32[8,4,8,128]{3,2,1,0:T(8,128)S(1)} %copy-done.8), channel_id=1, source_target_pairs={{0,3},{1,2},{2,1},{3,0},{4,7},{5,6},{6,5},{7,4},{8,11},{9,10},{10,... | collective-permute-start | bytes 393224 | tf_op jit(solution)/shard_map/ppermute | solution.py:552
  86.5 14.5 %all-to-all-start.1 = ((f32[8,18,8,128]{3,2,1,0:T(8,128)}), f32[8,18,8,128]{3,2,1,0:T(8,128)S(1)}, u32[]{:S(2)}, u32[]{:S(2)}) async-start(f32[8,18,8,128]{3,2,1,0:T(8,128)} %along_y.5), calls=%async_computation.1 | async-start | bytes 1179648 | tf_op jit(solution)/shard_map/all_to_all | solution.py:583
  101.0 13.2 %all-to-all-start = ((f32[8,16,8,128]{3,2,1,0:T(8,128)}), f32[8,16,8,128]{3,2,1,0:T(8,128)S(1)}, u32[]{:S(2)}, u32[]{:S(2)}) async-start(f32[8,16,8,128]{3,2,1,0:T(8,128)} %along_y.4), calls=%async_computation | async-start | bytes 1048576 | tf_op jit(solution)/shard_map/all_to_all | solution.py:583

commit v2 on v0

--- a/solution.py
+++ b/solution.py
@@ -1,8 +1,12 @@
+import functools
 import math
 
 import jax
 import jax.numpy as jnp
+import numpy as np
 from jax import lax
+from jax.experimental import pallas as pl
+from jax.experimental.pallas import tpu as pltpu
 from jax.sharding import PartitionSpec as P
 
 L = 64
@@ -103,7 +107,7 @@
     return (local_re, local_im)
 
 
-def body(forward_prop, backward_prop, gamma_table, source_site, momenta):
+def general_body(forward_prop, backward_prop, gamma_table, source_site, momenta):
     slices = forward_prop.shape[0]
     rows_x = forward_prop.shape[4]
     rows_y = backward_prop.shape[5] // LZ
@@ -132,6 +136,441 @@
     return (jnp.stack([corr_re, corr_im], 2), jnp.stack([listed_re, listed_im], 0))
 
 
+F32 = jnp.float32
+BF16 = jnp.bfloat16
+MIB = 2**20
+
+
+def split(values):
+    high = values.astype(BF16)
+    return (high, (values - high.astype(F32)).astype(BF16))
+
+
+def turn(out_wave, in_site):
+    angle = 2.0 * math.pi / L * np.mod(np.multiply.outer(out_wave, in_site), L)
+    cosine, sine = (np.cos(angle), np.sin(angle))
+    table = np.empty((len(out_wave), 2, 2, len(in_site)))
+    table[:, 0, 0] = cosine
+    table[:, 0, 1] = sine
+    table[:, 1, 0] = -sine
+    table[:, 1, 1] = cosine
+    return table
+
+
+def table_z():
+    wave = turn(np.arange(64), np.arange(64)).reshape(4, 2, 4, 2, 2, 2, 64)
+    full = np.zeros((4, 2, 4, 2, 2, 2, 2, 2, 64))
+    for y in range(2):
+        full[:, :, :, :, :, y, :, y, :] = wave
+    return jnp.asarray(full.reshape(4, 64, 256).astype(np.float32))
+
+
+def table_y():
+    wave = turn(np.arange(64), np.arange(64)).reshape(8, 8, 2, 2, 4, 8, 2)
+    full = np.zeros((4, 8, 2, 2, 8, 4, 8, 2, 2, 2))
+    for position in range(4):
+        for step in range(4):
+            source = position ^ step
+            for p in range(2):
+                full[position, :, p, :, :, step, :, p] = wave[:, :, :, :, source].transpose(
+                    0, 2, 1, 4, 3, 5
+                )
+    return jnp.asarray(full.reshape(4, 256, 256).astype(np.float32))
+
+
+def table_x():
+    wave = turn(np.arange(64), np.arange(64))
+    cosine, sine = (wave[:, 0, 0].T, wave[:, 0, 1].T)
+    table = np.concatenate([cosine, cosine, sine, sine], 1).astype(np.float32)
+    return jnp.asarray(table.reshape(8, 8, 256))
+
+
+def nt_dot(a, b):
+    return lax.dot_general(a, b, (((1,), (1,)), ((), ())), preferred_element_type=F32)
+
+
+def nn_dot(a, b):
+    return lax.dot_general(a, b, (((1,), (0,)), ((), ())), preferred_element_type=F32)
+
+
+def tn_dot(a, b):
+    return lax.dot_general(a, b, (((0,), (0,)), ((), ())), preferred_element_type=F32)
+
+
+def whole(shape):
+    return pl.BlockSpec(shape, lambda step: (0,) * len(shape))
+
+
+def cost(weight):
+    return pl.CostEstimate(flops=weight * 10**13, bytes_accessed=0, transcendentals=0)
+
+
+def contract_block(f_ref, b_ref):
+    def add(total, term):
+        return term if total is None else total + term
+
+    def load(ref, ri, row, pair):
+        both = ref[0, ri, row, 2 * pair : 2 * pair + 2].astype(F32)
+        return (both[0], both[1])
+
+    one, two, three = ([None] * 16, [None] * 16, [None] * 16)
+    for colour in range(3):
+        for pair in range(6):
+            back = [[load(b_ref, ri, 3 * s + colour, pair) for ri in (0, 1)] for s in range(4)]
+            forw = [[load(f_ref, ri, 3 * u + colour, pair) for ri in (0, 1)] for u in range(4)]
+            for h in (0, 1):
+                for s in range(4):
+                    b_re, b_im = (back[s][0][h], back[s][1][h])
+                    b_less, b_more = (b_re - b_im, b_re + b_im)
+                    for u in range(4):
+                        f_re, f_im = (forw[u][0][h], forw[u][1][h])
+                        f_more = f_re + f_im
+                        k = 4 * s + u
+                        one[k] = add(one[k], b_re * f_more)
+                        two[k] = add(two[k], b_less * f_im)
+                        three[k] = add(three[k], b_more * f_re)
+    return [(one[k] - two[k], one[k] - three[k]) for k in range(16)]
+
+
+def phases(index):
+    half = (((index + 32) & 63) - 32).astype(F32) * (math.pi / 64)
+    square = half * half
+    sine = jnp.full_like(square, -1 / math.factorial(11))
+    for n in (9, 7, 5, 3, 1):
+        sine = sine * square + (-1) ** (n // 2) / math.factorial(n)
+    sine = sine * half
+    cosine = jnp.full_like(square, 1 / math.factorial(12))
+    for n in (10, 8, 6, 4, 2, 0):
+        cosine = cosine * square + (-1) ** (n // 2) / math.factorial(n)
+    return (1.0 - 2.0 * sine * sine, 2.0 * sine * cosine)
+
+
+def iota(shape, dim):
+    return lax.broadcasted_iota(jnp.int32, shape, dim)
+
+
+def planes(ref):
+    re_high, re_low = split(ref[:, 0].reshape(128, 128))
+    im_high, im_low = split(ref[:, 1].reshape(128, 128))
+    return (jnp.concatenate([re_high, im_high], 1), jnp.concatenate([re_low, im_low], 1))
+
+
+def momentum_lanes(mom_ref):
+    lane = iota((1, 128), 1) & 31
+    rows = []
+    for k in range(3):
+        row = jnp.zeros((1, 128), jnp.int32)
+        for m in range(32):
+            row = jnp.where(lane == m, mom_ref[k, m], row)
+        rows.append(row)
+    return rows
+
+
+def momentum_tables(mom_ref, tm_high_ref, tm_low_ref):
+    _, mom_y, mom_z = momentum_lanes(mom_ref)
+    out_part = ((iota((64, 128), 1) >> 5) & 1) == 1
+    for y in range(2):
+        cosine, sine = phases(mom_z * iota((64, 128), 0) + mom_y * y)
+        less = jnp.where(out_part, cosine, sine)
+        none = jnp.where(out_part, -sine, cosine)
+        more = jnp.where(out_part, -cosine, -sine)
+        for part_in, blocks in ((0, (none, more)), (1, (less, none))):
+            for turned in range(2):
+                high, low = split(blocks[turned])
+                rows = pl.ds(128 * part_in + 64 * y, 64)
+                lanes = pl.ds(128 * turned, 128)
+                tm_high_ref[rows, lanes] = high
+                tm_low_ref[rows, lanes] = low
+
+
+def pair_kernel(start, apart, source_ref, mom_ref, f_ref, b_ref, wave_ref, *refs):
+    sends = refs[:4] if apart else [refs[0].at[k] for k in range(4)]
+    field_ref, w_high_ref, w_low_ref, tm_high_ref, tm_low_ref, total_ref = refs[4 if apart else 1 :]
+    step = pl.program_id(0)
+
+    @pl.when(step == 0)
+    def _():
+        blocks = [lax.axis_index("sy") ^ s if apart else s for s in range(4)]
+        high, low = split(jnp.concatenate([wave_ref[block] for block in blocks], 0))
+        w_high_ref[...] = high
+        w_low_ref[...] = low
+        momentum_tables(mom_ref, tm_high_ref, tm_low_ref)
+        total_ref[...] = jnp.zeros_like(total_ref)
+
+    for k, (real, imag) in enumerate(contract_block(f_ref, b_ref)):
+        field_ref[k, 0] = real
+        field_ref[k, 1] = imag
+    high, low = planes(field_ref)
+    out = nt_dot(w_high_ref[...], high) + nt_dot(w_low_ref[...], high) + nt_dot(w_high_ref[...], low)
+    out = out.reshape(4, 8, 8, 128)
+    for s in range(4):
+        sends[s][pl.ds(8 * step, 8)] = out[s]
+    proj = (
+        nn_dot(high, tm_high_ref[...])
+        + nn_dot(high, tm_low_ref[...])
+        + nn_dot(low, tm_high_ref[...])
+    )
+    value, turned = (proj[:, :128], proj[:, 128:])
+    mom_x, mom_y, mom_z = momentum_lanes(mom_ref)
+    cosine, sine = phases(2 * mom_y * (start + step))
+    total_ref[0] += cosine * value + sine * turned
+    total_ref[1] += cosine * turned - sine * value
+
+    @pl.when(step == pl.num_programs(0) - 1)
+    def _():
+        x = lax.axis_index("sx") * 8 - source_ref[0] + iota((8, 128), 0)
+        rest = (lax.axis_index("sy") * 16 - source_ref[1]) * mom_y - source_ref[2] * mom_z
+        cosine, sine = phases(x * mom_x + rest)
+        value = total_ref[0].reshape(16, 8, 128)
+        turned = total_ref[1].reshape(16, 8, 128)
+        summed = jnp.sum(value * cosine[None] + turned * sine[None], 1)
+        tile = jnp.where(iota((8, 128), 1) >= 64, summed[8:], summed[:8])
+        for s in range(4):
+            sends[s][sends[s].shape[0] - 1] = tile
+
+
+def pair_call(which, start, rows, apart, forward, backward, wave, source_site, momenta):
+    def block(step):
+        return (which, 0, 0, 0, 0, start + step)
+
+    shape = (8 * rows + 1, 8, 128)
+    shapes = [shape] * 4 if apart else [(4, *shape)]
+    out = pl.pallas_call(
+        functools.partial(pair_kernel, start, apart),
+        grid=(rows,),
+        in_specs=[pl.BlockSpec(memory_space=pltpu.SMEM)] * 2
+        + [pl.BlockSpec((1, 2, 12, 12, 8, 128), block)] * 2
+        + [whole((4, 64, 256))],
+        out_specs=[whole(shape) for shape in shapes],
+        out_shape=[jax.ShapeDtypeStruct(shape, F32) for shape in shapes],
+        scratch_shapes=[pltpu.VMEM((16, 2, 8, 128), F32)]
+        + [pltpu.VMEM((256, 256), BF16)] * 4
+        + [pltpu.VMEM((2, 128, 128), F32)],
+        compiler_params=pltpu.CompilerParams(vmem_limit_bytes=62 * MIB),
+        cost_estimate=cost(0),
+        name="contract_and_z",
+    )(source_site, momenta, forward, backward, wave)
+    return out if apart else out[0]
+
+
+def y_kernel(kinds, halves, apart_out, *refs):
+    pos = lax.axis_index("sy")
+    parts = []
+    for apart in kinds:
+        if apart:
+            parts.append(refs[:4])
+        else:
+            parts.append([refs[0].at[pos ^ s] for s in range(4)])
+        refs = refs[4 if apart else 1 :]
+    wave_ref, *sends, work_ref = refs
+    if not apart_out:
+        sends = [sends[0].at[k] for k in range(8)]
+    w_high, w_low = split(wave_ref[0])
+    for q in range(4 * halves):
+        data = []
+        for s in range(4):
+            for part in parts:
+                data += [part[s][8 * y + q] for y in range(part[s].shape[0] // 8)]
+        high, low = split(jnp.concatenate(data, 0))
+        out = nn_dot(w_high, high) + nn_dot(w_low, high) + nn_dot(w_high, low)
+        work_ref[q] = out.reshape(8, 2, 2, 8, 128)
+    extra = sum(ref[ref.shape[0] - 1] for part in parts for ref in part)
+    for h in range(halves):
+        for step in range(8):
+            block = lax.axis_index("sx") ^ step if apart_out else step
+            tiles = [
+                work_ref[4 * h + q, block, p, ri]
+                for ri in range(2)
+                for q in range(4)
+                for p in range(2)
+            ]
+            turned = jnp.concatenate(tiles, 0).T.reshape(16, 8, 128)
+            sends[step][pl.ds(16 * h, 16)] = turned
+    for step in range(8):
+        sends[step][sends[step].shape[0] - 1] = extra
+
+
+def y_call(messages, wave, apart_out, micros):
+    kinds = [isinstance(message, list) for message in messages]
+    operands = [x for message in messages for x in (message if isinstance(message, list) else [message])]
+    shapes = [(33, 8, 128)] * 8 if apart_out else [(8, 33, 8, 128)]
+    return pl.pallas_call(
+        functools.partial(y_kernel, kinds, 2, apart_out),
+        grid=(1,),
+        in_specs=[whole(x.shape) for x in operands]
+        + [pl.BlockSpec((1, 256, 256), lambda step: (lax.axis_index("sy"), 0, 0))],
+        out_specs=[whole(shape) for shape in shapes],
+        out_shape=[jax.ShapeDtypeStruct(shape, F32) for shape in shapes],
+        scratch_shapes=[pltpu.VMEM((8, 8, 2, 2, 8, 128), F32)],
+        compiler_params=pltpu.CompilerParams(vmem_limit_bytes=32 * MIB),
+        cost_estimate=cost(micros),
+        name="along_y",
+    )(*operands, wave)
+
+
+def x_kernel(count, first_half, last, table_ref, source_ref, rows_ref, wave_ref, *refs):
+    data_refs, work_ref = (refs[:count], refs[-1])
+    listed_ref = refs[-2] if first_half == 0 else None
+    out_ref = refs[-3] if first_half == 0 else refs[-2]
+    if count == 1:
+        data_refs = [data_refs[0].at[k] for k in range(8)]
+    step = pl.program_id(0)
+    half = first_half + step
+    first_x, first_y = (lax.axis_index("sx") * 8, lax.axis_index("sy") * 16)
+    blocks = [k if count == 1 else lax.axis_index("sx") ^ k for k in range(8)]
+    w_high, w_low = split(jnp.concatenate([wave_ref[block] for block in blocks], 0))
+    weights = jnp.concatenate([w_high, w_high, w_low], 0)
+    lower = iota((8, 128), 1) < 64
+    for f in range(16):
+        high, low = split(jnp.concatenate([ref[16 * step + f] for ref in data_refs], 0))
+        out = tn_dot(jnp.concatenate([high, low, high], 0), weights)
+        cosine = out[:, :128].reshape(2, 4, 2, 8, 128)
+        sine = out[:, 128:].reshape(2, 4, 2, 8, 128)
+        real = cosine[0] + sine[1]
+        imag = cosine[1] - sine[0]
+        for q in range(4):
+            lanes = pl.ds(128 * q, 128)
+            work_ref[f, 0, :, lanes] = jnp.where(lower, real[q, 0], real[q, 1])
+            work_ref[f, 1, :, lanes] = jnp.where(lower, imag[q, 0], imag[q, 1])
+    column = iota((8, 512), 1)
+    index = (first_x + iota((8, 512), 0)) * source_ref[1] + (column & 63) * source_ref[0]
+    cosine, sine = phases(index + (first_y + 8 * half + (column >> 6)) * source_ref[2])
+    for g in range(16):
+        real = jnp.zeros((8, 512), F32)
+        imag = jnp.zeros((8, 512), F32)
+        for s in range(4):
+            field = 4 * s + table_ref[8 * g + 2 * s]
+            power = table_ref[8 * g + 2 * s + 1]
+            odd = power & 1
+            sign_re = jnp.where((power == 0) | (power == 3), 1.0, -1.0).astype(F32)
+            sign_im = jnp.where(power < 2, 1.0, -1.0).astype(F32)
+            real += sign_re * work_ref[field, odd]
+            imag += sign_im * work_ref[field, 1 - odd]
+        out_ref[g, 0, 0] = real * cosine - imag * sine
+        out_ref[g, 0, 1] = real * sine + imag * cosine
+
+    def listed_sums():
+        total = sum(ref[ref.shape[0] - 1] for ref in data_refs)
+        rows = jnp.concatenate([total[:, 32 * k : 32 * k + 32] for k in range(4)], 0)
+        high, rest = split(rows)
+        middle, low = split(rows - high.astype(F32))
+        mix = mix_matrix(rows_ref[...]).astype(BF16)
+        sums = nn_dot(mix, high) + nn_dot(mix, middle) + nn_dot(mix, low)
+        if last:
+            for ri in range(2):
+                for g in range(16):
+                    row = slice(16 * ri + g, 16 * ri + g + 1)
+                    listed_ref[ri, g, 0:1] = refs[count][row, :]
+                    listed_ref[ri, g, 1:2] = sums[row]
+        else:
+            listed_ref[...] = sums
+
+    if first_half == 0:
+        pl.when(step == 0)(listed_sums)
+
+
+def x_call(which, half, halves, data, gammas, rows, source_site, wave, corr, listed):
+    in_specs = [
+        pl.BlockSpec(memory_space=pltpu.SMEM),
+        pl.BlockSpec(memory_space=pltpu.SMEM),
+        whole((16, 8)),
+        whole((8, 8, 256)),
+    ] + [whole(x.shape) for x in data]
+    operands = [gammas, source_site, rows, wave, *data]
+    aliases = {}
+    if listed is not None:
+        in_specs.append(whole((32, 32)))
+        operands.append(listed)
+    if corr is not None:
+        aliases = {len(operands): 0}
+        in_specs.append(pl.BlockSpec(memory_space=pl.ANY))
+        operands.append(corr)
+    shapes = [(16, 2, 2, 8, 1024)]
+    out_specs = [pl.BlockSpec((16, 1, 2, 8, 512), lambda step: (0, which, 0, 0, half + step))]
+    if half == 0:
+        shapes.append((32, 32) if listed is None else (2, 16, 2, 32))
+        out_specs.append(whole(shapes[1]))
+    return pl.pallas_call(
+        functools.partial(x_kernel, len(data), half, listed is not None),
+        grid=(halves,),
+        in_specs=in_specs,
+        out_specs=out_specs,
+        out_shape=[jax.ShapeDtypeStruct(shape, F32) for shape in shapes],
+        scratch_shapes=[pltpu.VMEM((16, 2, 8, 512), F32)],
+        input_output_aliases=aliases,
+        compiler_params=pltpu.CompilerParams(vmem_limit_bytes=32 * MIB),
+        cost_estimate=cost(0),
+        name="along_x",
+    )(*operands)
+
+
+def mix_matrix(gammas):
+    column = iota((16, 32), 1)
+    field = (column >> 4) * 8 + (column & 7)
+    on_imag = ((column >> 3) & 1) == 1
+    real = jnp.zeros((16, 32), F32)
+    imag = jnp.zeros((16, 32), F32)
+    for s in range(4):
+        match = field == 4 * s + gammas[:, 2 * s : 2 * s + 1]
+        power = gammas[:, 2 * s + 1 : 2 * s + 2]
+        unit_re = (power == 0).astype(F32) - (power == 2).astype(F32)
+        unit_im = (power == 1).astype(F32) - (power == 3).astype(F32)
+        real += jnp.where(match, jnp.where(on_imag, -unit_im, unit_re), 0.0)
+        imag += jnp.where(match, jnp.where(on_imag, unit_re, unit_im), 0.0)
+    return jnp.concatenate([real, imag], 0)
+
+
+def swap_sy(message):
+    out = [message[0]]
+    for step in range(1, 4):
+        out.append(lax.ppermute(message[step], "sy", [(k, k ^ step) for k in range(4)]))
+    return out
+
+
+def swap_sx_whole(message):
+    return [lax.all_to_all(message[0], "sx", 0, 0, tiled=True)]
+
+
+def swap_sx(message):
+    out = [message[0]]
+    for step in range(1, 8):
+        out.append(lax.ppermute(message[step], "sx", [(k, k ^ step) for k in range(8)]))
+    return out
+
+
+def after(values, *others):
+    return lax.optimization_barrier((values, others))[0]
+
+
+def block_body(forward_prop, backward_prop, gamma_table, source_site, momenta):
+    wave_z, wave_y, wave_x = (table_z(), table_y(), table_x())
+    inputs = (forward_prop, backward_prop, wave_z, source_site, momenta.T)
+    outer = (gamma_table.reshape(-1), gamma_table.reshape(16, 8), source_site, wave_x)
+    first = pair_call(0, 0, 8, True, *inputs)
+    inputs = after(inputs, first[0])
+    first = swap_sy(first)
+    third = pair_call(1, 0, 8, True, *inputs)
+    first, third = after((first, third))
+    third = swap_sy(third)
+    sent = y_call([first], wave_y, False, 0)
+    data = swap_sx_whole(sent)
+    third = after(third, sent[0])
+    sent = y_call([third], wave_y, True, 1)
+    data = after(data, sent[0])
+    corr, even = x_call(0, 0, 2, data, *outer, None, None)
+    third = swap_sx(sent)
+    corr, listed = x_call(1, 0, 2, third, *outer, corr, even)
+    return (corr, listed)
+
+
+def body(forward_prop, backward_prop, gamma_table, source_site, momenta):
+    sizes = (forward_prop.shape, lax.axis_size("sx"), lax.axis_size("sy"))
+    fits = sizes == ((2, 2, 12, 12, 8, 16 * LZ), 8, 4) and L == 64 and LZ == 64
+    fits = fits and gamma_table.shape[0] == 16 and momenta.shape[0] == 32
+    run = block_body if fits else general_body
+    return run(forward_prop, backward_prop, gamma_table, source_site, momenta)
+
+
 def solution(mesh):
     placed = (
         P(None, None, None, None, "sx", "sy"),

time: 1140 us -> 86.1 us (0.08); the launches traced: 1120 us -> 85 us
  local copies, waits for them, and re-layouts: 425 us -> 0.34 us
  matrix products: 318 us -> 0 us
  waiting for transfers between devices: 284 us -> 30.6 us
  blocking collectives: 41.3 us -> 0 us
  Pallas kernels: 0 us -> 34.7 us
  other arithmetic: 29.7 us -> 0 us
  starting transfers between devices: 4.53 us -> 18.6 us
  between operations: 14.7 us -> 0.72 us
    dot_general x24 -> x0, matrix products: 318 us -> none  [the longest x1 77.8 us: body(): jnp.einsum(pattern, backward[:, 0], forward[:, 1], preferred_element_type...]
    all_gather x1 -> x0, waiting for transfers between devices: 284 us -> none  [transform(): lax.all_gather(along_z, 'sy', axis=3, tiled=True)]
    unnamed x35 -> x13, local copies, waits for them, and re-layouts: 258 us -> 0.13 us
    psum x1 -> x0, blocking collectives: 41.3 us -> none  [body(): listed_re, listed_im = lax.psum((local_re, local_im), ('sx', 'sy'))]
    pallas_call x0 -> x6, Pallas kernels: none -> 34.7 us  [the longest x2 23.1 us: pair_call(): pl.pallas_call(functools.partial(pair_kernel, start, apart), grid=(rows,)...]
    reshape x2, local copies, waits for them, and re-layouts: 31.4 us -> 0.22 us  [the longest x1 0.14 us: block_body(): gamma_table.reshape(-1)]
    ppermute x0 -> x13, waiting for transfers between devices: none -> 30.6 us  [the longest x6 26.4 us: swap_sy(): lax.ppermute(message[step], 'sy', [(k, k ^ step) for k in range(4)])]
    sub x2 -> x0, local copies, waits for them, and re-layouts: 29.1 us -> none  [the longest x1 26.6 us: body(): jnp.einsum(pattern, backward[:, 0], forward[:, 1], preferred_element_type...]
  transfers between devices with their start and end apart: 2 -> 14, of which waited for: 1 -> 6; matrix products, arithmetic and copies ran while one was open for 2% -> 0% of each run, Pallas kernels for 0% -> 23%
where the time goes in v2:
time: 86.1 us; the launch traced here: 85 us
  Pallas kernels  34.7 us (40%)
  waiting for transfers between devices  30.6 us (36%)
  starting transfers between devices  18.6 us (22%)
    ppermute x6, waiting for transfers between devices, swap_sy(): lax.ppermute(message[step], 'sy', [(k, k ^ step) for k in range(4)])  26.4 us
    pallas_call x2, Pallas kernels, pair_call(): pl.pallas_call(functools.partial(pair_kernel, start, apart), grid=(rows,)...  23.1 us
    ppermute x7, starting transfers between devices, swap_sx(): lax.ppermute(message[step], 'sx', [(k, k ^ step) for k in range(8)])  7.4 us
    pallas_call x2, Pallas kernels, x_call(): pl.pallas_call(functools.partial(x_kernel, len(data), half, listed is not...  7.26 us
    ppermute x6, starting transfers between devices, swap_sy(): lax.ppermute(message[step], 'sy', [(k, k ^ step) for k in range(4)])  6.98 us
    pallas_call x2, Pallas kernels, y_call(): pl.pallas_call(functools.partial(y_kernel, kinds, 2, apart_out), grid=(1,...  4.41 us
    all_to_all x1, starting transfers between devices, swap_sx_whole(): return [lax.all_to_all(message[0], 'sx', 0, 0, tiled=True)]  4.24 us
    ppermute x7, waiting for transfers between devices, swap_sx(): lax.ppermute(message[step], 'sx', [(k, k ^ step) for k in range(8)])  4.17 us
  transfers between devices with their start and end apart: 14, of which 6 were waited for; matrix products, arithmetic and copies ran while one was open for 0% of the time, Pallas kernels for 23%

profile of v2, /device:TPU:16, one launch (start us, length us, event | category | flops | bytes accessed | tf_op | source)
XLA Modules:
  0.0 85.0 jit_solution(770742956862797300)
XLA Ops:
  0.6 11.5 %contract_and_z.2 = (f32[65,8,128]{2,1,0:T(8,128)}, f32[65,8,128]{2,1,0:T(8,128)}, f32[65,8,128]{2,1,0:T(8,128)}, f32[65,8,128]{2,1,0:T(8,128)}) custom-call(s32[3]{0:T(128)} %source_ref.6, s32[3,32]{1,0:T(4,128)} %bitcast.3, bf16[2,2,12,12,8,1024]{5,4,3,2,1,0:T(8,128)(2,1)} %f_ref.2, bf16[2,2,12,12,8,1024]{5,4,3,2,1,0:T(8,128)(2,1)} %b_ref.2, ...), custom_call_target="tpu_custom_call" | custom-call | tf_op jit(solution)/shard_map/contract_and_z/pallas_call | solution.py:338
  12.1 1.6 %collective-permute-start = (f32[65,8,128]{2,1,0:T(8,128)}, f32[65,8,128]{2,1,0:T(8,128)S(1)}, u32[]{:S(2)}, u32[]{:S(2)}) collective-permute-start(f32[65,8,128]{2,1,0:T(8,128)} %get-tuple-element.39), channel_id=1, source_target_pairs={{0,1},{1,0},{2,3},{3,2},{4,5},{5,4},{6,7},{7,6},{8,9},{9,8},{10,11... | collective-permute-start | bytes 798728 | tf_op jit(solution)/shard_map/ppermute | solution.py:526
  13.7 0.3 collective-permute-start.1
  14.0 1.6 %collective-permute-start.2 = (f32[65,8,128]{2,1,0:T(8,128)}, f32[65,8,128]{2,1,0:T(8,128)}, u32[]{:S(2)}, u32[]{:S(2)}) collective-permute-start(f32[65,8,128]{2,1,0:T(8,128)} %get-tuple-element.41), channel_id=1, source_target_pairs={{0,3},{1,2},{2,1},{3,0},{4,7},{5,6},{6,5},{7,4},{8,11},{9,10},{10,... | collective-permute-start | bytes 798728 | tf_op jit(solution)/shard_map/ppermute | solution.py:526
  15.6 0.0 copy-start
  15.6 0.0 copy-start.1
  15.6 11.6 %contract_and_z.3 = (f32[65,8,128]{2,1,0:T(8,128)}, f32[65,8,128]{2,1,0:T(8,128)}, f32[65,8,128]{2,1,0:T(8,128)}, f32[65,8,128]{2,1,0:T(8,128)}) custom-call(s32[3]{0:T(128)} %source_ref.6, s32[3,32]{1,0:T(4,128)} %bitcast.4, bf16[2,2,12,12,8,1024]{5,4,3,2,1,0:T(8,128)(2,1)} %f_ref.2, bf16[2,2,12,12,8,1024]{5,4,3,2,1,0:T(8,128)(2,1)} %b_ref.2, ...), custom_call_target="tpu_custom_call" | custom-call | tf_op jit(solution)/shard_map/contract_and_z/pallas_call | solution.py:338
  27.2 0.0 collective-permute-done.refs_1_
  27.2 5.4 %collective-permute-done.1.refs_2_ = f32[65,8,128]{2,1,0:T(8,128)S(1)} collective-permute-done((f32[65,8,128]{2,1,0:T(8,128)}, f32[65,8,128]{2,1,0:T(8,128)S(1)}, u32[]{:S(2)}, u32[]{:S(2)}) %collective-permute-start.1) | collective-permute-done | bytes 266272 | tf_op jit(solution)/shard_map/ppermute | solution.py:526
  32.6 6.3 %collective-permute-done.2.refs_3_ = f32[65,8,128]{2,1,0:T(8,128)} collective-permute-done((f32[65,8,128]{2,1,0:T(8,128)}, f32[65,8,128]{2,1,0:T(8,128)}, u32[]{:S(2)}, u32[]{:S(2)}) %collective-permute-start.2) | collective-permute-done | bytes 266272 | tf_op jit(solution)/shard_map/ppermute | solution.py:526
  38.9 0.0 copy-start.4
  38.9 0.0 collective-permute-start.3
  38.9 1.9 %collective-permute-start.4 = (f32[65,8,128]{2,1,0:T(8,128)}, f32[65,8,128]{2,1,0:T(8,128)S(1)}, u32[]{:S(2)}, u32[]{:S(2)}) collective-permute-start(f32[65,8,128]{2,1,0:T(8,128)} %get-tuple-element.53), channel_id=1, source_target_pairs={{0,2},{1,3},{2,0},{3,1},{4,6},{5,7},{6,4},{7,5},{8,10},{9,11},{10,... | collective-permute-start | bytes 798728 | tf_op jit(solution)/shard_map/ppermute | solution.py:526
  40.8 1.6 %collective-permute-start.5 = (f32[65,8,128]{2,1,0:T(8,128)}, f32[65,8,128]{2,1,0:T(8,128)S(1)}, u32[]{:S(2)}, u32[]{:S(2)}) collective-permute-start(f32[65,8,128]{2,1,0:T(8,128)} %get-tuple-element.54), channel_id=1, source_target_pairs={{0,3},{1,2},{2,1},{3,0},{4,7},{5,6},{6,5},{7,4},{8,11},{9,10},{10,... | collective-permute-start | bytes 798728 | tf_op jit(solution)/shard_map/ppermute | solution.py:526
  42.4 0.0 copy-done
  42.4 0.0 copy-done.1
  42.4 3.1 %along_y.2 = f32[8,33,8,128]{3,2,1,0:T(8,128)} custom-call(f32[65,8,128]{2,1,0:T(8,128)S(1)} %copy-done.1, f32[65,8,128]{2,1,0:T(8,128)S(1)} %collective-permute-done.refs_1_, f32[65,8,128]{2,1,0:T(8,128)S(1)} %collective-permute-done.1.refs_2_, f32[65,8,128]{2,1,0:T(8,128)} %collective-permute-done.2.refs_3_, f32[4,256,256]{2,1,0:T(8,128)S(1)} %copy-done), custom_call_target="tpu_custom_call" | custom-call | tf_op jit(solution)/shard_map/along_y/pallas_call | solution.py:397
  45.4 4.2 %all-to-all-start = ((f32[8,33,8,128]{3,2,1,0:T(8,128)}), f32[8,33,8,128]{3,2,1,0:T(8,128)}, u32[]{:S(2)}, u32[]{:S(2)}) async-start(f32[8,33,8,128]{3,2,1,0:T(8,128)} %along_y.2), calls=%async_computation | async-start | bytes 2162688 | tf_op jit(solution)/shard_map/all_to_all | solution.py:531
  49.7 0.0 collective-permute-done.3.refs_1_
  49.7 9.7 %collective-permute-done.4.refs_2_ = f32[65,8,128]{2,1,0:T(8,128)S(1)} collective-permute-done((f32[65,8,128]{2,1,0:T(8,128)}, f32[65,8,128]{2,1,0:T(8,128)S(1)}, u32[]{:S(2)}, u32[]{:S(2)}) %collective-permute-start.4) | collective-permute-done | bytes 266272 | tf_op jit(solution)/shard_map/ppermute | solution.py:526
  59.4 5.0 %collective-permute-done.5.refs_3_ = f32[65,8,128]{2,1,0:T(8,128)S(1)} collective-permute-done((f32[65,8,128]{2,1,0:T(8,128)}, f32[65,8,128]{2,1,0:T(8,128)S(1)}, u32[]{:S(2)}, u32[]{:S(2)}) %collective-permute-start.5) | collective-permute-done | bytes 266272 | tf_op jit(solution)/shard_map/ppermute | solution.py:526
  64.4 0.0 copy-done.4
  64.4 0.0 copy-start.5
  64.4 0.0 copy-start.2
  64.4 1.3 %along_y.3 = (f32[33,8,128]{2,1,0:T(8,128)S(1)}, f32[33,8,128]{2,1,0:T(8,128)S(1)}, f32[33,8,128]{2,1,0:T(8,128)S(1)}, f32[33,8,128]{2,1,0:T(8,128)S(1)}, f32[33...) custom-call(f32[65,8,128]{2,1,0:T(8,128)S(1)} %copy-done.4, ...), custom_call_target="tpu_custom_call" | custom-call | flops 9999999827968 | tf_op jit(solution)/shard_map/along_y/pallas_call | solution.py:397
  65.8 0.1 collective-permute-start.6
  65.9 1.6 %collective-permute-start.7 = (f32[33,8,128]{2,1,0:T(8,128)S(1)}, f32[33,8,128]{2,1,0:T(8,128)S(1)}, u32[]{:S(2)}, u32[]{:S(2)}) collective-permute-start(f32[33,8,128]{2,1,0:T(8,128)S(1)} %get-tuple-element.65), channel_id=1, source_target_pairs={{0,8},{4,12},{8,0},{12,4},{16,24},{20,28},{24,16},{28,20},{1,9},{5... | collective-permute-start | bytes 405512 | tf_op jit(solution)/shard_map/ppermute | solution.py:537
  67.4 0.3 collective-permute-start.8
  67.7 1.5 %collective-permute-start.9 = (f32[33,8,128]{2,1,0:T(8,128)S(1)}, f32[33,8,128]{2,1,0:T(8,128)S(1)}, u32[]{:S(2)}, u32[]{:S(2)}) collective-permute-start(f32[33,8,128]{2,1,0:T(8,128)S(1)} %get-tuple-element.67), channel_id=1, source_target_pairs={{0,16},{4,20},{8,24},{12,28},{16,0},{20,4},{24,8},{28,12},{1,17},{... | collective-permute-start | bytes 405512 | tf_op jit(solution)/shard_map/ppermute | solution.py:537
  69.3 0.2 collective-permute-start.10
  69.4 0.0 collective-permute-done.6.refs_1_
  69.4 2.5 %collective-permute-start.11 = (f32[33,8,128]{2,1,0:T(8,128)S(1)}, f32[33,8,128]{2,1,0:T(8,128)S(1)}, u32[]{:S(2)}, u32[]{:S(2)}) collective-permute-start(f32[33,8,128]{2,1,0:T(8,128)S(1)} %get-tuple-element.69), channel_id=1, source_target_pairs={{0,24},{4,28},{8,16},{12,20},{16,8},{20,12},{24,0},{28,4},{1,25},{... | collective-permute-start | bytes 405512 | tf_op jit(solution)/shard_map/ppermute | solution.py:537
  71.9 0.4 collective-permute-done.7.refs_2_
  72.3 1.3 %collective-permute-start.12 = (f32[33,8,128]{2,1,0:T(8,128)S(1)}, f32[33,8,128]{2,1,0:T(8,128)S(1)}, u32[]{:S(2)}, u32[]{:S(2)}) collective-permute-start(f32[33,8,128]{2,1,0:T(8,128)S(1)} %get-tuple-element.70), channel_id=1, source_target_pairs={{0,28},{4,24},{8,20},{12,16},{16,12},{20,8},{24,4},{28,0},{1,29},{... | collective-permute-start | bytes 405512 | tf_op jit(solution)/shard_map/ppermute | solution.py:537
  73.6 0.0 copy-done.5
  73.6 0.1 copy.14
  73.7 0.1 copy.16.rows_ref
  73.8 0.1 reshape.10.table_ref
  73.9 0.0 all-to-all-done.refs_0_
  73.9 0.0 copy-done.2
  74.0 0.0 copy-done.3
  74.0 4.0 %along_x.2 = (f32[16,2,2,8,1024]{4,3,2,1,0:T(8,128)}, f32[32,32]{1,0:T(8,128)S(1)}) custom-call(s32[128]{0:T(128)S(1)} %reshape.10.table_ref, s32[3]{0:T(128)S(1)} %copy-done.3, s32[16,8]{1,0:T(8,128)S(1)} %copy.16.rows_ref, f32[8,8,256]{2,1,0:T(8,128)S(1)} %copy-done.2, f32[8,33,8,128]{3,2,1,0:T(8,128)} %all-to-all-done.refs_0_), custom_call_target="tpu_custom_call" | custom-call | tf_op jit(solution)/shard_map/along_x/pallas_call | solution.py:493
  77.9 0.0 collective-permute-done.8.refs_3_
  77.9 0.0 collective-permute-done.9.refs_4_
  77.9 3.7 %collective-permute-done.10.refs_5_ = f32[33,8,128]{2,1,0:T(8,128)S(1)} collective-permute-done((f32[33,8,128]{2,1,0:T(8,128)S(1)}, f32[33,8,128]{2,1,0:T(8,128)S(1)}, u32[]{:S(2)}, u32[]{:S(2)}) %collective-permute-start.10) | collective-permute-done | bytes 135200 | tf_op jit(solution)/shard_map/ppermute | solution.py:537
  81.7 0.0 collective-permute-done.11.refs_6_
  81.7 0.0 collective-permute-done.12.refs_7_
  81.7 3.3 %along_x.3 = (f32[16,2,2,8,1024]{4,3,2,1,0:T(8,128)}, f32[2,16,2,32]{3,2,1,0:T(2,128)}) custom-call(s32[128]{0:T(128)S(1)} %reshape.10.table_ref, s32[3]{0:T(128)S(1)} %copy-done.3, s32[16,8]{1,0:T(8,128)S(1)} %copy.16.rows_ref, f32[8,8,256]{2,1,0:T(8,128)S(1)} %copy-done.2, ...), custom_call_target="tpu_custom_call", output_to_operand_aliasing={{0}: (13, {})} | custom-call | tf_op jit(solution)/shard_map/along_x/pallas_call | solution.py:493
  (1 shorter events, 0.0 us)
Async XLA Ops:
  12.1 15.1 %collective-permute-start = (f32[65,8,128]{2,1,0:T(8,128)}, f32[65,8,128]{2,1,0:T(8,128)S(1)}, u32[]{:S(2)}, u32[]{:S(2)}) collective-permute-start(f32[65,8,128]{2,1,0:T(8,128)} %get-tuple-element.39), channel_id=1, source_target_pairs={{0,1},{1,0},{2,3},{3,2},{4,5},{5,4},{6,7},{7,6},{8,9},{9,8},{10,11... | collective-permute-start | bytes 798728 | tf_op jit(solution)/shard_map/ppermute | solution.py:526
  13.7 18.9 %collective-permute-start.1 = (f32[65,8,128]{2,1,0:T(8,128)}, f32[65,8,128]{2,1,0:T(8,128)S(1)}, u32[]{:S(2)}, u32[]{:S(2)}) collective-permute-start(f32[65,8,128]{2,1,0:T(8,128)} %get-tuple-element.40), channel_id=1, source_target_pairs={{0,2},{1,3},{2,0},{3,1},{4,6},{5,7},{6,4},{7,5},{8,10},{9,11},{10,... | collective-permute-start | bytes 798728 | tf_op jit(solution)/shard_map/ppermute | solution.py:526
  14.0 24.9 %collective-permute-start.2 = (f32[65,8,128]{2,1,0:T(8,128)}, f32[65,8,128]{2,1,0:T(8,128)}, u32[]{:S(2)}, u32[]{:S(2)}) collective-permute-start(f32[65,8,128]{2,1,0:T(8,128)} %get-tuple-element.41), channel_id=1, source_target_pairs={{0,3},{1,2},{2,1},{3,0},{4,7},{5,6},{6,5},{7,4},{8,11},{9,10},{10,... | collective-permute-start | bytes 798728 | tf_op jit(solution)/shard_map/ppermute | solution.py:526
  15.6 26.8 %copy-start = (f32[4,256,256]{2,1,0:T(8,128)S(1)}, f32[4,256,256]{2,1,0:T(8,128)}, u32[]{:S(2)}) copy-start(f32[4,256,256]{2,1,0:T(8,128)} %constant.7.clone.refs_4_) | copy-start | bytes 3145732
  15.6 26.8 %copy-start.1 = (f32[65,8,128]{2,1,0:T(8,128)S(1)}, f32[65,8,128]{2,1,0:T(8,128)}, u32[]{:S(2)}) copy-start(f32[65,8,128]{2,1,0:T(8,128)} %get-tuple-element.55.refs_0_) | copy-start | bytes 798724
  38.9 25.5 %copy-start.4 = (f32[65,8,128]{2,1,0:T(8,128)S(1)}, f32[65,8,128]{2,1,0:T(8,128)}, u32[]{:S(2)}) copy-start(f32[65,8,128]{2,1,0:T(8,128)} %get-tuple-element.59.refs_0_) | copy-start | bytes 798724
  38.9 10.8 %collective-permute-start.3 = (f32[65,8,128]{2,1,0:T(8,128)}, f32[65,8,128]{2,1,0:T(8,128)S(1)}, u32[]{:S(2)}, u32[]{:S(2)}) collective-permute-start(f32[65,8,128]{2,1,0:T(8,128)} %get-tuple-element.52), channel_id=1, source_target_pairs={{0,1},{1,0},{2,3},{3,2},{4,5},{5,4},{6,7},{7,6},{8,9},{9,8},{10,11... | collective-permute-start | bytes 798728 | tf_op jit(solution)/shard_map/ppermute | solution.py:526
  38.9 20.5 %collective-permute-start.4 = (f32[65,8,128]{2,1,0:T(8,128)}, f32[65,8,128]{2,1,0:T(8,128)S(1)}, u32[]{:S(2)}, u32[]{:S(2)}) collective-permute-start(f32[65,8,128]{2,1,0:T(8,128)} %get-tuple-element.53), channel_id=1, source_target_pairs={{0,2},{1,3},{2,0},{3,1},{4,6},{5,7},{6,4},{7,5},{8,10},{9,11},{10,... | collective-permute-start | bytes 798728 | tf_op jit(solution)/shard_map/ppermute | solution.py:526
  40.8 23.6 %collective-permute-start.5 = (f32[65,8,128]{2,1,0:T(8,128)}, f32[65,8,128]{2,1,0:T(8,128)S(1)}, u32[]{:S(2)}, u32[]{:S(2)}) collective-permute-start(f32[65,8,128]{2,1,0:T(8,128)} %get-tuple-element.54), channel_id=1, source_target_pairs={{0,3},{1,2},{2,1},{3,0},{4,7},{5,6},{6,5},{7,4},{8,11},{9,10},{10,... | collective-permute-start | bytes 798728 | tf_op jit(solution)/shard_map/ppermute | solution.py:526
  45.4 28.5 %all-to-all-start = ((f32[8,33,8,128]{3,2,1,0:T(8,128)}), f32[8,33,8,128]{3,2,1,0:T(8,128)}, u32[]{:S(2)}, u32[]{:S(2)}) async-start(f32[8,33,8,128]{3,2,1,0:T(8,128)} %along_y.2), calls=%async_computation | async-start | bytes 2162688 | tf_op jit(solution)/shard_map/all_to_all | solution.py:531
  64.4 9.2 %copy-start.5 = (s32[16,4,2]{0,2,1:T(2,128)S(1)}, s32[16,4,2]{0,2,1:T(2,128)}, u32[]{:S(2)}) copy-start(s32[16,4,2]{0,2,1:T(2,128)} %param.10) | copy-start | bytes 1540
  64.4 9.5 %copy-start.2 = (f32[8,8,256]{2,1,0:T(8,128)S(1)}, f32[8,8,256]{2,1,0:T(8,128)}, u32[]{:S(2)}) copy-start(f32[8,8,256]{2,1,0:T(8,128)} %constant.8.clone.wave_ref) | copy-start | bytes 196612
  64.4 9.5 %copy-start.3 = (s32[3]{0:T(128)S(1)}, s32[3]{0:T(128)}, u32[]{:S(2)}) copy-start(s32[3]{0:T(128)} %source_ref.6) | copy-start | bytes 40
  65.8 3.6 %collective-permute-start.6 = (f32[33,8,128]{2,1,0:T(8,128)S(1)}, f32[33,8,128]{2,1,0:T(8,128)S(1)}, u32[]{:S(2)}, u32[]{:S(2)}) collective-permute-start(f32[33,8,128]{2,1,0:T(8,128)S(1)} %get-tuple-element.64), channel_id=1, source_target_pairs={{0,4},{4,0},{8,12},{12,8},{16,20},{20,16},{24,28},{28,24},{1,5},{5... | collective-permute-start | bytes 405512 | tf_op jit(solution)/shard_map/ppermute | solution.py:537
  65.9 6.5 %collective-permute-start.7 = (f32[33,8,128]{2,1,0:T(8,128)S(1)}, f32[33,8,128]{2,1,0:T(8,128)S(1)}, u32[]{:S(2)}, u32[]{:S(2)}) collective-permute-start(f32[33,8,128]{2,1,0:T(8,128)S(1)} %get-tuple-element.65), channel_id=1, source_target_pairs={{0,8},{4,12},{8,0},{12,4},{16,24},{20,28},{24,16},{28,20},{1,9},{5... | collective-permute-start | bytes 405512 | tf_op jit(solution)/shard_map/ppermute | solution.py:537
  67.4 10.5 %collective-permute-start.8 = (f32[33,8,128]{2,1,0:T(8,128)S(1)}, f32[33,8,128]{2,1,0:T(8,128)S(1)}, u32[]{:S(2)}, u32[]{:S(2)}) collective-permute-start(f32[33,8,128]{2,1,0:T(8,128)S(1)} %get-tuple-element.66), channel_id=1, source_target_pairs={{0,12},{4,8},{8,4},{12,0},{16,28},{20,24},{24,20},{28,16},{1,13},{... | collective-permute-start | bytes 405512 | tf_op jit(solution)/shard_map/ppermute | solution.py:537
  67.7 10.2 %collective-permute-start.9 = (f32[33,8,128]{2,1,0:T(8,128)S(1)}, f32[33,8,128]{2,1,0:T(8,128)S(1)}, u32[]{:S(2)}, u32[]{:S(2)}) collective-permute-start(f32[33,8,128]{2,1,0:T(8,128)S(1)} %get-tuple-element.67), channel_id=1, source_target_pairs={{0,16},{4,20},{8,24},{12,28},{16,0},{20,4},{24,8},{28,12},{1,17},{... | collective-permute-start | bytes 405512 | tf_op jit(solution)/shard_map/ppermute | solution.py:537
  69.3 12.4 %collective-permute-start.10 = (f32[33,8,128]{2,1,0:T(8,128)S(1)}, f32[33,8,128]{2,1,0:T(8,128)S(1)}, u32[]{:S(2)}, u32[]{:S(2)}) collective-permute-start(f32[33,8,128]{2,1,0:T(8,128)S(1)} %get-tuple-element.68), channel_id=1, source_target_pairs={{0,20},{4,16},{8,28},{12,24},{16,4},{20,0},{24,12},{28,8},{1,21},{... | collective-permute-start | bytes 405512 | tf_op jit(solution)/shard_map/ppermute | solution.py:537
  69.4 12.3 %collective-permute-start.11 = (f32[33,8,128]{2,1,0:T(8,128)S(1)}, f32[33,8,128]{2,1,0:T(8,128)S(1)}, u32[]{:S(2)}, u32[]{:S(2)}) collective-permute-start(f32[33,8,128]{2,1,0:T(8,128)S(1)} %get-tuple-element.69), channel_id=1, source_target_pairs={{0,24},{4,28},{8,16},{12,20},{16,8},{20,12},{24,0},{28,4},{1,25},{... | collective-permute-start | bytes 405512 | tf_op jit(solution)/shard_map/ppermute | solution.py:537
  72.3 9.4 %collective-permute-start.12 = (f32[33,8,128]{2,1,0:T(8,128)S(1)}, f32[33,8,128]{2,1,0:T(8,128)S(1)}, u32[]{:S(2)}, u32[]{:S(2)}) collective-permute-start(f32[33,8,128]{2,1,0:T(8,128)S(1)} %get-tuple-element.70), channel_id=1, source_target_pairs={{0,28},{4,24},{8,20},{12,16},{16,12},{20,8},{24,4},{28,0},{1,29},{... | collective-permute-start | bytes 405512 | tf_op jit(solution)/shard_map/ppermute | solution.py:537

commit v3 on v2

--- a/solution.py
+++ b/solution.py
@@ -283,101 +283,130 @@
                 tm_low_ref[rows, lanes] = low
 
 
-def pair_kernel(start, apart, source_ref, mom_ref, f_ref, b_ref, wave_ref, *refs):
-    sends = refs[:4] if apart else [refs[0].at[k] for k in range(4)]
-    field_ref, w_high_ref, w_low_ref, tm_high_ref, tm_low_ref, total_ref = refs[4 if apart else 1 :]
+def pair_kernel(listed, aliased, source_ref, mom_ref, f_ref, b_ref, wave_ref, *refs):
+    if aliased:
+        refs = refs[1:]
+    if listed:
+        old_ref, *sends, field_ref, w_high_ref, w_low_ref = refs[:8]
+        tm_high_ref, tm_low_ref, total_ref = refs[8:]
+    else:
+        *sends, fields_ref, field_ref, w_high_ref, w_low_ref = refs
     step = pl.program_id(0)
+    rows = pl.num_programs(0) - 1
+    row = jnp.maximum(step - 1, 0)
 
     @pl.when(step == 0)
     def _():
-        blocks = [lax.axis_index("sy") ^ s if apart else s for s in range(4)]
+        blocks = [lax.axis_index("sy") ^ s for s in range(4)]
         high, low = split(jnp.concatenate([wave_ref[block] for block in blocks], 0))
         w_high_ref[...] = high
         w_low_ref[...] = low
-        momentum_tables(mom_ref, tm_high_ref, tm_low_ref)
-        total_ref[...] = jnp.zeros_like(total_ref)
-
-    for k, (real, imag) in enumerate(contract_block(f_ref, b_ref)):
-        field_ref[k, 0] = real
-        field_ref[k, 1] = imag
-    high, low = planes(field_ref)
-    out = nt_dot(w_high_ref[...], high) + nt_dot(w_low_ref[...], high) + nt_dot(w_high_ref[...], low)
-    out = out.reshape(4, 8, 8, 128)
-    for s in range(4):
-        sends[s][pl.ds(8 * step, 8)] = out[s]
-    proj = (
-        nn_dot(high, tm_high_ref[...])
-        + nn_dot(high, tm_low_ref[...])
-        + nn_dot(low, tm_high_ref[...])
-    )
-    value, turned = (proj[:, :128], proj[:, 128:])
-    mom_x, mom_y, mom_z = momentum_lanes(mom_ref)
-    cosine, sine = phases(2 * mom_y * (start + step))
-    total_ref[0] += cosine * value + sine * turned
-    total_ref[1] += cosine * turned - sine * value
-
-    @pl.when(step == pl.num_programs(0) - 1)
+        if listed:
+            momentum_tables(mom_ref, tm_high_ref, tm_low_ref)
+            total_ref[...] = jnp.zeros_like(total_ref)
+
+    def project(t, high, low):
+        proj = (
+            nn_dot(high, tm_high_ref[...])
+            + nn_dot(high, tm_low_ref[...])
+            + nn_dot(low, tm_high_ref[...])
+        )
+        value, turned = (proj[:, :128], proj[:, 128:])
+        cosine, sine = phases(2 * momentum_lanes(mom_ref)[1] * row)
+        there = step > 0
+        total_ref[t, 0] += jnp.where(there, cosine * value + sine * turned, 0.0)
+        total_ref[t, 1] += jnp.where(there, cosine * turned - sine * value, 0.0)
+
+    def transform():
+        high, low = planes(field_ref)
+        w_high, w_low = (w_high_ref[...], w_low_ref[...])
+        out = nt_dot(w_high, high) + nt_dot(w_low, high) + nt_dot(w_high, low)
+        out = out.reshape(4, 8, 8, 128)
+        for s in range(4):
+            sends[s][pl.ds(8 * row, 8)] = out[s]
+        if listed:
+            project(1, high, low)
+            project(0, *planes(old_ref))
+
+    @pl.when(step < rows)
     def _():
-        x = lax.axis_index("sx") * 8 - source_ref[0] + iota((8, 128), 0)
-        rest = (lax.axis_index("sy") * 16 - source_ref[1]) * mom_y - source_ref[2] * mom_z
-        cosine, sine = phases(x * mom_x + rest)
-        value = total_ref[0].reshape(16, 8, 128)
-        turned = total_ref[1].reshape(16, 8, 128)
-        summed = jnp.sum(value * cosine[None] + turned * sine[None], 1)
-        tile = jnp.where(iota((8, 128), 1) >= 64, summed[8:], summed[:8])
-        for s in range(4):
-            sends[s][sends[s].shape[0] - 1] = tile
-
-
-def pair_call(which, start, rows, apart, forward, backward, wave, source_site, momenta):
+        transform()
+        for k, (real, imag) in enumerate(contract_block(f_ref, b_ref)):
+            field_ref[k, 0] = real
+            field_ref[k, 1] = imag
+            if not listed:
+                fields_ref[k, 0] = real
+                fields_ref[k, 1] = imag
+
+    @pl.when(step == rows)
+    def _():
+        transform()
+        if listed:
+            mom_x, mom_y, mom_z = momentum_lanes(mom_ref)
+            x = lax.axis_index("sx") * 8 - source_ref[0] + iota((8, 128), 0)
+            rest = (lax.axis_index("sy") * 16 - source_ref[1]) * mom_y - source_ref[2] * mom_z
+            cosine, sine = phases(x * mom_x + rest)
+            for t in range(2):
+                value = total_ref[t, 0].reshape(16, 8, 128)
+                turned = total_ref[t, 1].reshape(16, 8, 128)
+                summed = jnp.sum(value * cosine[None] + turned * sine[None], 1)
+                tile = jnp.where(iota((8, 128), 1) >= 64, summed[8:], summed[:8])
+                for s in range(4):
+                    sends[s][64 + t] = tile
+
+
+def pair_call(which, start, rows, listed, fields, forward, backward, wave, source_site, momenta):
     def block(step):
-        return (which, 0, 0, 0, 0, start + step)
-
-    shape = (8 * rows + 1, 8, 128)
-    shapes = [shape] * 4 if apart else [(4, *shape)]
-    out = pl.pallas_call(
-        functools.partial(pair_kernel, start, apart),
-        grid=(rows,),
-        in_specs=[pl.BlockSpec(memory_space=pltpu.SMEM)] * 2
-        + [pl.BlockSpec((1, 2, 12, 12, 8, 128), block)] * 2
-        + [whole((4, 64, 256))],
-        out_specs=[whole(shape) for shape in shapes],
+        return (which, 0, 0, 0, 0, start + jnp.minimum(step, rows - 1))
+
+    in_specs = [pl.BlockSpec(memory_space=pltpu.SMEM)] * 2
+    in_specs += [pl.BlockSpec((1, 2, 12, 12, 8, 128), block)] * 2 + [whole((4, 64, 256))]
+    operands = [source_site, momenta, forward, backward, wave]
+    shapes = [(8 * rows + 2 if listed else 8 * rows, 8, 128)] * 4
+    out_specs = [whole(shape) for shape in shapes]
+    scratch = [pltpu.VMEM((16, 2, 8, 128), F32)] + [pltpu.VMEM((256, 256), BF16)] * 2
+    aliases = {}
+    if listed:
+        in_specs.append(
+            pl.BlockSpec((16, 2, 8, 128), lambda step: (0, 0, 0, jnp.maximum(step - 1, 0)))
+        )
+        operands.append(fields)
+        scratch += [pltpu.VMEM((256, 256), BF16)] * 2 + [pltpu.VMEM((2, 2, 128, 128), F32)]
+    else:
+        shapes.append((16, 2, 8, 1024))
+        out_specs.append(pl.BlockSpec((16, 2, 8, 128), lambda step: (0, 0, 0, block(step)[5])))
+        if fields is not None:
+            in_specs.append(pl.BlockSpec(memory_space=pl.ANY))
+            operands.append(fields)
+            aliases = {5: 4}
+    return pl.pallas_call(
+        functools.partial(pair_kernel, listed, bool(aliases)),
+        grid=(rows + 1,),
+        in_specs=in_specs,
+        out_specs=out_specs,
         out_shape=[jax.ShapeDtypeStruct(shape, F32) for shape in shapes],
-        scratch_shapes=[pltpu.VMEM((16, 2, 8, 128), F32)]
-        + [pltpu.VMEM((256, 256), BF16)] * 4
-        + [pltpu.VMEM((2, 128, 128), F32)],
-        compiler_params=pltpu.CompilerParams(vmem_limit_bytes=62 * MIB),
+        scratch_shapes=scratch,
+        input_output_aliases=aliases,
+        compiler_params=pltpu.CompilerParams(vmem_limit_bytes=55 * MIB),
         cost_estimate=cost(0),
         name="contract_and_z",
-    )(source_site, momenta, forward, backward, wave)
-    return out if apart else out[0]
-
-
-def y_kernel(kinds, halves, apart_out, *refs):
-    pos = lax.axis_index("sy")
-    parts = []
-    for apart in kinds:
-        if apart:
-            parts.append(refs[:4])
-        else:
-            parts.append([refs[0].at[pos ^ s] for s in range(4)])
-        refs = refs[4 if apart else 1 :]
-    wave_ref, *sends, work_ref = refs
-    if not apart_out:
+    )(*operands)
+
+
+def y_kernel(parts, listed, apart, *refs):
+    messages = [refs[s + 4 * part] for s in range(4) for part in range(parts)]
+    wave_ref, *sends, work_ref = refs[4 * parts :]
+    if not apart:
         sends = [sends[0].at[k] for k in range(8)]
     w_high, w_low = split(wave_ref[0])
-    for q in range(4 * halves):
-        data = []
-        for s in range(4):
-            for part in parts:
-                data += [part[s][8 * y + q] for y in range(part[s].shape[0] // 8)]
+    for q in range(8):
+        data = [ref[8 * y + q] for ref in messages for y in range(ref.shape[0] // 8)]
         high, low = split(jnp.concatenate(data, 0))
         out = nn_dot(w_high, high) + nn_dot(w_low, high) + nn_dot(w_high, low)
         work_ref[q] = out.reshape(8, 2, 2, 8, 128)
-    extra = sum(ref[ref.shape[0] - 1] for part in parts for ref in part)
-    for h in range(halves):
+    for h in range(2):
         for step in range(8):
-            block = lax.axis_index("sx") ^ step if apart_out else step
+            block = lax.axis_index("sx") ^ step if apart else step
             tiles = [
                 work_ref[4 * h + q, block, p, ri]
                 for ri in range(2)
@@ -386,43 +415,45 @@
             ]
             turned = jnp.concatenate(tiles, 0).T.reshape(16, 8, 128)
             sends[step][pl.ds(16 * h, 16)] = turned
-    for step in range(8):
-        sends[step][sends[step].shape[0] - 1] = extra
-
-
-def y_call(messages, wave, apart_out, micros):
-    kinds = [isinstance(message, list) for message in messages]
-    operands = [x for message in messages for x in (message if isinstance(message, list) else [message])]
-    shapes = [(33, 8, 128)] * 8 if apart_out else [(8, 33, 8, 128)]
+    if listed:
+        for t in range(2):
+            share = sum(ref[64 + t] for ref in messages)
+            for step in range(8):
+                sends[step][32 + t] = share
+
+
+def y_call(listed, apart, weight, parts, wave):
+    messages = [x for part in parts for x in part]
+    tiles = 34 if listed else 32
+    shapes = [(tiles, 8, 128)] * 8 if apart else [(8, tiles, 8, 128)]
     return pl.pallas_call(
-        functools.partial(y_kernel, kinds, 2, apart_out),
+        functools.partial(y_kernel, len(parts), listed, apart),
         grid=(1,),
-        in_specs=[whole(x.shape) for x in operands]
+        in_specs=[whole(x.shape) for x in messages]
         + [pl.BlockSpec((1, 256, 256), lambda step: (lax.axis_index("sy"), 0, 0))],
         out_specs=[whole(shape) for shape in shapes],
         out_shape=[jax.ShapeDtypeStruct(shape, F32) for shape in shapes],
         scratch_shapes=[pltpu.VMEM((8, 8, 2, 2, 8, 128), F32)],
         compiler_params=pltpu.CompilerParams(vmem_limit_bytes=32 * MIB),
-        cost_estimate=cost(micros),
+        cost_estimate=cost(weight),
         name="along_y",
-    )(*operands, wave)
-
-
-def x_kernel(count, first_half, last, table_ref, source_ref, rows_ref, wave_ref, *refs):
+    )(*messages, wave)
+
+
+def x_kernel(count, listed, table_ref, source_ref, rows_ref, wave_ref, *refs):
     data_refs, work_ref = (refs[:count], refs[-1])
-    listed_ref = refs[-2] if first_half == 0 else None
-    out_ref = refs[-3] if first_half == 0 else refs[-2]
+    out_ref = refs[-3] if listed else refs[-2]
+    listed_ref = refs[-2] if listed else None
     if count == 1:
         data_refs = [data_refs[0].at[k] for k in range(8)]
-    step = pl.program_id(0)
-    half = first_half + step
+    half = pl.program_id(0)
     first_x, first_y = (lax.axis_index("sx") * 8, lax.axis_index("sy") * 16)
     blocks = [k if count == 1 else lax.axis_index("sx") ^ k for k in range(8)]
     w_high, w_low = split(jnp.concatenate([wave_ref[block] for block in blocks], 0))
     weights = jnp.concatenate([w_high, w_high, w_low], 0)
     lower = iota((8, 128), 1) < 64
     for f in range(16):
-        high, low = split(jnp.concatenate([ref[16 * step + f] for ref in data_refs], 0))
+        high, low = split(jnp.concatenate([ref[16 * half + f] for ref in data_refs], 0))
         out = tn_dot(jnp.concatenate([high, low, high], 0), weights)
         cosine = out[:, :128].reshape(2, 4, 2, 8, 128)
         sine = out[:, 128:].reshape(2, 4, 2, 8, 128)
@@ -450,26 +481,23 @@
         out_ref[g, 0, 1] = real * sine + imag * cosine
 
     def listed_sums():
-        total = sum(ref[ref.shape[0] - 1] for ref in data_refs)
-        rows = jnp.concatenate([total[:, 32 * k : 32 * k + 32] for k in range(4)], 0)
-        high, rest = split(rows)
-        middle, low = split(rows - high.astype(F32))
         mix = mix_matrix(rows_ref[...]).astype(BF16)
-        sums = nn_dot(mix, high) + nn_dot(mix, middle) + nn_dot(mix, low)
-        if last:
+        for t in range(2):
+            total = sum(ref[32 + t] for ref in data_refs)
+            rows = jnp.concatenate([total[:, 32 * k : 32 * k + 32] for k in range(4)], 0)
+            high, rest = split(rows)
+            middle, low = split(rows - high.astype(F32))
+            sums = nn_dot(mix, high) + nn_dot(mix, middle) + nn_dot(mix, low)
             for ri in range(2):
                 for g in range(16):
-                    row = slice(16 * ri + g, 16 * ri + g + 1)
-                    listed_ref[ri, g, 0:1] = refs[count][row, :]
-                    listed_ref[ri, g, 1:2] = sums[row]
-        else:
-            listed_ref[...] = sums
-
-    if first_half == 0:
-        pl.when(step == 0)(listed_sums)
-
-
-def x_call(which, half, halves, data, gammas, rows, source_site, wave, corr, listed):
+                    row = 16 * ri + g
+                    listed_ref[ri, g, t : t + 1] = sums[row : row + 1]
+
+    if listed:
+        pl.when(half == 0)(listed_sums)
+
+
+def x_call(which, data, gammas, rows, source_site, wave, corr):
     in_specs = [
         pl.BlockSpec(memory_space=pltpu.SMEM),
         pl.BlockSpec(memory_space=pltpu.SMEM),
@@ -478,21 +506,17 @@
     ] + [whole(x.shape) for x in data]
     operands = [gammas, source_site, rows, wave, *data]
     aliases = {}
-    if listed is not None:
-        in_specs.append(whole((32, 32)))
-        operands.append(listed)
+    shapes = [(16, 2, 2, 8, 1024)]
+    out_specs = [pl.BlockSpec((16, 1, 2, 8, 512), lambda step: (0, which, 0, 0, step))]
     if corr is not None:
         aliases = {len(operands): 0}
         in_specs.append(pl.BlockSpec(memory_space=pl.ANY))
         operands.append(corr)
-    shapes = [(16, 2, 2, 8, 1024)]
-    out_specs = [pl.BlockSpec((16, 1, 2, 8, 512), lambda step: (0, which, 0, 0, half + step))]
-    if half == 0:
-        shapes.append((32, 32) if listed is None else (2, 16, 2, 32))
+        shapes.append((2, 16, 2, 32))
         out_specs.append(whole(shapes[1]))
     return pl.pallas_call(
-        functools.partial(x_kernel, len(data), half, listed is not None),
-        grid=(halves,),
+        functools.partial(x_kernel, len(data), corr is not None),
+        grid=(2,),
         in_specs=in_specs,
         out_specs=out_specs,
         out_shape=[jax.ShapeDtypeStruct(shape, F32) for shape in shapes],
@@ -521,9 +545,9 @@
 
 
 def swap_sy(message):
-    out = [message[0]]
-    for step in range(1, 4):
-        out.append(lax.ppermute(message[step], "sy", [(k, k ^ step) for k in range(4)]))
+    out = list(message)
+    for step in (3, 2, 1):
+        out[step] = lax.ppermute(message[step], "sy", [(k, k ^ step) for k in range(4)])
     return out
 
 
@@ -532,9 +556,9 @@
 
 
 def swap_sx(message):
-    out = [message[0]]
-    for step in range(1, 8):
-        out.append(lax.ppermute(message[step], "sx", [(k, k ^ step) for k in range(8)]))
+    out = list(message)
+    for step in (1, 2, 3, 4, 5, 6, 7):
+        out[step] = lax.ppermute(message[step], "sx", [(k, k ^ step) for k in range(8)])
     return out
 
 
@@ -544,22 +568,26 @@
 
 def block_body(forward_prop, backward_prop, gamma_table, source_site, momenta):
     wave_z, wave_y, wave_x = (table_z(), table_y(), table_x())
-    inputs = (forward_prop, backward_prop, wave_z, source_site, momenta.T)
+    site, mom = (source_site, momenta.T)
     outer = (gamma_table.reshape(-1), gamma_table.reshape(16, 8), source_site, wave_x)
-    first = pair_call(0, 0, 8, True, *inputs)
-    inputs = after(inputs, first[0])
+    *first, fields = pair_call(0, 0, 3, False, None, forward_prop, backward_prop, wave_z, site, mom)
+    site, first = after((site, first))
     first = swap_sy(first)
-    third = pair_call(1, 0, 8, True, *inputs)
-    first, third = after((first, third))
+    *third, fields = pair_call(0, 3, 5, False, fields, forward_prop, backward_prop, wave_z, site, mom)
+    site, third = after((site, third))
+    first, third[1] = after((first, third[1]))
     third = swap_sy(third)
-    sent = y_call([first], wave_y, False, 0)
+    second = list(pair_call(1, 0, 8, True, fields, forward_prop, backward_prop, wave_z, site, mom))
+    third, second[1] = after((third, second[1]))
+    second = swap_sy(second)
+    sent = y_call(False, False, 0, [first, third], wave_y)
     data = swap_sx_whole(sent)
-    third = after(third, sent[0])
-    sent = y_call([third], wave_y, True, 1)
+    second[1:] = after(second[1:], sent[0])
+    sent = y_call(True, True, 1, [second], wave_y)
     data = after(data, sent[0])
-    corr, even = x_call(0, 0, 2, data, *outer, None, None)
-    third = swap_sx(sent)
-    corr, listed = x_call(1, 0, 2, third, *outer, corr, even)
+    (corr,) = x_call(0, data, *outer, None)
+    second = swap_sx(sent)
+    corr, listed = x_call(1, second, *outer, corr)
     return (corr, listed)
 
 

time: 86.1 us -> 82.9 us (0.963)
  waiting for transfers between devices: 30.6 us -> 19.3 us
  starting transfers between devices: 18.6 us -> 24 us
  Pallas kernels: 34.7 us -> 36.6 us
  local copies, waits for them, and re-layouts: 0.34 us -> 1.3 us
    ppermute x6 -> x9, waiting for transfers between devices: 26.4 us -> 14.3 us  [swap_sy(): lax.ppermute(message[step], 'sy', [(k, k ^ step) for k in range(4)])]
    ppermute x6 -> x9, starting transfers between devices: 6.98 us -> 12.4 us  [swap_sy(): lax.ppermute(message[step], 'sy', [(k, k ^ step) for k in range(4)])]
    pallas_call x6 -> x7, Pallas kernels: 34.7 us -> 36.6 us  [the longest x3 26.1 us: pair_call(): pl.pallas_call(functools.partial(pair_kernel, listed, bool(aliases)), gri...]
    unnamed x13 -> x15, local copies, waits for them, and re-layouts: 0.13 us -> 1.08 us
    ppermute x7, waiting for transfers between devices: 4.17 us -> 5.05 us  [swap_sx(): lax.ppermute(message[step], 'sx', [(k, k ^ step) for k in range(8)])]
  transfers between devices with their start and end apart: 14 -> 17, of which waited for: 6 -> 4; matrix products, arithmetic and copies ran while one was open for 0% -> 0% of each run, Pallas kernels for 23% -> 34%
where the time goes in v3:
time: 82.9 us; the launch traced here: 81.9 us
  Pallas kernels  36.6 us (44%)
  starting transfers between devices  24 us (29%)
  waiting for transfers between devices  19.3 us (23%)
  local copies, waits for them, and re-layouts  1.3 us (2%)
    pallas_call x3, Pallas kernels, pair_call(): pl.pallas_call(functools.partial(pair_kernel, listed, bool(aliases)), gri...  26.1 us
    ppermute x9, waiting for transfers between devices, swap_sy(): lax.ppermute(message[step], 'sy', [(k, k ^ step) for k in range(4)])  14.3 us
    ppermute x9, starting transfers between devices, swap_sy(): lax.ppermute(message[step], 'sy', [(k, k ^ step) for k in range(4)])  12.4 us
    ppermute x7, starting transfers between devices, swap_sx(): lax.ppermute(message[step], 'sx', [(k, k ^ step) for k in range(8)])  7.29 us
    pallas_call x2, Pallas kernels, x_call(): pl.pallas_call(functools.partial(x_kernel, len(data), corr is not None),...  7.05 us
    ppermute x7, waiting for transfers between devices, swap_sx(): lax.ppermute(message[step], 'sx', [(k, k ^ step) for k in range(8)])  5.05 us
    all_to_all x1, starting transfers between devices, swap_sx_whole(): return [lax.all_to_all(message[0], 'sx', 0, 0, tiled=True)]  4.26 us
    pallas_call x2, Pallas kernels, y_call(): pl.pallas_call(functools.partial(y_kernel, len(parts), listed, apart), gr...  3.41 us
  transfers between devices with their start and end apart: 17, of which 4 were waited for; matrix products, arithmetic and copies ran while one was open for 0% of the time, Pallas kernels for 34%

profile of v3, /device:TPU:16, one launch (start us, length us, event | category | flops | bytes accessed | tf_op | source)
XLA Modules:
  0.0 81.9 jit_solution(971512814240654951)
XLA Ops:
  0.6 5.7 %contract_and_z.3 = (f32[24,8,128]{2,1,0:T(8,128)}, f32[24,8,128]{2,1,0:T(8,128)}, f32[24,8,128]{2,1,0:T(8,128)}, f32[24,8,128]{2,1,0:T(8,128)}, f32[16,2,8,1024]{3,2,1,0:T(8,128)}) custom-call(s32[3]{0:T(128)} %source_ref.7, s32[3,32]{1,0:T(4,128)} %bitcast.2, bf16[2,2,12,12,8,1024]{5,4,3,2,1,0:T(8,128)(2,1)} %f_ref.5, ...), custom_call_target="tpu_custom_call" | custom-call | tf_op jit(solution)/shard_map/contract_and_z/pallas_call | solution.py:382
  6.3 1.6 %collective-permute-start = (f32[24,8,128]{2,1,0:T(8,128)}, f32[24,8,128]{2,1,0:T(8,128)S(1)}, u32[]{:S(2)}, u32[]{:S(2)}) collective-permute-start(f32[24,8,128]{2,1,0:T(8,128)} %get-tuple-element.63), channel_id=1, source_target_pairs={{0,1},{1,0},{2,3},{3,2},{4,5},{5,4},{6,7},{7,6},{8,9},{9,8},{10,11... | collective-permute-start | bytes 294920 | tf_op jit(solution)/shard_map/ppermute | solution.py:550
  7.9 0.3 collective-permute-start.1
  8.2 1.6 %collective-permute-start.2 = (f32[24,8,128]{2,1,0:T(8,128)}, f32[24,8,128]{2,1,0:T(8,128)S(1)}, u32[]{:S(2)}, u32[]{:S(2)}) collective-permute-start(f32[24,8,128]{2,1,0:T(8,128)} %get-tuple-element.65), channel_id=1, source_target_pairs={{0,3},{1,2},{2,1},{3,0},{4,7},{5,6},{6,5},{7,4},{8,11},{9,10},{10,... | collective-permute-start | bytes 294920 | tf_op jit(solution)/shard_map/ppermute | solution.py:550
  9.8 8.0 %contract_and_z.4 = (f32[40,8,128]{2,1,0:T(8,128)}, f32[40,8,128]{2,1,0:T(8,128)}, f32[40,8,128]{2,1,0:T(8,128)}, f32[40,8,128]{2,1,0:T(8,128)}, f32[16,2,8,1024]{3,2,1,0:T(8,128)}) custom-call(s32[3]{0:T(128)} %source_ref.7, s32[3,32]{1,0:T(4,128)} %bitcast.3, bf16[2,2,12,12,8,1024]{5,4,3,2,1,0:T(8,128)(2,1)} %f_ref.5, ...), custom_call_target="tpu_custom_call", output_to_operand_aliasing={{4}: (5, {})} | custom-call | tf_op jit(solution)/shard_map/contract_and_z/pallas_call | solution.py:382
  17.8 1.0 %collective-permute-start.4 = (f32[40,8,128]{2,1,0:T(8,128)}, f32[40,8,128]{2,1,0:T(8,128)S(1)}, u32[]{:S(2)}, u32[]{:S(2)}) collective-permute-start(f32[40,8,128]{2,1,0:T(8,128)} %get-tuple-element.68), channel_id=1, source_target_pairs={{0,2},{1,3},{2,0},{3,1},{4,6},{5,7},{6,4},{7,5},{8,10},{9,11},{10,... | collective-permute-start | bytes 491528 | tf_op jit(solution)/shard_map/ppermute | solution.py:550
  18.8 2.9 %collective-permute-start.5 = (f32[40,8,128]{2,1,0:T(8,128)}, f32[40,8,128]{2,1,0:T(8,128)S(1)}, u32[]{:S(2)}, u32[]{:S(2)}) collective-permute-start(f32[40,8,128]{2,1,0:T(8,128)} %get-tuple-element.69), channel_id=1, source_target_pairs={{0,3},{1,2},{2,1},{3,0},{4,7},{5,6},{6,5},{7,4},{8,11},{9,10},{10,... | collective-permute-start | bytes 491528 | tf_op jit(solution)/shard_map/ppermute | solution.py:550
  21.7 0.0 collective-permute-done.refs_1_
  21.7 0.0 collective-permute-done.1.refs_2_
  21.7 0.0 collective-permute-done.2.refs_3_
  21.7 0.5 collective-permute-start.3
  22.2 12.5 %contract_and_z.5 = (f32[66,8,128]{2,1,0:T(8,128)}, f32[66,8,128]{2,1,0:T(8,128)}, f32[66,8,128]{2,1,0:T(8,128)}, f32[66,8,128]{2,1,0:T(8,128)}) custom-call(s32[3]{0:T(128)} %source_ref.7, s32[3,32]{1,0:T(4,128)} %bitcast.4, bf16[2,2,12,12,8,1024]{5,4,3,2,1,0:T(8,128)(2,1)} %f_ref.5, bf16[2,2,12,12,8,1024]{5,4,3,2,1,0:T(8,128)(2,1)} %b_ref.5, ...), custom_call_target="tpu_custom_call" | custom-call | tf_op jit(solution)/shard_map/contract_and_z/pallas_call | solution.py:382
  34.7 1.0 %collective-permute-start.7 = (f32[66,8,128]{2,1,0:T(8,128)}, f32[66,8,128]{2,1,0:T(8,128)S(1)}, u32[]{:S(2)}, u32[]{:S(2)}) collective-permute-start(f32[66,8,128]{2,1,0:T(8,128)} %get-tuple-element.72), channel_id=1, source_target_pairs={{0,2},{1,3},{2,0},{3,1},{4,6},{5,7},{6,4},{7,5},{8,10},{9,11},{10,... | collective-permute-start | bytes 811016 | tf_op jit(solution)/shard_map/ppermute | solution.py:550
  35.7 2.0 %collective-permute-start.8 = (f32[66,8,128]{2,1,0:T(8,128)}, f32[66,8,128]{2,1,0:T(8,128)S(1)}, u32[]{:S(2)}, u32[]{:S(2)}) collective-permute-start(f32[66,8,128]{2,1,0:T(8,128)} %get-tuple-element.73), channel_id=1, source_target_pairs={{0,3},{1,2},{2,1},{3,0},{4,7},{5,6},{6,5},{7,4},{8,11},{9,10},{10,... | collective-permute-start | bytes 811016 | tf_op jit(solution)/shard_map/ppermute | solution.py:550
  37.8 0.0 collective-permute-done.4.refs_6_
  37.8 0.0 collective-permute-done.5.refs_7_
  37.8 0.0 collective-permute-done.3.refs_5_
  37.8 1.4 %collective-permute-start.6 = (f32[66,8,128]{2,1,0:T(8,128)}, f32[66,8,128]{2,1,0:T(8,128)S(1)}, u32[]{:S(2)}, u32[]{:S(2)}) collective-permute-start(f32[66,8,128]{2,1,0:T(8,128)} %get-tuple-element.71), channel_id=1, source_target_pairs={{0,1},{1,0},{2,3},{3,2},{4,5},{5,4},{6,7},{7,6},{8,9},{9,8},{10,11... | collective-permute-start | bytes 811016 | tf_op jit(solution)/shard_map/ppermute | solution.py:550
  39.2 0.0 copy-done
  39.2 0.0 copy-done.2
  39.2 0.0 copy-done.3
  39.2 2.1 %along_y.2 = f32[8,32,8,128]{3,2,1,0:T(8,128)} custom-call(f32[24,8,128]{2,1,0:T(8,128)S(1)} %copy-done.3, f32[24,8,128]{2,1,0:T(8,128)S(1)} %collective-permute-done.refs_1_, f32[24,8,128]{2,1,0:T(8,128)S(1)} %collective-permute-done.1.refs_2_, f32[24,8,128]{2,1,0:T(8,128)S(1)} %collective-permute-done.2.refs_3_, f32[40,8,128]{2,1,0:T(8,128)S(1)} %copy-done.2, ...), custom_call_target="tpu_custom_call" | custom-call | tf_op jit(solution)/shard_map/along_y/pallas_call | solution.py:429
  41.3 4.3 %all-to-all-start = ((f32[8,32,8,128]{3,2,1,0:T(8,128)}), f32[8,32,8,128]{3,2,1,0:T(8,128)}, u32[]{:S(2)}, u32[]{:S(2)}) async-start(f32[8,32,8,128]{3,2,1,0:T(8,128)} %along_y.2), calls=%async_computation | async-start | bytes 2097152 | tf_op jit(solution)/shard_map/all_to_all | solution.py:555
  45.6 7.6 %collective-permute-done.7.refs_2_ = f32[66,8,128]{2,1,0:T(8,128)S(1)} collective-permute-done((f32[66,8,128]{2,1,0:T(8,128)}, f32[66,8,128]{2,1,0:T(8,128)S(1)}, u32[]{:S(2)}, u32[]{:S(2)}) %collective-permute-start.7) | collective-permute-done | bytes 270368 | tf_op jit(solution)/shard_map/ppermute | solution.py:550
  53.2 6.6 %collective-permute-done.8.refs_3_ = f32[66,8,128]{2,1,0:T(8,128)S(1)} collective-permute-done((f32[66,8,128]{2,1,0:T(8,128)}, f32[66,8,128]{2,1,0:T(8,128)S(1)}, u32[]{:S(2)}, u32[]{:S(2)}) %collective-permute-start.8) | collective-permute-done | bytes 270368 | tf_op jit(solution)/shard_map/ppermute | solution.py:550
  59.8 0.0 collective-permute-done.6.refs_1_
  59.8 1.0 %copy-done.5 = f32[66,8,128]{2,1,0:T(8,128)S(1)} copy-done((f32[66,8,128]{2,1,0:T(8,128)S(1)}, f32[66,8,128]{2,1,0:T(8,128)}, u32[]{:S(2)}) %copy-start.5) | copy-done | bytes 270360
  60.8 1.3 %along_y.3 = (f32[34,8,128]{2,1,0:T(8,128)S(1)}, f32[34,8,128]{2,1,0:T(8,128)S(1)}, f32[34,8,128]{2,1,0:T(8,128)S(1)}, f32[34,8,128]{2,1,0:T(8,128)S(1)}, f32[34...) custom-call(f32[66,8,128]{2,1,0:T(8,128)S(1)} %copy-done.5, ...), custom_call_target="tpu_custom_call" | custom-call | flops 9999999827968 | tf_op jit(solution)/shard_map/along_y/pallas_call | solution.py:429
  62.1 0.2 collective-permute-start.9
  62.3 1.5 %collective-permute-start.10 = (f32[34,8,128]{2,1,0:T(8,128)S(1)}, f32[34,8,128]{2,1,0:T(8,128)S(1)}, u32[]{:S(2)}, u32[]{:S(2)}) collective-permute-start(f32[34,8,128]{2,1,0:T(8,128)S(1)} %get-tuple-element.87), channel_id=1, source_target_pairs={{0,8},{4,12},{8,0},{12,4},{16,24},{20,28},{24,16},{28,20},{1,9},{5... | collective-permute-start | bytes 417800 | tf_op jit(solution)/shard_map/ppermute | solution.py:561
  63.8 0.2 collective-permute-start.11
  64.0 1.5 %collective-permute-start.12 = (f32[34,8,128]{2,1,0:T(8,128)S(1)}, f32[34,8,128]{2,1,0:T(8,128)S(1)}, u32[]{:S(2)}, u32[]{:S(2)}) collective-permute-start(f32[34,8,128]{2,1,0:T(8,128)S(1)} %get-tuple-element.89), channel_id=1, source_target_pairs={{0,16},{4,20},{8,24},{12,28},{16,0},{20,4},{24,8},{28,12},{1,17},{... | collective-permute-start | bytes 417800 | tf_op jit(solution)/shard_map/ppermute | solution.py:561
  65.5 0.3 collective-permute-start.13
  65.8 0.0 collective-permute-done.9.refs_1_
  65.8 2.4 %collective-permute-start.14 = (f32[34,8,128]{2,1,0:T(8,128)S(1)}, f32[34,8,128]{2,1,0:T(8,128)S(1)}, u32[]{:S(2)}, u32[]{:S(2)}) collective-permute-start(f32[34,8,128]{2,1,0:T(8,128)S(1)} %get-tuple-element.91), channel_id=1, source_target_pairs={{0,24},{4,28},{8,16},{12,20},{16,8},{20,12},{24,0},{28,4},{1,25},{... | collective-permute-start | bytes 417800 | tf_op jit(solution)/shard_map/ppermute | solution.py:561
  68.2 0.6 collective-permute-done.10.refs_2_
  68.8 1.2 %collective-permute-start.15 = (f32[34,8,128]{2,1,0:T(8,128)S(1)}, f32[34,8,128]{2,1,0:T(8,128)S(1)}, u32[]{:S(2)}, u32[]{:S(2)}) collective-permute-start(f32[34,8,128]{2,1,0:T(8,128)S(1)} %get-tuple-element.92), channel_id=1, source_target_pairs={{0,28},{4,24},{8,20},{12,16},{16,12},{20,8},{24,4},{28,0},{1,29},{... | collective-permute-start | bytes 417800 | tf_op jit(solution)/shard_map/ppermute | solution.py:561
  70.0 0.1 copy.15
  70.1 0.1 copy.17.rows_ref
  70.2 0.1 reshape.10.table_ref
  70.3 0.0 all-to-all-done.refs_0_
  70.4 3.7 %along_x.2.refs_8_ = f32[16,2,2,8,1024]{4,3,2,1,0:T(8,128)} custom-call(s32[128]{0:T(128)S(1)} %reshape.10.table_ref, s32[3]{0:T(128)S(1)} %copy-done.4, s32[16,8]{1,0:T(8,128)S(1)} %copy.17.rows_ref, f32[8,8,256]{2,1,0:T(8,128)S(1)} %copy-done.1, f32[8,32,8,128]{3,2,1,0:T(8,128)} %all-to-all-done.refs_0_), custom_call_target="tpu_custom_call" | custom-call | tf_op jit(solution)/shard_map/along_x/pallas_call | solution.py:517
  74.1 0.0 collective-permute-done.11.refs_3_
  74.1 0.0 collective-permute-done.12.refs_4_
  74.1 4.4 %collective-permute-done.13.refs_5_ = f32[34,8,128]{2,1,0:T(8,128)S(1)} collective-permute-done((f32[34,8,128]{2,1,0:T(8,128)S(1)}, f32[34,8,128]{2,1,0:T(8,128)S(1)}, u32[]{:S(2)}, u32[]{:S(2)}) %collective-permute-start.13) | collective-permute-done | bytes 139296 | tf_op jit(solution)/shard_map/ppermute | solution.py:561
  78.5 0.0 collective-permute-done.14.refs_6_
  78.5 0.0 collective-permute-done.15.refs_7_
  78.5 3.3 %along_x.3 = (f32[16,2,2,8,1024]{4,3,2,1,0:T(8,128)}, f32[2,16,2,32]{3,2,1,0:T(2,128)}) custom-call(s32[128]{0:T(128)S(1)} %reshape.10.table_ref, s32[3]{0:T(128)S(1)} %copy-done.4, s32[16,8]{1,0:T(8,128)S(1)} %copy.17.rows_ref, f32[8,8,256]{2,1,0:T(8,128)S(1)} %copy-done.1, ...), custom_call_target="tpu_custom_call", output_to_operand_aliasing={{0}: (12, {})} | custom-call | tf_op jit(solution)/shard_map/along_x/pallas_call | solution.py:517
  (10 shorter events, 0.0 us)
Async XLA Ops:
  6.3 15.4 %collective-permute-start = (f32[24,8,128]{2,1,0:T(8,128)}, f32[24,8,128]{2,1,0:T(8,128)S(1)}, u32[]{:S(2)}, u32[]{:S(2)}) collective-permute-start(f32[24,8,128]{2,1,0:T(8,128)} %get-tuple-element.63), channel_id=1, source_target_pairs={{0,1},{1,0},{2,3},{3,2},{4,5},{5,4},{6,7},{7,6},{8,9},{9,8},{10,11... | collective-permute-start | bytes 294920 | tf_op jit(solution)/shard_map/ppermute | solution.py:550
  7.9 13.8 %collective-permute-start.1 = (f32[24,8,128]{2,1,0:T(8,128)}, f32[24,8,128]{2,1,0:T(8,128)S(1)}, u32[]{:S(2)}, u32[]{:S(2)}) collective-permute-start(f32[24,8,128]{2,1,0:T(8,128)} %get-tuple-element.64), channel_id=1, source_target_pairs={{0,2},{1,3},{2,0},{3,1},{4,6},{5,7},{6,4},{7,5},{8,10},{9,11},{10,... | collective-permute-start | bytes 294920 | tf_op jit(solution)/shard_map/ppermute | solution.py:550
  8.2 13.5 %collective-permute-start.2 = (f32[24,8,128]{2,1,0:T(8,128)}, f32[24,8,128]{2,1,0:T(8,128)S(1)}, u32[]{:S(2)}, u32[]{:S(2)}) collective-permute-start(f32[24,8,128]{2,1,0:T(8,128)} %get-tuple-element.65), channel_id=1, source_target_pairs={{0,3},{1,2},{2,1},{3,0},{4,7},{5,6},{6,5},{7,4},{8,11},{9,10},{10,... | collective-permute-start | bytes 294920 | tf_op jit(solution)/shard_map/ppermute | solution.py:550
  17.8 20.0 %collective-permute-start.4 = (f32[40,8,128]{2,1,0:T(8,128)}, f32[40,8,128]{2,1,0:T(8,128)S(1)}, u32[]{:S(2)}, u32[]{:S(2)}) collective-permute-start(f32[40,8,128]{2,1,0:T(8,128)} %get-tuple-element.68), channel_id=1, source_target_pairs={{0,2},{1,3},{2,0},{3,1},{4,6},{5,7},{6,4},{7,5},{8,10},{9,11},{10,... | collective-permute-start | bytes 491528 | tf_op jit(solution)/shard_map/ppermute | solution.py:550
  18.8 19.0 %collective-permute-start.5 = (f32[40,8,128]{2,1,0:T(8,128)}, f32[40,8,128]{2,1,0:T(8,128)S(1)}, u32[]{:S(2)}, u32[]{:S(2)}) collective-permute-start(f32[40,8,128]{2,1,0:T(8,128)} %get-tuple-element.69), channel_id=1, source_target_pairs={{0,3},{1,2},{2,1},{3,0},{4,7},{5,6},{6,5},{7,4},{8,11},{9,10},{10,... | collective-permute-start | bytes 491528 | tf_op jit(solution)/shard_map/ppermute | solution.py:550
  21.7 16.1 %collective-permute-start.3 = (f32[40,8,128]{2,1,0:T(8,128)}, f32[40,8,128]{2,1,0:T(8,128)S(1)}, u32[]{:S(2)}, u32[]{:S(2)}) collective-permute-start(f32[40,8,128]{2,1,0:T(8,128)} %get-tuple-element.67), channel_id=1, source_target_pairs={{0,1},{1,0},{2,3},{3,2},{4,5},{5,4},{6,7},{7,6},{8,9},{9,8},{10,11... | collective-permute-start | bytes 491528 | tf_op jit(solution)/shard_map/ppermute | solution.py:550
  22.2 17.0 %copy-start = (f32[4,256,256]{2,1,0:T(8,128)S(1)}, f32[4,256,256]{2,1,0:T(8,128)}, u32[]{:S(2)}) copy-start(f32[4,256,256]{2,1,0:T(8,128)} %constant.7.clone.refs_8_.refs_4_) | copy-start | bytes 3145732
  22.2 17.0 %copy-start.2 = (f32[40,8,128]{2,1,0:T(8,128)S(1)}, f32[40,8,128]{2,1,0:T(8,128)}, u32[]{:S(2)}) copy-start(f32[40,8,128]{2,1,0:T(8,128)} %get-tuple-element.78.refs_4_) | copy-start | bytes 491524
  22.2 17.0 %copy-start.3 = (f32[24,8,128]{2,1,0:T(8,128)S(1)}, f32[24,8,128]{2,1,0:T(8,128)}, u32[]{:S(2)}) copy-start(f32[24,8,128]{2,1,0:T(8,128)} %get-tuple-element.74.refs_0_) | copy-start | bytes 294916
  34.7 18.4 %collective-permute-start.7 = (f32[66,8,128]{2,1,0:T(8,128)}, f32[66,8,128]{2,1,0:T(8,128)S(1)}, u32[]{:S(2)}, u32[]{:S(2)}) collective-permute-start(f32[66,8,128]{2,1,0:T(8,128)} %get-tuple-element.72), channel_id=1, source_target_pairs={{0,2},{1,3},{2,0},{3,1},{4,6},{5,7},{6,4},{7,5},{8,10},{9,11},{10,... | collective-permute-start | bytes 811016 | tf_op jit(solution)/shard_map/ppermute | solution.py:550
  35.7 24.1 %collective-permute-start.8 = (f32[66,8,128]{2,1,0:T(8,128)}, f32[66,8,128]{2,1,0:T(8,128)S(1)}, u32[]{:S(2)}, u32[]{:S(2)}) collective-permute-start(f32[66,8,128]{2,1,0:T(8,128)} %get-tuple-element.73), channel_id=1, source_target_pairs={{0,3},{1,2},{2,1},{3,0},{4,7},{5,6},{6,5},{7,4},{8,11},{9,10},{10,... | collective-permute-start | bytes 811016 | tf_op jit(solution)/shard_map/ppermute | solution.py:550
  37.8 22.0 %collective-permute-start.6 = (f32[66,8,128]{2,1,0:T(8,128)}, f32[66,8,128]{2,1,0:T(8,128)S(1)}, u32[]{:S(2)}, u32[]{:S(2)}) collective-permute-start(f32[66,8,128]{2,1,0:T(8,128)} %get-tuple-element.71), channel_id=1, source_target_pairs={{0,1},{1,0},{2,3},{3,2},{4,5},{5,4},{6,7},{7,6},{8,9},{9,8},{10,11... | collective-permute-start | bytes 811016 | tf_op jit(solution)/shard_map/ppermute | solution.py:550
  41.3 29.0 %all-to-all-start = ((f32[8,32,8,128]{3,2,1,0:T(8,128)}), f32[8,32,8,128]{3,2,1,0:T(8,128)}, u32[]{:S(2)}, u32[]{:S(2)}) async-start(f32[8,32,8,128]{3,2,1,0:T(8,128)} %along_y.2), calls=%async_computation | async-start | bytes 2097152 | tf_op jit(solution)/shard_map/all_to_all | solution.py:555
  59.8 1.0 %copy-start.5 = (f32[66,8,128]{2,1,0:T(8,128)S(1)}, f32[66,8,128]{2,1,0:T(8,128)}, u32[]{:S(2)}) copy-start(f32[66,8,128]{2,1,0:T(8,128)} %get-tuple-element.60.refs_0_) | copy-start | bytes 811012
  60.8 9.2 %copy-start.6 = (s32[16,4,2]{0,2,1:T(2,128)S(1)}, s32[16,4,2]{0,2,1:T(2,128)}, u32[]{:S(2)}) copy-start(s32[16,4,2]{0,2,1:T(2,128)} %param.10) | copy-start | bytes 1540
  60.8 9.6 %copy-start.1 = (f32[8,8,256]{2,1,0:T(8,128)S(1)}, f32[8,8,256]{2,1,0:T(8,128)}, u32[]{:S(2)}) copy-start(f32[8,8,256]{2,1,0:T(8,128)} %constant.8.clone.wave_ref) | copy-start | bytes 196612
  60.8 9.6 %copy-start.4 = (s32[3]{0:T(128)S(1)}, s32[3]{0:T(128)}, u32[]{:S(2)}) copy-start(s32[3]{0:T(128)} %source_ref.7) | copy-start | bytes 40
  62.1 3.7 %collective-permute-start.9 = (f32[34,8,128]{2,1,0:T(8,128)S(1)}, f32[34,8,128]{2,1,0:T(8,128)S(1)}, u32[]{:S(2)}, u32[]{:S(2)}) collective-permute-start(f32[34,8,128]{2,1,0:T(8,128)S(1)} %get-tuple-element.86), channel_id=1, source_target_pairs={{0,4},{4,0},{8,12},{12,8},{16,20},{20,16},{24,28},{28,24},{1,5},{5... | collective-permute-start | bytes 417800 | tf_op jit(solution)/shard_map/ppermute | solution.py:561
  62.3 6.5 %collective-permute-start.10 = (f32[34,8,128]{2,1,0:T(8,128)S(1)}, f32[34,8,128]{2,1,0:T(8,128)S(1)}, u32[]{:S(2)}, u32[]{:S(2)}) collective-permute-start(f32[34,8,128]{2,1,0:T(8,128)S(1)} %get-tuple-element.87), channel_id=1, source_target_pairs={{0,8},{4,12},{8,0},{12,4},{16,24},{20,28},{24,16},{28,20},{1,9},{5... | collective-permute-start | bytes 417800 | tf_op jit(solution)/shard_map/ppermute | solution.py:561
  63.8 10.3 %collective-permute-start.11 = (f32[34,8,128]{2,1,0:T(8,128)S(1)}, f32[34,8,128]{2,1,0:T(8,128)S(1)}, u32[]{:S(2)}, u32[]{:S(2)}) collective-permute-start(f32[34,8,128]{2,1,0:T(8,128)S(1)} %get-tuple-element.88), channel_id=1, source_target_pairs={{0,12},{4,8},{8,4},{12,0},{16,28},{20,24},{24,20},{28,16},{1,13},{... | collective-permute-start | bytes 417800 | tf_op jit(solution)/shard_map/ppermute | solution.py:561
  64.0 10.1 %collective-permute-start.12 = (f32[34,8,128]{2,1,0:T(8,128)S(1)}, f32[34,8,128]{2,1,0:T(8,128)S(1)}, u32[]{:S(2)}, u32[]{:S(2)}) collective-permute-start(f32[34,8,128]{2,1,0:T(8,128)S(1)} %get-tuple-element.89), channel_id=1, source_target_pairs={{0,16},{4,20},{8,24},{12,28},{16,0},{20,4},{24,8},{28,12},{1,17},{... | collective-permute-start | bytes 417800 | tf_op jit(solution)/shard_map/ppermute | solution.py:561
  65.5 13.0 %collective-permute-start.13 = (f32[34,8,128]{2,1,0:T(8,128)S(1)}, f32[34,8,128]{2,1,0:T(8,128)S(1)}, u32[]{:S(2)}, u32[]{:S(2)}) collective-permute-start(f32[34,8,128]{2,1,0:T(8,128)S(1)} %get-tuple-element.90), channel_id=1, source_target_pairs={{0,20},{4,16},{8,28},{12,24},{16,4},{20,0},{24,12},{28,8},{1,21},{... | collective-permute-start | bytes 417800 | tf_op jit(solution)/shard_map/ppermute | solution.py:561
  65.8 12.7 %collective-permute-start.14 = (f32[34,8,128]{2,1,0:T(8,128)S(1)}, f32[34,8,128]{2,1,0:T(8,128)S(1)}, u32[]{:S(2)}, u32[]{:S(2)}) collective-permute-start(f32[34,8,128]{2,1,0:T(8,128)S(1)} %get-tuple-element.91), channel_id=1, source_target_pairs={{0,24},{4,28},{8,16},{12,20},{16,8},{20,12},{24,0},{28,4},{1,25},{... | collective-permute-start | bytes 417800 | tf_op jit(solution)/shard_map/ppermute | solution.py:561
  68.8 9.7 %collective-permute-start.15 = (f32[34,8,128]{2,1,0:T(8,128)S(1)}, f32[34,8,128]{2,1,0:T(8,128)S(1)}, u32[]{:S(2)}, u32[]{:S(2)}) collective-permute-start(f32[34,8,128]{2,1,0:T(8,128)S(1)} %get-tuple-element.92), channel_id=1, source_target_pairs={{0,28},{4,24},{8,20},{12,16},{16,12},{20,8},{24,4},{28,0},{1,29},{... | collective-permute-start | bytes 417800 | tf_op jit(solution)/shard_map/ppermute | solution.py:561

commit v4 on v3

--- a/solution.py
+++ b/solution.py
@@ -139,6 +139,7 @@
 F32 = jnp.float32
 BF16 = jnp.bfloat16
 MIB = 2**20
+SX_ORDER = (0, 1, 4, 2, 6, 5, 3, 7)
 
 
 def split(values):
@@ -205,12 +206,12 @@
     return pl.CostEstimate(flops=weight * 10**13, bytes_accessed=0, transcendentals=0)
 
 
-def contract_block(f_ref, b_ref):
+def contract_block(f_ref, b_ref, lanes):
     def add(total, term):
         return term if total is None else total + term
 
     def load(ref, ri, row, pair):
-        both = ref[0, ri, row, 2 * pair : 2 * pair + 2].astype(F32)
+        both = ref[0, ri, row, 2 * pair : 2 * pair + 2, :, lanes].astype(F32)
         return (both[0], both[1])
 
     one, two, three = ([None] * 16, [None] * 16, [None] * 16)
@@ -249,9 +250,9 @@
     return lax.broadcasted_iota(jnp.int32, shape, dim)
 
 
-def planes(ref):
-    re_high, re_low = split(ref[:, 0].reshape(128, 128))
-    im_high, im_low = split(ref[:, 1].reshape(128, 128))
+def planes(ref, lanes):
+    re_high, re_low = split(ref[:, 0, :, lanes].reshape(128, 128))
+    im_high, im_low = split(ref[:, 1, :, lanes].reshape(128, 128))
     return (jnp.concatenate([re_high, im_high], 1), jnp.concatenate([re_low, im_low], 1))
 
 
@@ -292,8 +293,8 @@
     else:
         *sends, fields_ref, field_ref, w_high_ref, w_low_ref = refs
     step = pl.program_id(0)
-    rows = pl.num_programs(0) - 1
-    row = jnp.maximum(step - 1, 0)
+    steps = pl.num_programs(0) - 1
+    parts = f_ref.shape[5] // 128
 
     @pl.when(step == 0)
     def _():
@@ -305,7 +306,7 @@
             momentum_tables(mom_ref, tm_high_ref, tm_low_ref)
             total_ref[...] = jnp.zeros_like(total_ref)
 
-    def project(t, high, low):
+    def project(t, high, low, row, there):
         proj = (
             nn_dot(high, tm_high_ref[...])
             + nn_dot(high, tm_low_ref[...])
@@ -313,34 +314,40 @@
         )
         value, turned = (proj[:, :128], proj[:, 128:])
         cosine, sine = phases(2 * momentum_lanes(mom_ref)[1] * row)
-        there = step > 0
         total_ref[t, 0] += jnp.where(there, cosine * value + sine * turned, 0.0)
         total_ref[t, 1] += jnp.where(there, cosine * turned - sine * value, 0.0)
 
-    def transform():
-        high, low = planes(field_ref)
+    def transform(row, there):
+        high, low = planes(field_ref, pl.ds(0, 128))
         w_high, w_low = (w_high_ref[...], w_low_ref[...])
         out = nt_dot(w_high, high) + nt_dot(w_low, high) + nt_dot(w_high, low)
-        out = out.reshape(4, 8, 8, 128)
+        halves = len(sends) // 4
+        count = 8 // halves
+        out = out.reshape(4, halves, count, 8, 128)
         for s in range(4):
-            sends[s][pl.ds(8 * row, 8)] = out[s]
+            for h in range(halves):
+                sends[4 * h + s][pl.ds(count * row, count)] = out[s, h]
         if listed:
-            project(1, high, low)
-            project(0, *planes(old_ref))
-
-    @pl.when(step < rows)
+            project(1, high, low, row, there)
+
+    @pl.when(step < steps)
     def _():
-        transform()
-        for k, (real, imag) in enumerate(contract_block(f_ref, b_ref)):
-            field_ref[k, 0] = real
-            field_ref[k, 1] = imag
-            if not listed:
-                fields_ref[k, 0] = real
-                fields_ref[k, 1] = imag
-
-    @pl.when(step == rows)
+        for part in range(parts):
+            lanes = pl.ds(128 * part, 128)
+            row = parts * step + part
+            transform(jnp.maximum(row - 1, 0), row > 0)
+            if listed:
+                project(0, *planes(old_ref, lanes), row, True)
+            for k, (real, imag) in enumerate(contract_block(f_ref, b_ref, lanes)):
+                field_ref[k, 0] = real
+                field_ref[k, 1] = imag
+                if not listed:
+                    fields_ref[k, 0, :, lanes] = real
+                    fields_ref[k, 1, :, lanes] = imag
+
+    @pl.when(step == steps)
     def _():
-        transform()
+        transform(parts * steps - 1, True)
         if listed:
             mom_x, mom_y, mom_z = momentum_lanes(mom_ref)
             x = lax.axis_index("sx") * 8 - source_ref[0] + iota((8, 128), 0)
@@ -355,12 +362,15 @@
                     sends[s][64 + t] = tile
 
 
-def pair_call(which, start, rows, listed, fields, forward, backward, wave, source_site, momenta):
+def pair_call(which, start, rows, parts, listed, fields, forward, backward, wave, source_site, momenta):
+    steps = rows // parts
+    lanes = 128 * parts
+
     def block(step):
-        return (which, 0, 0, 0, 0, start + jnp.minimum(step, rows - 1))
+        return (which, 0, 0, 0, 0, start // parts + jnp.minimum(step, steps - 1))
 
     in_specs = [pl.BlockSpec(memory_space=pltpu.SMEM)] * 2
-    in_specs += [pl.BlockSpec((1, 2, 12, 12, 8, 128), block)] * 2 + [whole((4, 64, 256))]
+    in_specs += [pl.BlockSpec((1, 2, 12, 12, 8, lanes), block)] * 2 + [whole((4, 64, 256))]
     operands = [source_site, momenta, forward, backward, wave]
     shapes = [(8 * rows + 2 if listed else 8 * rows, 8, 128)] * 4
     out_specs = [whole(shape) for shape in shapes]
@@ -368,20 +378,20 @@
     aliases = {}
     if listed:
         in_specs.append(
-            pl.BlockSpec((16, 2, 8, 128), lambda step: (0, 0, 0, jnp.maximum(step - 1, 0)))
+            pl.BlockSpec((16, 2, 8, lanes), lambda step: (0, 0, 0, block(step)[5]))
         )
         operands.append(fields)
         scratch += [pltpu.VMEM((256, 256), BF16)] * 2 + [pltpu.VMEM((2, 2, 128, 128), F32)]
     else:
         shapes.append((16, 2, 8, 1024))
-        out_specs.append(pl.BlockSpec((16, 2, 8, 128), lambda step: (0, 0, 0, block(step)[5])))
+        out_specs.append(pl.BlockSpec((16, 2, 8, lanes), lambda step: (0, 0, 0, block(step)[5])))
         if fields is not None:
             in_specs.append(pl.BlockSpec(memory_space=pl.ANY))
             operands.append(fields)
             aliases = {5: 4}
     return pl.pallas_call(
         functools.partial(pair_kernel, listed, bool(aliases)),
-        grid=(rows + 1,),
+        grid=(steps + 1,),
         in_specs=in_specs,
         out_specs=out_specs,
         out_shape=[jax.ShapeDtypeStruct(shape, F32) for shape in shapes],
@@ -393,17 +403,25 @@
     )(*operands)
 
 
-def y_kernel(parts, listed, apart, *refs):
+def y_kernel(parts, listed, apart, kept, *refs):
     messages = [refs[s + 4 * part] for s in range(4) for part in range(parts)]
+    if kept:
+        refs[-2][...] = refs[4 * parts + 1][...]
+        refs = refs[: 4 * parts + 1] + refs[4 * parts + 2 : -2] + refs[-1:]
     wave_ref, *sends, work_ref = refs[4 * parts :]
     if not apart:
         sends = [sends[0].at[k] for k in range(8)]
     w_high, w_low = split(wave_ref[0])
-    for q in range(8):
-        data = [ref[8 * y + q] for ref in messages for y in range(ref.shape[0] // 8)]
+    for q in range(0, 8, 2):
+        data = [
+            jnp.concatenate([ref[8 * y + q], ref[8 * y + q + 1]], 1)
+            for ref in messages
+            for y in range(ref.shape[0] // 8)
+        ]
         high, low = split(jnp.concatenate(data, 0))
         out = nn_dot(w_high, high) + nn_dot(w_low, high) + nn_dot(w_high, low)
-        work_ref[q] = out.reshape(8, 2, 2, 8, 128)
+        work_ref[q] = out[:, :128].reshape(8, 2, 2, 8, 128)
+        work_ref[q + 1] = out[:, 128:].reshape(8, 2, 2, 8, 128)
     for h in range(2):
         for step in range(8):
             block = lax.axis_index("sx") ^ step if apart else step
@@ -422,22 +440,25 @@
                 sends[step][32 + t] = share
 
 
-def y_call(listed, apart, weight, parts, wave):
+def y_call(listed, apart, weight, parts, wave, kept=None):
     messages = [x for part in parts for x in part]
     tiles = 34 if listed else 32
     shapes = [(tiles, 8, 128)] * 8 if apart else [(8, tiles, 8, 128)]
+    extra = [] if kept is None else [kept]
+    shapes += [x.shape for x in extra]
     return pl.pallas_call(
-        functools.partial(y_kernel, len(parts), listed, apart),
+        functools.partial(y_kernel, len(parts), listed, apart, kept is not None),
         grid=(1,),
         in_specs=[whole(x.shape) for x in messages]
-        + [pl.BlockSpec((1, 256, 256), lambda step: (lax.axis_index("sy"), 0, 0))],
+        + [pl.BlockSpec((1, 256, 256), lambda step: (lax.axis_index("sy"), 0, 0))]
+        + [whole(x.shape) for x in extra],
         out_specs=[whole(shape) for shape in shapes],
         out_shape=[jax.ShapeDtypeStruct(shape, F32) for shape in shapes],
         scratch_shapes=[pltpu.VMEM((8, 8, 2, 2, 8, 128), F32)],
         compiler_params=pltpu.CompilerParams(vmem_limit_bytes=32 * MIB),
         cost_estimate=cost(weight),
         name="along_y",
-    )(*messages, wave)
+    )(*messages, wave, *extra)
 
 
 def x_kernel(count, listed, table_ref, source_ref, rows_ref, wave_ref, *refs):
@@ -448,13 +469,19 @@
         data_refs = [data_refs[0].at[k] for k in range(8)]
     half = pl.program_id(0)
     first_x, first_y = (lax.axis_index("sx") * 8, lax.axis_index("sy") * 16)
-    blocks = [k if count == 1 else lax.axis_index("sx") ^ k for k in range(8)]
+    blocks = range(8) if count == 1 else [lax.axis_index("sx") ^ k for k in SX_ORDER]
     w_high, w_low = split(jnp.concatenate([wave_ref[block] for block in blocks], 0))
     weights = jnp.concatenate([w_high, w_high, w_low], 0)
     lower = iota((8, 128), 1) < 64
     for f in range(16):
-        high, low = split(jnp.concatenate([ref[16 * half + f] for ref in data_refs], 0))
-        out = tn_dot(jnp.concatenate([high, low, high], 0), weights)
+        if f % 4 == 0:
+            data = []
+            for k in range(f, f + 4):
+                parts = [ref[16 * half + k] for ref in data_refs]
+                high, low = split(jnp.concatenate(parts, 0))
+                data.append(jnp.concatenate([high, low, high], 0))
+            group = tn_dot(jnp.concatenate(data, 1), weights)
+        out = group[128 * (f % 4) : 128 * (f % 4 + 1)]
         cosine = out[:, :128].reshape(2, 4, 2, 8, 128)
         sine = out[:, 128:].reshape(2, 4, 2, 8, 128)
         real = cosine[0] + sine[1]
@@ -498,6 +525,8 @@
 
 
 def x_call(which, data, gammas, rows, source_site, wave, corr):
+    if len(data) == 8:
+        data = [data[k] for k in SX_ORDER]
     in_specs = [
         pl.BlockSpec(memory_space=pltpu.SMEM),
         pl.BlockSpec(memory_space=pltpu.SMEM),
@@ -557,7 +586,7 @@
 
 def swap_sx(message):
     out = list(message)
-    for step in (1, 2, 3, 4, 5, 6, 7):
+    for step in SX_ORDER[1:]:
         out[step] = lax.ppermute(message[step], "sx", [(k, k ^ step) for k in range(8)])
     return out
 
@@ -570,17 +599,17 @@
     wave_z, wave_y, wave_x = (table_z(), table_y(), table_x())
     site, mom = (source_site, momenta.T)
     outer = (gamma_table.reshape(-1), gamma_table.reshape(16, 8), source_site, wave_x)
-    *first, fields = pair_call(0, 0, 3, False, None, forward_prop, backward_prop, wave_z, site, mom)
+    *first, fields = pair_call(0, 0, 3, 1, False, None, forward_prop, backward_prop, wave_z, site, mom)
     site, first = after((site, first))
     first = swap_sy(first)
-    *third, fields = pair_call(0, 3, 5, False, fields, forward_prop, backward_prop, wave_z, site, mom)
+    *third, fields = pair_call(0, 3, 5, 1, False, fields, forward_prop, backward_prop, wave_z, site, mom)
     site, third = after((site, third))
     first, third[1] = after((first, third[1]))
     third = swap_sy(third)
-    second = list(pair_call(1, 0, 8, True, fields, forward_prop, backward_prop, wave_z, site, mom))
+    second = list(pair_call(1, 0, 8, 2, True, fields, forward_prop, backward_prop, wave_z, site, mom))
     third, second[1] = after((third, second[1]))
     second = swap_sy(second)
-    sent = y_call(False, False, 0, [first, third], wave_y)
+    *sent, second[0] = y_call(False, False, 0, [first, third], wave_y, second[0])
     data = swap_sx_whole(sent)
     second[1:] = after(second[1:], sent[0])
     sent = y_call(True, True, 1, [second], wave_y)

time: 82.9 us -> 79.4 us (0.958)
  Pallas kernels: 36.6 us -> 34.4 us
  waiting for transfers between devices: 19.3 us -> 17.3 us
    ppermute x7, waiting for transfers between devices: 5.05 us -> 3.58 us  [swap_sx(): lax.ppermute(message[step], 'sx', [(k, k ^ step) for k in range(8)])]
    pallas_call x3, Pallas kernels: 26.1 us -> 24.7 us  [pair_call(): pl.pallas_call(functools.partial(pair_kernel, listed, bool(aliases)), gri...]
  transfers between devices with their start and end apart: 17 -> 17, of which waited for: 4 -> 5; matrix products, arithmetic and copies ran while one was open for 0% -> 0% of each run, Pallas kernels for 34% -> 33%
where the time goes in v4:
time: 79.4 us; the launch traced here: 78.2 us
  Pallas kernels  34.4 us (43%)
  starting transfers between devices  24.5 us (31%)
  waiting for transfers between devices  17.3 us (22%)
  local copies, waits for them, and re-layouts  1.29 us (2%)
    pallas_call x3, Pallas kernels, pair_call(): pl.pallas_call(functools.partial(pair_kernel, listed, bool(aliases)), gri...  24.7 us
    ppermute x9, waiting for transfers between devices, swap_sy(): lax.ppermute(message[step], 'sy', [(k, k ^ step) for k in range(4)])  13.7 us
    ppermute x9, starting transfers between devices, swap_sy(): lax.ppermute(message[step], 'sy', [(k, k ^ step) for k in range(4)])  12.4 us
    ppermute x7, starting transfers between devices, swap_sx(): lax.ppermute(message[step], 'sx', [(k, k ^ step) for k in range(8)])  7.86 us
    pallas_call x2, Pallas kernels, x_call(): pl.pallas_call(functools.partial(x_kernel, len(data), corr is not None),...  7.03 us
    all_to_all x1, starting transfers between devices, swap_sx_whole(): return [lax.all_to_all(message[0], 'sx', 0, 0, tiled=True)]  4.24 us
    ppermute x7, waiting for transfers between devices, swap_sx(): lax.ppermute(message[step], 'sx', [(k, k ^ step) for k in range(8)])  3.58 us
    pallas_call x2, Pallas kernels, y_call(): pl.pallas_call(functools.partial(y_kernel, len(parts), listed, apart, kep...  2.65 us
  transfers between devices with their start and end apart: 17, of which 5 were waited for; matrix products, arithmetic and copies ran while one was open for 0% of the time, Pallas kernels for 33%

profile of v4, /device:TPU:16, one launch (start us, length us, event | category | flops | bytes accessed | tf_op | source)
XLA Modules:
  0.0 78.2 jit_solution(7184298223573470760)
XLA Ops:
  0.6 5.6 %contract_and_z.3 = (f32[24,8,128]{2,1,0:T(8,128)}, f32[24,8,128]{2,1,0:T(8,128)}, f32[24,8,128]{2,1,0:T(8,128)}, f32[24,8,128]{2,1,0:T(8,128)}, f32[16,2,8,1024]{3,2,1,0:T(8,128)}) custom-call(s32[3]{0:T(128)} %source_ref.7, s32[3,32]{1,0:T(4,128)} %bitcast.2, bf16[2,2,12,12,8,1024]{5,4,3,2,1,0:T(8,128)(2,1)} %f_ref.5, ...), custom_call_target="tpu_custom_call" | custom-call | tf_op jit(solution)/shard_map/contract_and_z/pallas_call | solution.py:392
  6.3 1.6 %collective-permute-start = (f32[24,8,128]{2,1,0:T(8,128)}, f32[24,8,128]{2,1,0:T(8,128)S(1)}, u32[]{:S(2)}, u32[]{:S(2)}) collective-permute-start(f32[24,8,128]{2,1,0:T(8,128)} %get-tuple-element.55), channel_id=1, source_target_pairs={{0,1},{1,0},{2,3},{3,2},{4,5},{5,4},{6,7},{7,6},{8,9},{9,8},{10,11... | collective-permute-start | bytes 294920 | tf_op jit(solution)/shard_map/ppermute | solution.py:579
  7.9 0.3 collective-permute-start.1
  8.2 1.6 %collective-permute-start.2 = (f32[24,8,128]{2,1,0:T(8,128)}, f32[24,8,128]{2,1,0:T(8,128)S(1)}, u32[]{:S(2)}, u32[]{:S(2)}) collective-permute-start(f32[24,8,128]{2,1,0:T(8,128)} %get-tuple-element.57), channel_id=1, source_target_pairs={{0,3},{1,2},{2,1},{3,0},{4,7},{5,6},{6,5},{7,4},{8,11},{9,10},{10,... | collective-permute-start | bytes 294920 | tf_op jit(solution)/shard_map/ppermute | solution.py:579
  9.8 8.0 %contract_and_z.4 = (f32[40,8,128]{2,1,0:T(8,128)}, f32[40,8,128]{2,1,0:T(8,128)}, f32[40,8,128]{2,1,0:T(8,128)}, f32[40,8,128]{2,1,0:T(8,128)}, f32[16,2,8,1024]{3,2,1,0:T(8,128)}) custom-call(s32[3]{0:T(128)} %source_ref.7, s32[3,32]{1,0:T(4,128)} %bitcast.3, bf16[2,2,12,12,8,1024]{5,4,3,2,1,0:T(8,128)(2,1)} %f_ref.5, ...), custom_call_target="tpu_custom_call", output_to_operand_aliasing={{4}: (5, {})} | custom-call | tf_op jit(solution)/shard_map/contract_and_z/pallas_call | solution.py:392
  17.7 1.0 %collective-permute-start.4 = (f32[40,8,128]{2,1,0:T(8,128)}, f32[40,8,128]{2,1,0:T(8,128)S(1)}, u32[]{:S(2)}, u32[]{:S(2)}) collective-permute-start(f32[40,8,128]{2,1,0:T(8,128)} %get-tuple-element.71), channel_id=1, source_target_pairs={{0,2},{1,3},{2,0},{3,1},{4,6},{5,7},{6,4},{7,5},{8,10},{9,11},{10,... | collective-permute-start | bytes 491528 | tf_op jit(solution)/shard_map/ppermute | solution.py:579
  18.8 2.9 %collective-permute-start.5 = (f32[40,8,128]{2,1,0:T(8,128)}, f32[40,8,128]{2,1,0:T(8,128)S(1)}, u32[]{:S(2)}, u32[]{:S(2)}) collective-permute-start(f32[40,8,128]{2,1,0:T(8,128)} %get-tuple-element.72), channel_id=1, source_target_pairs={{0,3},{1,2},{2,1},{3,0},{4,7},{5,6},{6,5},{7,4},{8,11},{9,10},{10,... | collective-permute-start | bytes 491528 | tf_op jit(solution)/shard_map/ppermute | solution.py:579
  21.7 0.0 collective-permute-done.refs_1_
  21.7 0.0 collective-permute-done.1.refs_2_
  21.7 0.0 collective-permute-done.2.refs_3_
  21.7 0.5 collective-permute-start.3
  22.2 11.1 %contract_and_z.5 = (f32[66,8,128]{2,1,0:T(8,128)}, f32[66,8,128]{2,1,0:T(8,128)}, f32[66,8,128]{2,1,0:T(8,128)}, f32[66,8,128]{2,1,0:T(8,128)}) custom-call(s32[3]{0:T(128)} %source_ref.7, s32[3,32]{1,0:T(4,128)} %bitcast.4, bf16[2,2,12,12,8,1024]{5,4,3,2,1,0:T(8,128)(2,1)} %f_ref.5, bf16[2,2,12,12,8,1024]{5,4,3,2,1,0:T(8,128)(2,1)} %b_ref.5, ...), custom_call_target="tpu_custom_call" | custom-call | tf_op jit(solution)/shard_map/contract_and_z/pallas_call | solution.py:392
  33.3 1.0 %collective-permute-start.7 = (f32[66,8,128]{2,1,0:T(8,128)}, f32[66,8,128]{2,1,0:T(8,128)S(1)}, u32[]{:S(2)}, u32[]{:S(2)}) collective-permute-start(f32[66,8,128]{2,1,0:T(8,128)} %get-tuple-element.83), channel_id=1, source_target_pairs={{0,2},{1,3},{2,0},{3,1},{4,6},{5,7},{6,4},{7,5},{8,10},{9,11},{10,... | collective-permute-start | bytes 811016 | tf_op jit(solution)/shard_map/ppermute | solution.py:579
  34.3 2.0 %collective-permute-start.8 = (f32[66,8,128]{2,1,0:T(8,128)}, f32[66,8,128]{2,1,0:T(8,128)S(1)}, u32[]{:S(2)}, u32[]{:S(2)}) collective-permute-start(f32[66,8,128]{2,1,0:T(8,128)} %get-tuple-element.84), channel_id=1, source_target_pairs={{0,3},{1,2},{2,1},{3,0},{4,7},{5,6},{6,5},{7,4},{8,11},{9,10},{10,... | collective-permute-start | bytes 811016 | tf_op jit(solution)/shard_map/ppermute | solution.py:579
  36.4 0.0 collective-permute-done.4.refs_6_
  36.4 0.0 collective-permute-done.5.refs_7_
  36.4 0.0 collective-permute-done.3.refs_5_
  36.4 1.4 %collective-permute-start.6 = (f32[66,8,128]{2,1,0:T(8,128)}, f32[66,8,128]{2,1,0:T(8,128)S(1)}, u32[]{:S(2)}, u32[]{:S(2)}) collective-permute-start(f32[66,8,128]{2,1,0:T(8,128)} %get-tuple-element.82), channel_id=1, source_target_pairs={{0,1},{1,0},{2,3},{3,2},{4,5},{5,4},{6,7},{7,6},{8,9},{9,8},{10,11... | collective-permute-start | bytes 811016 | tf_op jit(solution)/shard_map/ppermute | solution.py:579
  37.8 0.0 copy-done
  37.8 0.0 copy-done.4
  37.8 0.9 %copy-done.1 = f32[66,8,128]{2,1,0:T(8,128)S(1)} copy-done((f32[66,8,128]{2,1,0:T(8,128)S(1)}, f32[66,8,128]{2,1,0:T(8,128)}, u32[]{:S(2)}) %copy-start.1) | copy-done | bytes 270360
  38.8 1.7 %along_y.2 = (f32[8,32,8,128]{3,2,1,0:T(8,128)}, f32[66,8,128]{2,1,0:T(8,128)S(1)}) custom-call(f32[24,8,128]{2,1,0:T(8,128)S(1)} %copy-done.4, f32[24,8,128]{2,1,0:T(8,128)S(1)} %collective-permute-done.refs_1_, f32[24,8,128]{2,1,0:T(8,128)S(1)} %collective-permute-done.1.refs_2_, f32[24,8,128]{2,1,0:T(8,128)S(1)} %collective-permute-done.2.refs_3_, ...), custom_call_target="tpu_custom_call" | custom-call | tf_op jit(solution)/shard_map/along_y/pallas_call | solution.py:449
  40.5 4.2 %all-to-all-start = ((f32[8,32,8,128]{3,2,1,0:T(8,128)}), f32[8,32,8,128]{3,2,1,0:T(8,128)}, u32[]{:S(2)}, u32[]{:S(2)}) async-start(f32[8,32,8,128]{3,2,1,0:T(8,128)} %get-tuple-element.85), calls=%async_computation | async-start | bytes 2097152 | tf_op jit(solution)/shard_map/all_to_all | solution.py:584
  44.7 7.0 %collective-permute-done.7.refs_2_ = f32[66,8,128]{2,1,0:T(8,128)S(1)} collective-permute-done((f32[66,8,128]{2,1,0:T(8,128)}, f32[66,8,128]{2,1,0:T(8,128)S(1)}, u32[]{:S(2)}, u32[]{:S(2)}) %collective-permute-start.7) | collective-permute-done | bytes 270368 | tf_op jit(solution)/shard_map/ppermute | solution.py:579
  51.8 6.6 %collective-permute-done.8.refs_3_ = f32[66,8,128]{2,1,0:T(8,128)S(1)} collective-permute-done((f32[66,8,128]{2,1,0:T(8,128)}, f32[66,8,128]{2,1,0:T(8,128)S(1)}, u32[]{:S(2)}, u32[]{:S(2)}) %collective-permute-start.8) | collective-permute-done | bytes 270368 | tf_op jit(solution)/shard_map/ppermute | solution.py:579
  58.4 0.0 collective-permute-done.6.refs_1_
  58.4 0.9 %along_y.3 = (f32[34,8,128]{2,1,0:T(8,128)S(1)}, f32[34,8,128]{2,1,0:T(8,128)S(1)}, f32[34,8,128]{2,1,0:T(8,128)S(1)}, f32[34,8,128]{2,1,0:T(8,128)S(1)}, f32[34...) custom-call(f32[66,8,128]{2,1,0:T(8,128)S(1)} %get-tuple-element.81.refs, ...), custom_call_target="tpu_custom_call" | custom-call | flops 9999999827968 | tf_op jit(solution)/shard_map/along_y/pallas_call | solution.py:449
  59.4 0.2 collective-permute-start.9
  59.6 1.5 %collective-permute-start.10 = (f32[34,8,128]{2,1,0:T(8,128)S(1)}, f32[34,8,128]{2,1,0:T(8,128)S(1)}, u32[]{:S(2)}, u32[]{:S(2)}) collective-permute-start(f32[34,8,128]{2,1,0:T(8,128)S(1)} %get-tuple-element.91), channel_id=1, source_target_pairs={{0,16},{4,20},{8,24},{12,28},{16,0},{20,4},{24,8},{28,12},{1,17},{... | collective-permute-start | bytes 417800 | tf_op jit(solution)/shard_map/ppermute | solution.py:590
  61.1 1.4 %collective-permute-start.11 = (f32[34,8,128]{2,1,0:T(8,128)S(1)}, f32[34,8,128]{2,1,0:T(8,128)S(1)}, u32[]{:S(2)}, u32[]{:S(2)}) collective-permute-start(f32[34,8,128]{2,1,0:T(8,128)S(1)} %get-tuple-element.92), channel_id=1, source_target_pairs={{0,8},{4,12},{8,0},{12,4},{16,24},{20,28},{24,16},{28,20},{1,9},{5... | collective-permute-start | bytes 417800 | tf_op jit(solution)/shard_map/ppermute | solution.py:590
  62.5 0.6 collective-permute-start.12
  63.1 0.6 collective-permute-start.13
  63.7 0.0 collective-permute-done.9.refs_1_
  63.7 2.0 %collective-permute-start.14 = (f32[34,8,128]{2,1,0:T(8,128)S(1)}, f32[34,8,128]{2,1,0:T(8,128)S(1)}, u32[]{:S(2)}, u32[]{:S(2)}) collective-permute-start(f32[34,8,128]{2,1,0:T(8,128)S(1)} %get-tuple-element.95), channel_id=1, source_target_pairs={{0,12},{4,8},{8,4},{12,0},{16,28},{20,24},{24,20},{28,16},{1,13},{... | collective-permute-start | bytes 417800 | tf_op jit(solution)/shard_map/ppermute | solution.py:590
  65.7 0.0 collective-permute-done.10.refs_2_
  65.7 1.5 %collective-permute-start.15 = (f32[34,8,128]{2,1,0:T(8,128)S(1)}, f32[34,8,128]{2,1,0:T(8,128)S(1)}, u32[]{:S(2)}, u32[]{:S(2)}) collective-permute-start(f32[34,8,128]{2,1,0:T(8,128)S(1)} %get-tuple-element.96), channel_id=1, source_target_pairs={{0,28},{4,24},{8,20},{12,16},{16,12},{20,8},{24,4},{28,0},{1,29},{... | collective-permute-start | bytes 417800 | tf_op jit(solution)/shard_map/ppermute | solution.py:590
  67.2 0.0 copy-done.6
  67.2 0.1 copy.15
  67.4 0.1 copy.17.rows_ref
  67.4 0.1 reshape.10.table_ref
  67.6 0.0 all-to-all-done.refs_0_
  67.6 3.7 %along_x.2.refs_8_ = f32[16,2,2,8,1024]{4,3,2,1,0:T(8,128)} custom-call(s32[128]{0:T(128)S(1)} %reshape.10.table_ref, s32[3]{0:T(128)S(1)} %copy-done.5, s32[16,8]{1,0:T(8,128)S(1)} %copy.17.rows_ref, f32[8,8,256]{2,1,0:T(8,128)S(1)} %copy-done.2, f32[8,32,8,128]{3,2,1,0:T(8,128)} %all-to-all-done.refs_0_), custom_call_target="tpu_custom_call" | custom-call | tf_op jit(solution)/shard_map/along_x/pallas_call | solution.py:546
  71.3 0.0 collective-permute-done.11.refs_3_
  71.4 0.0 collective-permute-done.12.refs_4_
  71.4 0.6 collective-permute-done.13.refs_5_
  71.9 0.6 collective-permute-done.14.refs_6_
  72.6 2.4 %collective-permute-done.15.refs_7_ = f32[34,8,128]{2,1,0:T(8,128)S(1)} collective-permute-done((f32[34,8,128]{2,1,0:T(8,128)S(1)}, f32[34,8,128]{2,1,0:T(8,128)S(1)}, u32[]{:S(2)}, u32[]{:S(2)}) %collective-permute-start.15) | collective-permute-done | bytes 139296 | tf_op jit(solution)/shard_map/ppermute | solution.py:590
  74.9 3.3 %along_x.3 = (f32[16,2,2,8,1024]{4,3,2,1,0:T(8,128)}, f32[2,16,2,32]{3,2,1,0:T(2,128)}) custom-call(s32[128]{0:T(128)S(1)} %reshape.10.table_ref, s32[3]{0:T(128)S(1)} %copy-done.5, s32[16,8]{1,0:T(8,128)S(1)} %copy.17.rows_ref, f32[8,8,256]{2,1,0:T(8,128)S(1)} %copy-done.2, ...), custom_call_target="tpu_custom_call", output_to_operand_aliasing={{0}: (12, {})} | custom-call | tf_op jit(solution)/shard_map/along_x/pallas_call | solution.py:546
  (10 shorter events, 0.0 us)
Async XLA Ops:
  6.3 15.4 %collective-permute-start = (f32[24,8,128]{2,1,0:T(8,128)}, f32[24,8,128]{2,1,0:T(8,128)S(1)}, u32[]{:S(2)}, u32[]{:S(2)}) collective-permute-start(f32[24,8,128]{2,1,0:T(8,128)} %get-tuple-element.55), channel_id=1, source_target_pairs={{0,1},{1,0},{2,3},{3,2},{4,5},{5,4},{6,7},{7,6},{8,9},{9,8},{10,11... | collective-permute-start | bytes 294920 | tf_op jit(solution)/shard_map/ppermute | solution.py:579
  7.9 13.8 %collective-permute-start.1 = (f32[24,8,128]{2,1,0:T(8,128)}, f32[24,8,128]{2,1,0:T(8,128)S(1)}, u32[]{:S(2)}, u32[]{:S(2)}) collective-permute-start(f32[24,8,128]{2,1,0:T(8,128)} %get-tuple-element.56), channel_id=1, source_target_pairs={{0,2},{1,3},{2,0},{3,1},{4,6},{5,7},{6,4},{7,5},{8,10},{9,11},{10,... | collective-permute-start | bytes 294920 | tf_op jit(solution)/shard_map/ppermute | solution.py:579
  8.2 13.5 %collective-permute-start.2 = (f32[24,8,128]{2,1,0:T(8,128)}, f32[24,8,128]{2,1,0:T(8,128)S(1)}, u32[]{:S(2)}, u32[]{:S(2)}) collective-permute-start(f32[24,8,128]{2,1,0:T(8,128)} %get-tuple-element.57), channel_id=1, source_target_pairs={{0,3},{1,2},{2,1},{3,0},{4,7},{5,6},{6,5},{7,4},{8,11},{9,10},{10,... | collective-permute-start | bytes 294920 | tf_op jit(solution)/shard_map/ppermute | solution.py:579
  17.7 18.6 %collective-permute-start.4 = (f32[40,8,128]{2,1,0:T(8,128)}, f32[40,8,128]{2,1,0:T(8,128)S(1)}, u32[]{:S(2)}, u32[]{:S(2)}) collective-permute-start(f32[40,8,128]{2,1,0:T(8,128)} %get-tuple-element.71), channel_id=1, source_target_pairs={{0,2},{1,3},{2,0},{3,1},{4,6},{5,7},{6,4},{7,5},{8,10},{9,11},{10,... | collective-permute-start | bytes 491528 | tf_op jit(solution)/shard_map/ppermute | solution.py:579
  18.8 17.6 %collective-permute-start.5 = (f32[40,8,128]{2,1,0:T(8,128)}, f32[40,8,128]{2,1,0:T(8,128)S(1)}, u32[]{:S(2)}, u32[]{:S(2)}) collective-permute-start(f32[40,8,128]{2,1,0:T(8,128)} %get-tuple-element.72), channel_id=1, source_target_pairs={{0,3},{1,2},{2,1},{3,0},{4,7},{5,6},{6,5},{7,4},{8,11},{9,10},{10,... | collective-permute-start | bytes 491528 | tf_op jit(solution)/shard_map/ppermute | solution.py:579
  21.7 14.7 %collective-permute-start.3 = (f32[40,8,128]{2,1,0:T(8,128)}, f32[40,8,128]{2,1,0:T(8,128)S(1)}, u32[]{:S(2)}, u32[]{:S(2)}) collective-permute-start(f32[40,8,128]{2,1,0:T(8,128)} %get-tuple-element.70), channel_id=1, source_target_pairs={{0,1},{1,0},{2,3},{3,2},{4,5},{5,4},{6,7},{7,6},{8,9},{9,8},{10,11... | collective-permute-start | bytes 491528 | tf_op jit(solution)/shard_map/ppermute | solution.py:579
  22.2 15.6 %copy-start = (f32[4,256,256]{2,1,0:T(8,128)S(1)}, f32[4,256,256]{2,1,0:T(8,128)}, u32[]{:S(2)}) copy-start(f32[4,256,256]{2,1,0:T(8,128)} %constant.7.clone.refs_8_.refs_4_) | copy-start | bytes 3145732
  22.2 15.6 %copy-start.3 = (f32[40,8,128]{2,1,0:T(8,128)S(1)}, f32[40,8,128]{2,1,0:T(8,128)}, u32[]{:S(2)}) copy-start(f32[40,8,128]{2,1,0:T(8,128)} %get-tuple-element.76.refs_4_) | copy-start | bytes 491524
  22.2 15.6 %copy-start.4 = (f32[24,8,128]{2,1,0:T(8,128)S(1)}, f32[24,8,128]{2,1,0:T(8,128)}, u32[]{:S(2)}) copy-start(f32[24,8,128]{2,1,0:T(8,128)} %get-tuple-element.65.refs_0_) | copy-start | bytes 294916
  33.3 18.4 %collective-permute-start.7 = (f32[66,8,128]{2,1,0:T(8,128)}, f32[66,8,128]{2,1,0:T(8,128)S(1)}, u32[]{:S(2)}, u32[]{:S(2)}) collective-permute-start(f32[66,8,128]{2,1,0:T(8,128)} %get-tuple-element.83), channel_id=1, source_target_pairs={{0,2},{1,3},{2,0},{3,1},{4,6},{5,7},{6,4},{7,5},{8,10},{9,11},{10,... | collective-permute-start | bytes 811016 | tf_op jit(solution)/shard_map/ppermute | solution.py:579
  34.3 24.1 %collective-permute-start.8 = (f32[66,8,128]{2,1,0:T(8,128)}, f32[66,8,128]{2,1,0:T(8,128)S(1)}, u32[]{:S(2)}, u32[]{:S(2)}) collective-permute-start(f32[66,8,128]{2,1,0:T(8,128)} %get-tuple-element.84), channel_id=1, source_target_pairs={{0,3},{1,2},{2,1},{3,0},{4,7},{5,6},{6,5},{7,4},{8,11},{9,10},{10,... | collective-permute-start | bytes 811016 | tf_op jit(solution)/shard_map/ppermute | solution.py:579
  36.4 22.0 %collective-permute-start.6 = (f32[66,8,128]{2,1,0:T(8,128)}, f32[66,8,128]{2,1,0:T(8,128)S(1)}, u32[]{:S(2)}, u32[]{:S(2)}) collective-permute-start(f32[66,8,128]{2,1,0:T(8,128)} %get-tuple-element.82), channel_id=1, source_target_pairs={{0,1},{1,0},{2,3},{3,2},{4,5},{5,4},{6,7},{7,6},{8,9},{9,8},{10,11... | collective-permute-start | bytes 811016 | tf_op jit(solution)/shard_map/ppermute | solution.py:579
  37.8 1.0 %copy-start.1 = (f32[66,8,128]{2,1,0:T(8,128)S(1)}, f32[66,8,128]{2,1,0:T(8,128)}, u32[]{:S(2)}) copy-start(f32[66,8,128]{2,1,0:T(8,128)} %get-tuple-element.80.refs_9_) | copy-start | bytes 811012
  40.5 27.1 %all-to-all-start = ((f32[8,32,8,128]{3,2,1,0:T(8,128)}), f32[8,32,8,128]{3,2,1,0:T(8,128)}, u32[]{:S(2)}, u32[]{:S(2)}) async-start(f32[8,32,8,128]{3,2,1,0:T(8,128)} %get-tuple-element.85), calls=%async_computation | async-start | bytes 2097152 | tf_op jit(solution)/shard_map/all_to_all | solution.py:584
  58.4 8.8 %copy-start.6 = (s32[16,4,2]{0,2,1:T(2,128)S(1)}, s32[16,4,2]{0,2,1:T(2,128)}, u32[]{:S(2)}) copy-start(s32[16,4,2]{0,2,1:T(2,128)} %param.10) | copy-start | bytes 1540
  58.4 9.2 %copy-start.2 = (f32[8,8,256]{2,1,0:T(8,128)S(1)}, f32[8,8,256]{2,1,0:T(8,128)}, u32[]{:S(2)}) copy-start(f32[8,8,256]{2,1,0:T(8,128)} %constant.8.clone.wave_ref) | copy-start | bytes 196612
  58.4 9.2 %copy-start.5 = (s32[3]{0:T(128)S(1)}, s32[3]{0:T(128)}, u32[]{:S(2)}) copy-start(s32[3]{0:T(128)} %source_ref.7) | copy-start | bytes 40
  59.4 4.3 %collective-permute-start.9 = (f32[34,8,128]{2,1,0:T(8,128)S(1)}, f32[34,8,128]{2,1,0:T(8,128)S(1)}, u32[]{:S(2)}, u32[]{:S(2)}) collective-permute-start(f32[34,8,128]{2,1,0:T(8,128)S(1)} %get-tuple-element.90), channel_id=1, source_target_pairs={{0,4},{4,0},{8,12},{12,8},{16,20},{20,16},{24,28},{28,24},{1,5},{5... | collective-permute-start | bytes 417800 | tf_op jit(solution)/shard_map/ppermute | solution.py:590
  59.6 6.2 %collective-permute-start.10 = (f32[34,8,128]{2,1,0:T(8,128)S(1)}, f32[34,8,128]{2,1,0:T(8,128)S(1)}, u32[]{:S(2)}, u32[]{:S(2)}) collective-permute-start(f32[34,8,128]{2,1,0:T(8,128)S(1)} %get-tuple-element.91), channel_id=1, source_target_pairs={{0,16},{4,20},{8,24},{12,28},{16,0},{20,4},{24,8},{28,12},{1,17},{... | collective-permute-start | bytes 417800 | tf_op jit(solution)/shard_map/ppermute | solution.py:590
  61.1 10.3 %collective-permute-start.11 = (f32[34,8,128]{2,1,0:T(8,128)S(1)}, f32[34,8,128]{2,1,0:T(8,128)S(1)}, u32[]{:S(2)}, u32[]{:S(2)}) collective-permute-start(f32[34,8,128]{2,1,0:T(8,128)S(1)} %get-tuple-element.92), channel_id=1, source_target_pairs={{0,8},{4,12},{8,0},{12,4},{16,24},{20,28},{24,16},{28,20},{1,9},{5... | collective-permute-start | bytes 417800 | tf_op jit(solution)/shard_map/ppermute | solution.py:590
  62.5 8.8 %collective-permute-start.12 = (f32[34,8,128]{2,1,0:T(8,128)S(1)}, f32[34,8,128]{2,1,0:T(8,128)S(1)}, u32[]{:S(2)}, u32[]{:S(2)}) collective-permute-start(f32[34,8,128]{2,1,0:T(8,128)S(1)} %get-tuple-element.93), channel_id=1, source_target_pairs={{0,24},{4,28},{8,16},{12,20},{16,8},{20,12},{24,0},{28,4},{1,25},{... | collective-permute-start | bytes 417800 | tf_op jit(solution)/shard_map/ppermute | solution.py:590
  63.1 8.9 %collective-permute-start.13 = (f32[34,8,128]{2,1,0:T(8,128)S(1)}, f32[34,8,128]{2,1,0:T(8,128)S(1)}, u32[]{:S(2)}, u32[]{:S(2)}) collective-permute-start(f32[34,8,128]{2,1,0:T(8,128)S(1)} %get-tuple-element.94), channel_id=1, source_target_pairs={{0,20},{4,16},{8,28},{12,24},{16,4},{20,0},{24,12},{28,8},{1,21},{... | collective-permute-start | bytes 417800 | tf_op jit(solution)/shard_map/ppermute | solution.py:590
  63.7 8.8 %collective-permute-start.14 = (f32[34,8,128]{2,1,0:T(8,128)S(1)}, f32[34,8,128]{2,1,0:T(8,128)S(1)}, u32[]{:S(2)}, u32[]{:S(2)}) collective-permute-start(f32[34,8,128]{2,1,0:T(8,128)S(1)} %get-tuple-element.95), channel_id=1, source_target_pairs={{0,12},{4,8},{8,4},{12,0},{16,28},{20,24},{24,20},{28,16},{1,13},{... | collective-permute-start | bytes 417800 | tf_op jit(solution)/shard_map/ppermute | solution.py:590
  65.7 9.2 %collective-permute-start.15 = (f32[34,8,128]{2,1,0:T(8,128)S(1)}, f32[34,8,128]{2,1,0:T(8,128)S(1)}, u32[]{:S(2)}, u32[]{:S(2)}) collective-permute-start(f32[34,8,128]{2,1,0:T(8,128)S(1)} %get-tuple-element.96), channel_id=1, source_target_pairs={{0,28},{4,24},{8,20},{12,16},{16,12},{20,8},{24,4},{28,0},{1,29},{... | collective-permute-start | bytes 417800 | tf_op jit(solution)/shard_map/ppermute | solution.py:590

commit v5 on v4

--- a/solution.py
+++ b/solution.py
@@ -139,7 +139,7 @@
 F32 = jnp.float32
 BF16 = jnp.bfloat16
 MIB = 2**20
-SX_ORDER = (0, 1, 4, 2, 6, 5, 3, 7)
+SX_ORDER = (0, 4, 2, 6, 1, 5, 3, 7)
 
 
 def split(values):

time: 79.4 us -> 79.4 us (level)
  waiting for transfers between devices: 17.3 us -> 19.3 us
  starting transfers between devices: 24.5 us -> 22.7 us
    ppermute x7, waiting for transfers between devices: 3.58 us -> 5.59 us  [swap_sx(): lax.ppermute(message[step], 'sx', [(k, k ^ step) for k in range(8)])]
    ppermute x7, starting transfers between devices: 7.86 us -> 6.03 us  [swap_sx(): lax.ppermute(message[step], 'sx', [(k, k ^ step) for k in range(8)])]
  transfers between devices with their start and end apart: 17 -> 17, of which waited for: 5 -> 6; matrix products, arithmetic and copies ran while one was open for 0% -> 0% of each run, Pallas kernels for 33% -> 32%
where the time goes in v5:
time: 79.4 us; the launch traced here: 78.4 us
  Pallas kernels  34.4 us (43%)
  starting transfers between devices  22.7 us (29%)
  waiting for transfers between devices  19.3 us (24%)
  local copies, waits for them, and re-layouts  1.29 us (2%)
    pallas_call x3, Pallas kernels, pair_call(): pl.pallas_call(functools.partial(pair_kernel, listed, bool(aliases)), gri...  24.7 us
    ppermute x9, waiting for transfers between devices, swap_sy(): lax.ppermute(message[step], 'sy', [(k, k ^ step) for k in range(4)])  13.7 us
    ppermute x9, starting transfers between devices, swap_sy(): lax.ppermute(message[step], 'sy', [(k, k ^ step) for k in range(4)])  12.4 us
    pallas_call x2, Pallas kernels, x_call(): pl.pallas_call(functools.partial(x_kernel, len(data), corr is not None),...  7.04 us
    ppermute x7, starting transfers between devices, swap_sx(): lax.ppermute(message[step], 'sx', [(k, k ^ step) for k in range(8)])  6.03 us
    ppermute x7, waiting for transfers between devices, swap_sx(): lax.ppermute(message[step], 'sx', [(k, k ^ step) for k in range(8)])  5.59 us
    all_to_all x1, starting transfers between devices, swap_sx_whole(): return [lax.all_to_all(message[0], 'sx', 0, 0, tiled=True)]  4.24 us
    pallas_call x2, Pallas kernels, y_call(): pl.pallas_call(functools.partial(y_kernel, len(parts), listed, apart, kep...  2.65 us
  transfers between devices with their start and end apart: 17, of which 6 were waited for; matrix products, arithmetic and copies ran while one was open for 0% of the time, Pallas kernels for 32%

profile of v5, /device:TPU:16, one launch (start us, length us, event | category | flops | bytes accessed | tf_op | source)
XLA Modules:
  0.0 78.4 jit_solution(12281826578013881459)
XLA Ops:
  0.6 5.6 %contract_and_z.3 = (f32[24,8,128]{2,1,0:T(8,128)}, f32[24,8,128]{2,1,0:T(8,128)}, f32[24,8,128]{2,1,0:T(8,128)}, f32[24,8,128]{2,1,0:T(8,128)}, f32[16,2,8,1024]{3,2,1,0:T(8,128)}) custom-call(s32[3]{0:T(128)} %source_ref.7, s32[3,32]{1,0:T(4,128)} %bitcast.2, bf16[2,2,12,12,8,1024]{5,4,3,2,1,0:T(8,128)(2,1)} %f_ref.5, ...), custom_call_target="tpu_custom_call" | custom-call | tf_op jit(solution)/shard_map/contract_and_z/pallas_call | solution.py:392
  6.3 1.6 %collective-permute-start = (f32[24,8,128]{2,1,0:T(8,128)}, f32[24,8,128]{2,1,0:T(8,128)S(1)}, u32[]{:S(2)}, u32[]{:S(2)}) collective-permute-start(f32[24,8,128]{2,1,0:T(8,128)} %get-tuple-element.55), channel_id=1, source_target_pairs={{0,1},{1,0},{2,3},{3,2},{4,5},{5,4},{6,7},{7,6},{8,9},{9,8},{10,11... | collective-permute-start | bytes 294920 | tf_op jit(solution)/shard_map/ppermute | solution.py:579
  7.9 0.3 collective-permute-start.1
  8.2 1.6 %collective-permute-start.2 = (f32[24,8,128]{2,1,0:T(8,128)}, f32[24,8,128]{2,1,0:T(8,128)S(1)}, u32[]{:S(2)}, u32[]{:S(2)}) collective-permute-start(f32[24,8,128]{2,1,0:T(8,128)} %get-tuple-element.57), channel_id=1, source_target_pairs={{0,3},{1,2},{2,1},{3,0},{4,7},{5,6},{6,5},{7,4},{8,11},{9,10},{10,... | collective-permute-start | bytes 294920 | tf_op jit(solution)/shard_map/ppermute | solution.py:579
  9.8 8.0 %contract_and_z.4 = (f32[40,8,128]{2,1,0:T(8,128)}, f32[40,8,128]{2,1,0:T(8,128)}, f32[40,8,128]{2,1,0:T(8,128)}, f32[40,8,128]{2,1,0:T(8,128)}, f32[16,2,8,1024]{3,2,1,0:T(8,128)}) custom-call(s32[3]{0:T(128)} %source_ref.7, s32[3,32]{1,0:T(4,128)} %bitcast.3, bf16[2,2,12,12,8,1024]{5,4,3,2,1,0:T(8,128)(2,1)} %f_ref.5, ...), custom_call_target="tpu_custom_call", output_to_operand_aliasing={{4}: (5, {})} | custom-call | tf_op jit(solution)/shard_map/contract_and_z/pallas_call | solution.py:392
  17.7 1.0 %collective-permute-start.4 = (f32[40,8,128]{2,1,0:T(8,128)}, f32[40,8,128]{2,1,0:T(8,128)S(1)}, u32[]{:S(2)}, u32[]{:S(2)}) collective-permute-start(f32[40,8,128]{2,1,0:T(8,128)} %get-tuple-element.71), channel_id=1, source_target_pairs={{0,2},{1,3},{2,0},{3,1},{4,6},{5,7},{6,4},{7,5},{8,10},{9,11},{10,... | collective-permute-start | bytes 491528 | tf_op jit(solution)/shard_map/ppermute | solution.py:579
  18.8 2.9 %collective-permute-start.5 = (f32[40,8,128]{2,1,0:T(8,128)}, f32[40,8,128]{2,1,0:T(8,128)S(1)}, u32[]{:S(2)}, u32[]{:S(2)}) collective-permute-start(f32[40,8,128]{2,1,0:T(8,128)} %get-tuple-element.72), channel_id=1, source_target_pairs={{0,3},{1,2},{2,1},{3,0},{4,7},{5,6},{6,5},{7,4},{8,11},{9,10},{10,... | collective-permute-start | bytes 491528 | tf_op jit(solution)/shard_map/ppermute | solution.py:579
  21.7 0.0 collective-permute-done.refs_1_
  21.7 0.0 collective-permute-done.1.refs_2_
  21.7 0.0 collective-permute-done.2.refs_3_
  21.7 0.5 collective-permute-start.3
  22.2 11.1 %contract_and_z.5 = (f32[66,8,128]{2,1,0:T(8,128)}, f32[66,8,128]{2,1,0:T(8,128)}, f32[66,8,128]{2,1,0:T(8,128)}, f32[66,8,128]{2,1,0:T(8,128)}) custom-call(s32[3]{0:T(128)} %source_ref.7, s32[3,32]{1,0:T(4,128)} %bitcast.4, bf16[2,2,12,12,8,1024]{5,4,3,2,1,0:T(8,128)(2,1)} %f_ref.5, bf16[2,2,12,12,8,1024]{5,4,3,2,1,0:T(8,128)(2,1)} %b_ref.5, ...), custom_call_target="tpu_custom_call" | custom-call | tf_op jit(solution)/shard_map/contract_and_z/pallas_call | solution.py:392
  33.3 1.0 %collective-permute-start.7 = (f32[66,8,128]{2,1,0:T(8,128)}, f32[66,8,128]{2,1,0:T(8,128)S(1)}, u32[]{:S(2)}, u32[]{:S(2)}) collective-permute-start(f32[66,8,128]{2,1,0:T(8,128)} %get-tuple-element.83), channel_id=1, source_target_pairs={{0,2},{1,3},{2,0},{3,1},{4,6},{5,7},{6,4},{7,5},{8,10},{9,11},{10,... | collective-permute-start | bytes 811016 | tf_op jit(solution)/shard_map/ppermute | solution.py:579
  34.3 2.0 %collective-permute-start.8 = (f32[66,8,128]{2,1,0:T(8,128)}, f32[66,8,128]{2,1,0:T(8,128)S(1)}, u32[]{:S(2)}, u32[]{:S(2)}) collective-permute-start(f32[66,8,128]{2,1,0:T(8,128)} %get-tuple-element.84), channel_id=1, source_target_pairs={{0,3},{1,2},{2,1},{3,0},{4,7},{5,6},{6,5},{7,4},{8,11},{9,10},{10,... | collective-permute-start | bytes 811016 | tf_op jit(solution)/shard_map/ppermute | solution.py:579
  36.4 0.0 collective-permute-done.4.refs_6_
  36.4 0.0 collective-permute-done.5.refs_7_
  36.4 0.0 collective-permute-done.3.refs_5_
  36.4 1.4 %collective-permute-start.6 = (f32[66,8,128]{2,1,0:T(8,128)}, f32[66,8,128]{2,1,0:T(8,128)S(1)}, u32[]{:S(2)}, u32[]{:S(2)}) collective-permute-start(f32[66,8,128]{2,1,0:T(8,128)} %get-tuple-element.82), channel_id=1, source_target_pairs={{0,1},{1,0},{2,3},{3,2},{4,5},{5,4},{6,7},{7,6},{8,9},{9,8},{10,11... | collective-permute-start | bytes 811016 | tf_op jit(solution)/shard_map/ppermute | solution.py:579
  37.8 0.0 copy-done
  37.8 0.0 copy-done.3
  37.8 0.0 copy-done.4
  37.8 0.9 %copy-done.1 = f32[66,8,128]{2,1,0:T(8,128)S(1)} copy-done((f32[66,8,128]{2,1,0:T(8,128)S(1)}, f32[66,8,128]{2,1,0:T(8,128)}, u32[]{:S(2)}) %copy-start.1) | copy-done | bytes 270360
  38.8 1.7 %along_y.2 = (f32[8,32,8,128]{3,2,1,0:T(8,128)}, f32[66,8,128]{2,1,0:T(8,128)S(1)}) custom-call(f32[24,8,128]{2,1,0:T(8,128)S(1)} %copy-done.4, f32[24,8,128]{2,1,0:T(8,128)S(1)} %collective-permute-done.refs_1_, f32[24,8,128]{2,1,0:T(8,128)S(1)} %collective-permute-done.1.refs_2_, f32[24,8,128]{2,1,0:T(8,128)S(1)} %collective-permute-done.2.refs_3_, ...), custom_call_target="tpu_custom_call" | custom-call | tf_op jit(solution)/shard_map/along_y/pallas_call | solution.py:449
  40.5 4.2 %all-to-all-start = ((f32[8,32,8,128]{3,2,1,0:T(8,128)}), f32[8,32,8,128]{3,2,1,0:T(8,128)}, u32[]{:S(2)}, u32[]{:S(2)}) async-start(f32[8,32,8,128]{3,2,1,0:T(8,128)} %get-tuple-element.85), calls=%async_computation | async-start | bytes 2097152 | tf_op jit(solution)/shard_map/all_to_all | solution.py:584
  44.7 7.0 %collective-permute-done.7.refs_2_ = f32[66,8,128]{2,1,0:T(8,128)S(1)} collective-permute-done((f32[66,8,128]{2,1,0:T(8,128)}, f32[66,8,128]{2,1,0:T(8,128)S(1)}, u32[]{:S(2)}, u32[]{:S(2)}) %collective-permute-start.7) | collective-permute-done | bytes 270368 | tf_op jit(solution)/shard_map/ppermute | solution.py:579
  51.8 6.6 %collective-permute-done.8.refs_3_ = f32[66,8,128]{2,1,0:T(8,128)S(1)} collective-permute-done((f32[66,8,128]{2,1,0:T(8,128)}, f32[66,8,128]{2,1,0:T(8,128)S(1)}, u32[]{:S(2)}, u32[]{:S(2)}) %collective-permute-start.8) | collective-permute-done | bytes 270368 | tf_op jit(solution)/shard_map/ppermute | solution.py:579
  58.4 0.0 collective-permute-done.6.refs_1_
  58.4 0.9 %along_y.3 = (f32[34,8,128]{2,1,0:T(8,128)S(1)}, f32[34,8,128]{2,1,0:T(8,128)S(1)}, f32[34,8,128]{2,1,0:T(8,128)S(1)}, f32[34,8,128]{2,1,0:T(8,128)S(1)}, f32[34...) custom-call(f32[66,8,128]{2,1,0:T(8,128)S(1)} %get-tuple-element.81.refs, ...), custom_call_target="tpu_custom_call" | custom-call | flops 9999999827968 | tf_op jit(solution)/shard_map/along_y/pallas_call | solution.py:449
  59.4 1.6 %collective-permute-start.9 = (f32[34,8,128]{2,1,0:T(8,128)S(1)}, f32[34,8,128]{2,1,0:T(8,128)S(1)}, u32[]{:S(2)}, u32[]{:S(2)}) collective-permute-start(f32[34,8,128]{2,1,0:T(8,128)S(1)} %get-tuple-element.90), channel_id=1, source_target_pairs={{0,16},{4,20},{8,24},{12,28},{16,0},{20,4},{24,8},{28,12},{1,17},{... | collective-permute-start | bytes 417800 | tf_op jit(solution)/shard_map/ppermute | solution.py:590
  61.0 1.5 %collective-permute-start.10 = (f32[34,8,128]{2,1,0:T(8,128)S(1)}, f32[34,8,128]{2,1,0:T(8,128)S(1)}, u32[]{:S(2)}, u32[]{:S(2)}) collective-permute-start(f32[34,8,128]{2,1,0:T(8,128)S(1)} %get-tuple-element.91), channel_id=1, source_target_pairs={{0,8},{4,12},{8,0},{12,4},{16,24},{20,28},{24,16},{28,20},{1,9},{5... | collective-permute-start | bytes 417800 | tf_op jit(solution)/shard_map/ppermute | solution.py:590
  62.4 0.5 collective-permute-start.11
  62.9 0.0 collective-permute-start.12
  62.9 1.6 %collective-permute-start.13 = (f32[34,8,128]{2,1,0:T(8,128)S(1)}, f32[34,8,128]{2,1,0:T(8,128)S(1)}, u32[]{:S(2)}, u32[]{:S(2)}) collective-permute-start(f32[34,8,128]{2,1,0:T(8,128)S(1)} %get-tuple-element.94), channel_id=1, source_target_pairs={{0,20},{4,16},{8,28},{12,24},{16,4},{20,0},{24,12},{28,8},{1,21},{... | collective-permute-start | bytes 417800 | tf_op jit(solution)/shard_map/ppermute | solution.py:590
  64.6 0.6 collective-permute-done.9.refs_1_
  65.1 0.5 collective-permute-start.14
  65.7 1.9 %collective-permute-done.10.refs_2_ = f32[34,8,128]{2,1,0:T(8,128)S(1)} collective-permute-done((f32[34,8,128]{2,1,0:T(8,128)S(1)}, f32[34,8,128]{2,1,0:T(8,128)S(1)}, u32[]{:S(2)}, u32[]{:S(2)}) %collective-permute-start.10) | collective-permute-done | bytes 139296 | tf_op jit(solution)/shard_map/ppermute | solution.py:590
  67.5 0.3 collective-permute-start.15
  67.8 0.1 copy.15
  68.0 0.1 copy.17.rows_ref
  68.0 0.1 reshape.10.table_ref
  68.2 0.0 all-to-all-done.refs_0_
  68.2 3.7 %along_x.2.refs_8_ = f32[16,2,2,8,1024]{4,3,2,1,0:T(8,128)} custom-call(s32[128]{0:T(128)S(1)} %reshape.10.table_ref, s32[3]{0:T(128)S(1)} %copy-done.5, s32[16,8]{1,0:T(8,128)S(1)} %copy.17.rows_ref, f32[8,8,256]{2,1,0:T(8,128)S(1)} %copy-done.2, f32[8,32,8,128]{3,2,1,0:T(8,128)} %all-to-all-done.refs_0_), custom_call_target="tpu_custom_call" | custom-call | tf_op jit(solution)/shard_map/along_x/pallas_call | solution.py:546
  71.9 0.0 collective-permute-done.11.refs_3_
  72.0 0.0 collective-permute-done.12.refs_4_
  72.0 0.0 collective-permute-done.13.refs_5_
  72.0 0.3 collective-permute-done.14.refs_6_
  72.3 2.8 %collective-permute-done.15.refs_7_ = f32[34,8,128]{2,1,0:T(8,128)S(1)} collective-permute-done((f32[34,8,128]{2,1,0:T(8,128)S(1)}, f32[34,8,128]{2,1,0:T(8,128)S(1)}, u32[]{:S(2)}, u32[]{:S(2)}) %collective-permute-start.15) | collective-permute-done | bytes 139296 | tf_op jit(solution)/shard_map/ppermute | solution.py:590
  75.1 3.3 %along_x.3 = (f32[16,2,2,8,1024]{4,3,2,1,0:T(8,128)}, f32[2,16,2,32]{3,2,1,0:T(2,128)}) custom-call(s32[128]{0:T(128)S(1)} %reshape.10.table_ref, s32[3]{0:T(128)S(1)} %copy-done.5, s32[16,8]{1,0:T(8,128)S(1)} %copy.17.rows_ref, f32[8,8,256]{2,1,0:T(8,128)S(1)} %copy-done.2, ...), custom_call_target="tpu_custom_call", output_to_operand_aliasing={{0}: (12, {})} | custom-call | tf_op jit(solution)/shard_map/along_x/pallas_call | solution.py:546
  (10 shorter events, 0.0 us)
Async XLA Ops:
  6.3 15.4 %collective-permute-start = (f32[24,8,128]{2,1,0:T(8,128)}, f32[24,8,128]{2,1,0:T(8,128)S(1)}, u32[]{:S(2)}, u32[]{:S(2)}) collective-permute-start(f32[24,8,128]{2,1,0:T(8,128)} %get-tuple-element.55), channel_id=1, source_target_pairs={{0,1},{1,0},{2,3},{3,2},{4,5},{5,4},{6,7},{7,6},{8,9},{9,8},{10,11... | collective-permute-start | bytes 294920 | tf_op jit(solution)/shard_map/ppermute | solution.py:579
  7.9 13.8 %collective-permute-start.1 = (f32[24,8,128]{2,1,0:T(8,128)}, f32[24,8,128]{2,1,0:T(8,128)S(1)}, u32[]{:S(2)}, u32[]{:S(2)}) collective-permute-start(f32[24,8,128]{2,1,0:T(8,128)} %get-tuple-element.56), channel_id=1, source_target_pairs={{0,2},{1,3},{2,0},{3,1},{4,6},{5,7},{6,4},{7,5},{8,10},{9,11},{10,... | collective-permute-start | bytes 294920 | tf_op jit(solution)/shard_map/ppermute | solution.py:579
  8.2 13.5 %collective-permute-start.2 = (f32[24,8,128]{2,1,0:T(8,128)}, f32[24,8,128]{2,1,0:T(8,128)S(1)}, u32[]{:S(2)}, u32[]{:S(2)}) collective-permute-start(f32[24,8,128]{2,1,0:T(8,128)} %get-tuple-element.57), channel_id=1, source_target_pairs={{0,3},{1,2},{2,1},{3,0},{4,7},{5,6},{6,5},{7,4},{8,11},{9,10},{10,... | collective-permute-start | bytes 294920 | tf_op jit(solution)/shard_map/ppermute | solution.py:579
  17.7 18.6 %collective-permute-start.4 = (f32[40,8,128]{2,1,0:T(8,128)}, f32[40,8,128]{2,1,0:T(8,128)S(1)}, u32[]{:S(2)}, u32[]{:S(2)}) collective-permute-start(f32[40,8,128]{2,1,0:T(8,128)} %get-tuple-element.71), channel_id=1, source_target_pairs={{0,2},{1,3},{2,0},{3,1},{4,6},{5,7},{6,4},{7,5},{8,10},{9,11},{10,... | collective-permute-start | bytes 491528 | tf_op jit(solution)/shard_map/ppermute | solution.py:579
  18.8 17.6 %collective-permute-start.5 = (f32[40,8,128]{2,1,0:T(8,128)}, f32[40,8,128]{2,1,0:T(8,128)S(1)}, u32[]{:S(2)}, u32[]{:S(2)}) collective-permute-start(f32[40,8,128]{2,1,0:T(8,128)} %get-tuple-element.72), channel_id=1, source_target_pairs={{0,3},{1,2},{2,1},{3,0},{4,7},{5,6},{6,5},{7,4},{8,11},{9,10},{10,... | collective-permute-start | bytes 491528 | tf_op jit(solution)/shard_map/ppermute | solution.py:579
  21.7 14.7 %collective-permute-start.3 = (f32[40,8,128]{2,1,0:T(8,128)}, f32[40,8,128]{2,1,0:T(8,128)S(1)}, u32[]{:S(2)}, u32[]{:S(2)}) collective-permute-start(f32[40,8,128]{2,1,0:T(8,128)} %get-tuple-element.70), channel_id=1, source_target_pairs={{0,1},{1,0},{2,3},{3,2},{4,5},{5,4},{6,7},{7,6},{8,9},{9,8},{10,11... | collective-permute-start | bytes 491528 | tf_op jit(solution)/shard_map/ppermute | solution.py:579
  22.2 15.6 %copy-start = (f32[4,256,256]{2,1,0:T(8,128)S(1)}, f32[4,256,256]{2,1,0:T(8,128)}, u32[]{:S(2)}) copy-start(f32[4,256,256]{2,1,0:T(8,128)} %constant.7.clone.refs_8_.refs_4_) | copy-start | bytes 3145732
  22.2 15.6 %copy-start.3 = (f32[40,8,128]{2,1,0:T(8,128)S(1)}, f32[40,8,128]{2,1,0:T(8,128)}, u32[]{:S(2)}) copy-start(f32[40,8,128]{2,1,0:T(8,128)} %get-tuple-element.76.refs_4_) | copy-start | bytes 491524
  22.2 15.6 %copy-start.4 = (f32[24,8,128]{2,1,0:T(8,128)S(1)}, f32[24,8,128]{2,1,0:T(8,128)}, u32[]{:S(2)}) copy-start(f32[24,8,128]{2,1,0:T(8,128)} %get-tuple-element.65.refs_0_) | copy-start | bytes 294916
  33.3 18.4 %collective-permute-start.7 = (f32[66,8,128]{2,1,0:T(8,128)}, f32[66,8,128]{2,1,0:T(8,128)S(1)}, u32[]{:S(2)}, u32[]{:S(2)}) collective-permute-start(f32[66,8,128]{2,1,0:T(8,128)} %get-tuple-element.83), channel_id=1, source_target_pairs={{0,2},{1,3},{2,0},{3,1},{4,6},{5,7},{6,4},{7,5},{8,10},{9,11},{10,... | collective-permute-start | bytes 811016 | tf_op jit(solution)/shard_map/ppermute | solution.py:579
  34.3 24.1 %collective-permute-start.8 = (f32[66,8,128]{2,1,0:T(8,128)}, f32[66,8,128]{2,1,0:T(8,128)S(1)}, u32[]{:S(2)}, u32[]{:S(2)}) collective-permute-start(f32[66,8,128]{2,1,0:T(8,128)} %get-tuple-element.84), channel_id=1, source_target_pairs={{0,3},{1,2},{2,1},{3,0},{4,7},{5,6},{6,5},{7,4},{8,11},{9,10},{10,... | collective-permute-start | bytes 811016 | tf_op jit(solution)/shard_map/ppermute | solution.py:579
  36.4 22.0 %collective-permute-start.6 = (f32[66,8,128]{2,1,0:T(8,128)}, f32[66,8,128]{2,1,0:T(8,128)S(1)}, u32[]{:S(2)}, u32[]{:S(2)}) collective-permute-start(f32[66,8,128]{2,1,0:T(8,128)} %get-tuple-element.82), channel_id=1, source_target_pairs={{0,1},{1,0},{2,3},{3,2},{4,5},{5,4},{6,7},{7,6},{8,9},{9,8},{10,11... | collective-permute-start | bytes 811016 | tf_op jit(solution)/shard_map/ppermute | solution.py:579
  37.8 1.0 %copy-start.1 = (f32[66,8,128]{2,1,0:T(8,128)S(1)}, f32[66,8,128]{2,1,0:T(8,128)}, u32[]{:S(2)}) copy-start(f32[66,8,128]{2,1,0:T(8,128)} %get-tuple-element.80.refs_9_) | copy-start | bytes 811012
  40.5 27.7 %all-to-all-start = ((f32[8,32,8,128]{3,2,1,0:T(8,128)}), f32[8,32,8,128]{3,2,1,0:T(8,128)}, u32[]{:S(2)}, u32[]{:S(2)}) async-start(f32[8,32,8,128]{3,2,1,0:T(8,128)} %get-tuple-element.85), calls=%async_computation | async-start | bytes 2097152 | tf_op jit(solution)/shard_map/all_to_all | solution.py:584
  58.4 9.4 %copy-start.6 = (s32[16,4,2]{0,2,1:T(2,128)S(1)}, s32[16,4,2]{0,2,1:T(2,128)}, u32[]{:S(2)}) copy-start(s32[16,4,2]{0,2,1:T(2,128)} %param.10) | copy-start | bytes 1540
  58.4 9.8 %copy-start.2 = (f32[8,8,256]{2,1,0:T(8,128)S(1)}, f32[8,8,256]{2,1,0:T(8,128)}, u32[]{:S(2)}) copy-start(f32[8,8,256]{2,1,0:T(8,128)} %constant.8.clone.wave_ref) | copy-start | bytes 196612
  58.4 9.8 %copy-start.5 = (s32[3]{0:T(128)S(1)}, s32[3]{0:T(128)}, u32[]{:S(2)}) copy-start(s32[3]{0:T(128)} %source_ref.7) | copy-start | bytes 40
  59.4 5.8 %collective-permute-start.9 = (f32[34,8,128]{2,1,0:T(8,128)S(1)}, f32[34,8,128]{2,1,0:T(8,128)S(1)}, u32[]{:S(2)}, u32[]{:S(2)}) collective-permute-start(f32[34,8,128]{2,1,0:T(8,128)S(1)} %get-tuple-element.90), channel_id=1, source_target_pairs={{0,16},{4,20},{8,24},{12,28},{16,0},{20,4},{24,8},{28,12},{1,17},{... | collective-permute-start | bytes 417800 | tf_op jit(solution)/shard_map/ppermute | solution.py:590
  61.0 6.6 %collective-permute-start.10 = (f32[34,8,128]{2,1,0:T(8,128)S(1)}, f32[34,8,128]{2,1,0:T(8,128)S(1)}, u32[]{:S(2)}, u32[]{:S(2)}) collective-permute-start(f32[34,8,128]{2,1,0:T(8,128)S(1)} %get-tuple-element.91), channel_id=1, source_target_pairs={{0,8},{4,12},{8,0},{12,4},{16,24},{20,28},{24,16},{28,20},{1,9},{5... | collective-permute-start | bytes 417800 | tf_op jit(solution)/shard_map/ppermute | solution.py:590
  62.4 9.5 %collective-permute-start.11 = (f32[34,8,128]{2,1,0:T(8,128)S(1)}, f32[34,8,128]{2,1,0:T(8,128)S(1)}, u32[]{:S(2)}, u32[]{:S(2)}) collective-permute-start(f32[34,8,128]{2,1,0:T(8,128)S(1)} %get-tuple-element.92), channel_id=1, source_target_pairs={{0,24},{4,28},{8,16},{12,20},{16,8},{20,12},{24,0},{28,4},{1,25},{... | collective-permute-start | bytes 417800 | tf_op jit(solution)/shard_map/ppermute | solution.py:590
  62.9 9.0 %collective-permute-start.12 = (f32[34,8,128]{2,1,0:T(8,128)S(1)}, f32[34,8,128]{2,1,0:T(8,128)S(1)}, u32[]{:S(2)}, u32[]{:S(2)}) collective-permute-start(f32[34,8,128]{2,1,0:T(8,128)S(1)} %get-tuple-element.93), channel_id=1, source_target_pairs={{0,4},{4,0},{8,12},{12,8},{16,20},{20,16},{24,28},{28,24},{1,5},{5... | collective-permute-start | bytes 417800 | tf_op jit(solution)/shard_map/ppermute | solution.py:590
  62.9 9.0 %collective-permute-start.13 = (f32[34,8,128]{2,1,0:T(8,128)S(1)}, f32[34,8,128]{2,1,0:T(8,128)S(1)}, u32[]{:S(2)}, u32[]{:S(2)}) collective-permute-start(f32[34,8,128]{2,1,0:T(8,128)S(1)} %get-tuple-element.94), channel_id=1, source_target_pairs={{0,20},{4,16},{8,28},{12,24},{16,4},{20,0},{24,12},{28,8},{1,21},{... | collective-permute-start | bytes 417800 | tf_op jit(solution)/shard_map/ppermute | solution.py:590
  65.1 7.2 %collective-permute-start.14 = (f32[34,8,128]{2,1,0:T(8,128)S(1)}, f32[34,8,128]{2,1,0:T(8,128)S(1)}, u32[]{:S(2)}, u32[]{:S(2)}) collective-permute-start(f32[34,8,128]{2,1,0:T(8,128)S(1)} %get-tuple-element.95), channel_id=1, source_target_pairs={{0,12},{4,8},{8,4},{12,0},{16,28},{20,24},{24,20},{28,16},{1,13},{... | collective-permute-start | bytes 417800 | tf_op jit(solution)/shard_map/ppermute | solution.py:590
  67.5 7.6 %collective-permute-start.15 = (f32[34,8,128]{2,1,0:T(8,128)S(1)}, f32[34,8,128]{2,1,0:T(8,128)S(1)}, u32[]{:S(2)}, u32[]{:S(2)}) collective-permute-start(f32[34,8,128]{2,1,0:T(8,128)S(1)} %get-tuple-element.96), channel_id=1, source_target_pairs={{0,28},{4,24},{8,20},{12,16},{16,12},{20,8},{24,4},{28,0},{1,29},{... | collective-permute-start | bytes 417800 | tf_op jit(solution)/shard_map/ppermute | solution.py:590
